TPU v7x, 32 devices: a whole 2x2x4 slice. The times are simulated.
32 devices in a mesh: row: 8 (over y, x, core), loop: 4 (over z).
Axes of the slice: x: 2, y: 2, z: 4, core: 2. Of those that a mesh axis runs over, the one named last changes fastest.
Arguments:
- features: bfloat16 [65536, 256], P(('row', 'loop')), may hold values from -6 to 6
- weight: bfloat16 [256, 256], replicated, may hold values from -0.375 to 0.375
- local_tiles: bfloat16 [4096, 128, 128], P(('row', 'loop')), may hold values from -0.1875 to 0.1875
- local_ids: int32 [4096], P(('row', 'loop')), may hold values from 0 to 255, as said below
- local_live: int32 [4096], P(('row', 'loop')), may hold values 0 or 1
- send_rows: int32 [32, 8, 256], P(('row', 'loop')), may hold values from 0 to 2047
- send_count: int32 [32, 8], P(('row', 'loop')), may hold values from 0 to 256, as said below
- edge_tiles: bfloat16 [4608, 128, 128], P(('row', 'loop')), may hold values from -0.25 to 0.25
- edge_ids: int32 [4608], P(('row', 'loop')), may hold values from 0 to 255, as said below
- edge_live: int32 [4608], P(('row', 'loop')), may hold values 0 or 1
- hub_feats: bfloat16 [1024, 256], P('loop'), may hold values from -6 to 6
- hub_adj: bfloat16 [65536, 1024], P(('row', 'loop')), may hold values from -0.25 to 0.25
- hub_live: int32 [512, 8], P(('row', 'loop')), may hold values 0 or 1
Outputs:
- layer_out: bfloat16 [65536, 256], P(('row', 'loop'))
Inputs may be any that keep to these rules, and one draw needn't show every extreme that they name: `local_ids`: each entry is i * 16 + j, a tile of one block's 16 x 16 grid; the 128 entries of one device are distinct. `edge_ids`: each entry is i * 16 + j, a tile of a 16 x 16 grid; the 144 entries of one device are distinct. Only the first send_count[d, s] slots of send_rows[d, s] are sent with data. For every loop index, all devices of that loop index send 256 rows to one common row index.
All inputs are finite; a program needn't handle non-finite values. No bound on the sum of `local_live` or of `edge_live` or of `hub_live` on one device may be relied on, other than what follows from the above.
Results may differ from a plain program's by a relative error of at most 0.005.
Values may be sent and summed in bfloat16 or wider, within the bound.
No kernel may reach another device: no remote copies, remote signals or barrier semaphores. Data moves between devices by JAX's collectives and lax.ppermute only.
A program may use at most 256 MiB of HBM per device.

v0:
```python
import jax
import jax.numpy as jnp
from jax import lax
from jax.sharding import PartitionSpec as P


def tile_term(tile_set, tile_ids, tile_live, panels, out_tiles, in_tiles):
    tile_size = tile_set.shape[1]
    width = panels.shape[1]
    live_float = tile_live.astype(jnp.float32)
    panel_grid = panels.reshape(in_tiles, tile_size * width)
    col_select = ((tile_ids % in_tiles)[:, None] == jnp.arange(in_tiles)[None, :]).astype(
        jnp.bfloat16
    )
    gathered = jnp.dot(col_select, panel_grid, preferred_element_type=jnp.float32).astype(
        jnp.bfloat16
    )
    gathered = gathered.reshape(tile_ids.shape[0], tile_size, width)
    products = jnp.einsum("tab,tbf->taf", tile_set, gathered, preferred_element_type=jnp.float32)
    row_select = ((tile_ids // in_tiles)[None, :] == jnp.arange(out_tiles)[:, None]).astype(
        jnp.float32
    )
    row_select = row_select * live_float[None, :]
    summed = jnp.dot(
        row_select,
        products.reshape(tile_ids.shape[0], tile_size * width),
        precision=lax.Precision.HIGHEST,
    )
    return summed.reshape(out_tiles * tile_size, width)


def per_device(
    features,
    weight,
    local_tiles,
    local_ids,
    local_live,
    send_rows,
    send_count,
    edge_tiles,
    edge_ids,
    edge_live,
    hub_feats,
    hub_adj,
    hub_live,
):
    row_count, width = features.shape
    tile_size = local_tiles.shape[1]
    row_tiles = row_count // tile_size
    peers = lax.axis_size("row")
    slot_count = send_rows.shape[2]
    picked = features[send_rows[0]]
    kept_mask = jnp.arange(slot_count)[None, :] < send_count[0][:, None]
    outgoing = jnp.where(kept_mask[:, :, None], picked, jnp.zeros((), jnp.bfloat16))
    incoming = lax.all_to_all(outgoing, "row", split_axis=0, concat_axis=0, tiled=True)
    received = incoming.reshape(peers * slot_count, width)
    local_sum = tile_term(local_tiles, local_ids, local_live, features, row_tiles, row_tiles)
    edge_sum = tile_term(
        edge_tiles, edge_ids, edge_live, received, row_tiles, peers * slot_count // tile_size
    )
    hub_mask = jnp.repeat(jnp.repeat(hub_live, tile_size, 0), tile_size, 1).astype(jnp.bfloat16)
    masked_adj = hub_adj * hub_mask
    hub_sum = jnp.dot(
        masked_adj,
        lax.all_gather(hub_feats, "loop", axis=0, tiled=True),
        preferred_element_type=jnp.float32,
    )
    aggregated = (local_sum + edge_sum + hub_sum).astype(jnp.bfloat16)
    return jax.nn.relu(jnp.dot(aggregated, weight, preferred_element_type=jnp.float32)).astype(
        jnp.bfloat16
    )


def solution(mesh):
    placed = (
        P(("row", "loop"), None),
        P(),
        P(("row", "loop"), None, None),
        P(("row", "loop")),
        P(("row", "loop")),
        P(("row", "loop"), None, None),
        P(("row", "loop"), None),
        P(("row", "loop"), None, None),
        P(("row", "loop")),
        P(("row", "loop")),
        P("loop", None),
        P(("row", "loop"), None),
        P(("row", "loop"), None),
    )
    return jax.shard_map(
        per_device, mesh=mesh, in_specs=placed, out_specs=P(("row", "loop"), None), check_vma=False
    )
```

profile of v0, /device:TPU:1, one launch (start us, length us, event | category | flops | bytes accessed | tf_op | source)
XLA Modules:
  0.0 169.9 jit_solution(3745849159486833839)
XLA Ops:
  0.0 0.7 fusion.8
  0.8 0.7 iota_compare_fusion.6
  1.5 8.1 %gather_fusion = bf16[2048,256]{1,0:T(8,128)(2,1)S(1)} fusion(bf16[2048,256]{1,0:T(8,128)(2,1)} %param.13, s32[2048]{0:T(1024)S(1)} %broadcast_clamp_fusion), kind=kCustom, calls=%fused_computation | custom fusion | bytes 2105344 | tf_op jit(solution)/shard_map/gather | solution.py:52
  9.6 0.0 copy-start.7
  9.6 1.2 broadcast_select_fusion
  10.8 5.2 %all-to-all-start = ((bf16[8,256,256]{2,1,0:T(8,128)(2,1)}), bf16[8,256,256]{2,1,0:T(8,128)(2,1)S(1)}, u32[]{:S(2)}, u32[]{:S(2)}) async-start(bf16[8,256,256]{2,1,0:T(8,128)(2,1)} %broadcast_select_fusion), calls=%async_computation | async-start | bytes 2097152 | tf_op jit(solution)/shard_map/all_to_all | solution.py:55
  16.1 0.5 reshape.80
  16.6 5.6 %convolution_convert_fusion.1 = bf16[128,32768]{1,0:T(8,128)(2,1)} fusion(bf16[16,32768]{1,0:T(8,128)(2,1)S(1)} %reshape.80, s32[128]{0:T(128)S(1)} %get-tuple-element.8), kind=kOutput, calls=%fused_computation.2 | convolution fusion | flops 138414080 | bytes 9437696 | tf_op jit(solution)/shard_map/dot_general | solution.py:15
  22.2 9.1 %copy.24 = bf16[16,8,128,256]{3,2,1,0:T(8,128)(2,1)} copy(bf16[16,8,128,256]{3,1,2,0:T(8,128)(2,1)} %bitcast.47) | data formatting | bytes 16777216
  31.3 12.7 %convolution_bitcast_fusion.1 = f32[128,128,256]{1,2,0:T(8,128)} fusion(bf16[128,128,256]{2,1,0:T(8,128)(2,1)} %bitcast.46, bf16[128,128,128]{2,1,0:T(8,128)(2,1)} %param.15), kind=kOutput, calls=%fused_computation.5 | convolution fusion | flops 1073741824 | bytes 29360128 | tf_op jit(solution)/shard_map/tab,tbf->taf/dot_general | solution.py:19
  44.0 17.7 %copy.18 = f32[128,128,256]{0,2,1:T(8,128)} copy(f32[128,128,256]{1,2,0:T(8,128)} %convolution_bitcast_fusion.1) | data formatting | bytes 33554432 | tf_op jit(solution)/shard_map/tab,tbf->taf/dot_general | solution.py:19
  61.8 0.1 copy.21
  61.8 15.9 %all_gather.3 = bf16[1024,256]{1,0:T(8,128)(2,1)} all-gather(bf16[256,256]{1,0:T(8,128)(2,1)S(1)} %copy-done.3), channel_id=1, replica_groups=mesh['row'=8,'loop'=4] {'loop'}, dimensions={0}, use_global_device_ids=true | all-gather | bytes 655360 | tf_op jit(solution)/shard_map/all_gather | solution.py:65
  77.7 16.5 %fusion.12 = f32[16,32768]{1,0:T(8,128)S(1)} fusion(f32[128,32768]{0,1:T(8,128)} %bitcast.43, f32[128]{0:T(128)S(1)} %convert_element_type.33, s32[128]{0:T(128)S(1)} %get-tuple-element.7), kind=kOutput, calls=%fused_computation.26 | convolution fusion | flops 805310464 | bytes 18875392 | tf_op jit(solution)/shard_map/dot_general | solution.py:24
  94.3 1.3 reshape_reshape.3
  95.6 6.3 %convolution_convert_fusion = bf16[144,32768]{1,0:T(8,128)(2,1)} fusion(bf16[16,32768]{1,0:T(8,128)(2,1)} %reshape_reshape.3, s32[144]{0:T(256)S(1)} %get-tuple-element.6), kind=kOutput, calls=%fused_computation.1 | convolution fusion | flops 155715840 | bytes 10486336 | tf_op jit(solution)/shard_map/dot_general | solution.py:15
  101.9 10.2 %copy.26 = bf16[18,8,128,256]{3,2,1,0:T(8,128)(2,1)} copy(bf16[18,8,128,256]{3,1,2,0:T(8,128)(2,1)} %bitcast.44) | data formatting | bytes 18874368
  112.1 14.3 %convolution_bitcast_fusion = f32[144,128,256]{1,2,0:T(8,128)} fusion(bf16[144,128,256]{2,1,0:T(8,128)(2,1)} %bitcast.45, bf16[144,128,128]{2,1,0:T(8,128)(2,1)} %param.20), kind=kOutput, calls=%fused_computation.4 | convolution fusion | flops 1207959552 | bytes 33030144 | tf_op jit(solution)/shard_map/tab,tbf->taf/dot_general | solution.py:19
  126.4 18.8 %copy.27 = f32[18,8,128,256]{3,1,2,0:T(8,128)} copy(f32[18,8,128,256]{2,3,1,0:T(8,128)} %bitcast.42) | data formatting | bytes 37748736
  145.2 12.9 %convolution_add_fusion = f32[16,32768]{1,0:T(8,128)} fusion(f32[16,32768]{1,0:T(8,128)S(1)} %fusion.12, f32[144,32768]{1,0:T(8,128)} %bitcast.41, f32[144]{0:T(256)S(1)} %convert_element_type.35, s32[144]{0:T(256)S(1)} %get-tuple-element.5), kind=kOutput, calls=%fused_computation.3 | convolution fusion | flops 906498560 | bytes 23069824 | tf_op jit(solution)/shard_map/dot_general | solution.py:24
  158.1 1.8 %add.41 = f32[2048,256]{1,0:T(8,128)S(1)} reshape(f32[16,32768]{1,0:T(8,128)} %convolution_add_fusion) | data formatting | bytes 4194304 | tf_op jit(solution)/shard_map/add | solution.py:68
  159.8 0.1 broadcast_in_dim.18
  159.9 3.8 %broadcast_in_dim.19 = bf16[2048,8,128]{2,1,0:T(8,128)(2,1)} broadcast(bf16[2048,8]{1,0:T(8,128)(2,1)S(1)} %bitcast.50), dimensions={0,1} | broadcast | bytes 4227072 | tf_op jit(solution)/shard_map/broadcast_in_dim | solution.py:61
  163.8 6.1 %fusion.4 = bf16[2048,256]{1,0:T(8,128)(2,1)} fusion(bf16[256,256]{1,0:T(8,128)(2,1)S(1)} %copy-done, f32[2048,256]{1,0:T(8,128)S(1)} %add.41, bf16[1024,256]{1,0:T(8,128)(2,1)S(1)} %copy-done.2, bf16[2048,1024]{1,0:T(8,128)(2,1)} %param.24, bf16[256,8,8,128]{3,2,1,0:T(8,128)(2,1)} %bitcast.48), kind=kOutput, calls=%fused_computation.12 | convolution fusion | flops 1346371584 | bytes 12189696 | tf_op jit(solution)/shard_map/dot_general | solution.py:69
  (25 shorter events, 0.1 us)
Async XLA Ops:
  0.0 163.8 %copy-start = (bf16[256,256]{1,0:T(8,128)(2,1)S(1)}, bf16[256,256]{1,0:T(8,128)(2,1)}, u32[]{:S(2)}) copy-start(bf16[256,256]{1,0:T(8,128)(2,1)} %param.14) | copy-start | bytes 393220
  1.5 14.6 %copy-start.1 = (bf16[2048,256]{1,0:T(8,128)(2,1)S(1)}, bf16[2048,256]{1,0:T(8,128)(2,1)}, u32[]{:S(2)}) copy-start(bf16[2048,256]{1,0:T(8,128)(2,1)} %param.13) | copy-start | bytes 3145732
  9.6 7.0 %copy-start.7 = (s32[128]{0:T(128)S(1)}, s32[128]{0:T(128)}, u32[]{:S(2)}) copy-start(s32[128]{0:T(128)} %param.16) | copy-start | bytes 1540
  10.8 83.4 %all-to-all-start = ((bf16[8,256,256]{2,1,0:T(8,128)(2,1)}), bf16[8,256,256]{2,1,0:T(8,128)(2,1)S(1)}, u32[]{:S(2)}, u32[]{:S(2)}) async-start(bf16[8,256,256]{2,1,0:T(8,128)(2,1)} %broadcast_select_fusion), calls=%async_computation | async-start | bytes 2097152 | tf_op jit(solution)/shard_map/all_to_all | solution.py:55
  44.0 17.7 %copy-start.8 = (s32[128]{0:T(128)S(1)}, s32[128]{0:T(128)}, u32[]{:S(2)}) copy-start(s32[128]{0:T(128)} %param.17) | copy-start | bytes 1540
  44.0 17.7 %copy-start.5 = (s32[144]{0:T(256)S(1)}, s32[144]{0:T(256)}, u32[]{:S(2)}) copy-start(s32[144]{0:T(256)} %param.21) | copy-start | bytes 1732
  44.0 17.7 %copy-start.6 = (s32[144]{0:T(256)S(1)}, s32[144]{0:T(256)}, u32[]{:S(2)}) copy-start(s32[144]{0:T(256)} %param.22) | copy-start | bytes 1732
  44.0 17.8 %copy-start.4 = (s32[16,8]{0,1:T(8,128)S(1)}, s32[16,8]{0,1:T(8,128)}, u32[]{:S(2)}) copy-start(s32[16,8]{0,1:T(8,128)} %param.25) | copy-start | bytes 1540
  44.0 17.9 %copy-start.3 = (bf16[256,256]{1,0:T(8,128)(2,1)S(1)}, bf16[256,256]{1,0:T(8,128)(2,1)}, u32[]{:S(2)}) copy-start(bf16[256,256]{1,0:T(8,128)(2,1)} %param.23) | copy-start | bytes 393220
  158.1 5.7 %copy-start.2 = (bf16[1024,256]{1,0:T(8,128)(2,1)S(1)}, bf16[1024,256]{1,0:T(8,128)(2,1)}, u32[]{:S(2)}) copy-start(bf16[1024,256]{1,0:T(8,128)(2,1)} %all_gather.3) | copy-start | bytes 1572868
where the time goes:
time: 172 us; the launch traced here: 170 us
  matrix products  74.4 us (43%)
  local copies, waits for them, and re-layouts  71.5 us (42%)
  blocking collectives  15.9 us (9%)
  starting transfers between devices  5.22 us (3%)
  other arithmetic  2.74 us (2%)
    unnamed x22, local copies, waits for them, and re-layouts  38.1 us
    dot_general x2, matrix products, tile_term(): jnp.dot(row_select, products.reshape(tile_ids.shape[0], tile_size * width...  29.4 us
    dot_general x2, matrix products, tile_term(): jnp.einsum('tab,tbf->taf', tile_set, gathered, preferred_element_type=jnp...  27 us
    dot_general x1, local copies, waits for them, and re-layouts, tile_term(): jnp.einsum('tab,tbf->taf', tile_set, gathered, preferred_element_type=jnp...  17.7 us
    all_gather x1, blocking collectives, per_device(): lax.all_gather(hub_feats, 'loop', axis=0, tiled=True)  15.9 us
    dot_general x2, matrix products, tile_term(): jnp.dot(col_select, panel_grid, preferred_element_type=jnp.float32)  11.9 us
    gather x1, local copies, waits for them, and re-layouts, per_device(): picked = features[send_rows[0]]  8.09 us
    dot_general x1, matrix products, per_device(): jnp.dot(aggregated, weight, preferred_element_type=jnp.float32)  6.1 us
  transfers between devices with their start and end apart: 1, of which 0 were waited for; matrix products, arithmetic and copies ran while one was open for 37% of the time, Pallas kernels for 0%

commit v1 on v0

v1 whole, which is shorter than its diff:
```python
import functools

import jax
import jax.numpy as jnp
from jax import lax
from jax.experimental import pallas as pl
from jax.experimental.pallas import tpu as pltpu
from jax.sharding import PartitionSpec as P

BF = jnp.bfloat16
F32 = jnp.float32
I32 = jnp.int32
VMEM = pl.BlockSpec(memory_space=pltpu.VMEM)
SMEM = pl.BlockSpec(memory_space=pltpu.SMEM)
HBM = pl.BlockSpec(memory_space=pl.ANY)
MIB = 1 << 20


def params(mib):
    return pltpu.CompilerParams(vmem_limit_bytes=mib * MIB)


def dot(a, b):
    return jnp.dot(a, b, preferred_element_type=F32)


def gather_rows(send_ref, count_ref, feat_ref, peer):
    slots = send_ref.shape[1]
    rows = feat_ref.shape[0]
    index = send_ref[pl.ds(peer, 1), :]
    slot = lax.broadcasted_iota(I32, (1, slots), 1)
    index = jnp.where(slot < count_ref[0, peer], index, -1)
    lane = lax.broadcasted_iota(I32, (128, 128), 1)
    picks = []
    for part in range(slots // 128):
        column = jnp.broadcast_to(index[:, part * 128 : (part + 1) * 128], (128, 128)).T
        picks.append(
            jnp.concatenate(
                [jnp.where(column == lane + c * 128, 1.0, 0.0).astype(BF) for c in range(rows // 128)], axis=1
            )
        )
    return dot(jnp.concatenate(picks, axis=0), feat_ref[...]).astype(BF)


def pack_kernel(offsets, send_ref, count_ref, feat_ref, *out_refs):
    me = lax.axis_index("row")
    slots = send_ref.shape[1]
    for out_ref, group in zip(out_refs, offsets):
        for n, offset in enumerate(group):
            out_ref[n * slots : (n + 1) * slots, :] = gather_rows(send_ref, count_ref, feat_ref, me ^ offset)


def pack(offsets, send_rows, send_count, features):
    slots, width = send_rows.shape[1], features.shape[1]
    return pl.pallas_call(
        functools.partial(pack_kernel, offsets),
        out_shape=[jax.ShapeDtypeStruct((len(group) * slots, width), BF) for group in offsets],
        in_specs=[VMEM, SMEM, VMEM],
        out_specs=[VMEM] * len(offsets),
        compiler_params=params(16),
        name="pack",
    )(send_rows, send_count, features)


def fill_map(ids_ref, live_ref, map_ref):
    for cell in range(map_ref.shape[0]):
        map_ref[cell] = -1
    for t in range(ids_ref.shape[0]):
        map_ref[ids_ref[t]] = jnp.where(live_ref[t] > 0, t, -1)


def cell_tile(tiles_ref, map_ref, cell):
    slot = map_ref[cell]
    tile = tiles_ref[jnp.maximum(slot, 0)]
    return jnp.where(slot >= 0, tile, jnp.zeros_like(tile))


def local_kernel(block, ids_ref, live_ref, tiles_ref, feat_ref, out_ref, map_ref):
    fill_map(ids_ref, live_ref, map_ref)
    size = tiles_ref.shape[1]
    cols = feat_ref.shape[0] // size

    def body(m, _):
        rows = [
            jnp.concatenate([cell_tile(tiles_ref, map_ref, (m * block + i) * cols + j) for j in range(cols)], axis=1)
            for i in range(block)
        ]
        start = pl.multiple_of(m * block * size, block * size)
        out_ref[pl.ds(start, block * size), :] = dot(jnp.concatenate(rows, axis=0), feat_ref[...])
        return 0

    lax.fori_loop(0, out_ref.shape[0] // (block * size), body, 0)


def local_term(ids, live, tiles, features):
    return pl.pallas_call(
        functools.partial(local_kernel, 4),
        out_shape=jax.ShapeDtypeStruct(features.shape, F32),
        in_specs=[SMEM, SMEM, VMEM, VMEM],
        out_specs=VMEM,
        scratch_shapes=[pltpu.SMEM(((features.shape[0] // tiles.shape[1]) ** 2,), I32)],
        compiler_params=params(16),
        name="local",
    )(ids, live, tiles, features)


def edge_kernel(block, pieces, late, hubs, counts, *refs):
    ids_ref, live_ref, hub_live_ref, tiles_ref, adj_ref, acc_ref = refs[:6]
    array_refs = refs[6 : 6 + counts]
    out_ref, late_ref, map_ref, rhs_ref = refs[6 + counts :]
    me, loop = lax.axis_index("row"), lax.axis_index("loop")
    core = lax.rem(me, 2)
    size = tiles_ref.shape[1]
    rows, depth = adj_ref.shape
    cols = map_ref.shape[0] // (rows // size)
    slots = late_ref.shape[1] // len(late)
    per = slots // size
    fill_map(ids_ref, live_ref, map_ref)
    for array, first, count, offset, half in hubs:
        if half is None:
            start = pl.multiple_of((loop ^ offset) * count, count)
        else:
            start = pl.multiple_of((loop ^ offset) * 2 * count + (core ^ half) * count, count)
        rhs_ref[pl.ds(start, count), :] = array_refs[array][first : first + count, :]
    for n, (array, first, offset) in enumerate(pieces):
        rhs_ref[depth + n * slots : depth + (n + 1) * slots, :] = array_refs[array][first : first + slots, :]

    def body(m, _):
        blocks = []
        for i in range(block):
            row = m * block + i
            start = pl.multiple_of(row * size, size)
            line = []
            for b in range(depth // size):
                cell = adj_ref[pl.ds(start, size), b * size : (b + 1) * size]
                line.append(jnp.where(hub_live_ref[row, b] > 0, cell, jnp.zeros_like(cell)))
            for array, first, offset in pieces:
                for j in range(per):
                    line.append(cell_tile(tiles_ref, map_ref, row * cols + (me ^ offset) * per + j))
            blocks.append(jnp.concatenate(line, axis=1))
            for n, offset in enumerate(late):
                for j in range(per):
                    at = n * slots + j * size
                    late_ref[pl.ds(start, size), at : at + size] = cell_tile(
                        tiles_ref, map_ref, row * cols + (me ^ offset) * per + j
                    )
        span = pl.ds(pl.multiple_of(m * block * size, block * size), block * size)
        out_ref[span, :] = acc_ref[span, :] + dot(jnp.concatenate(blocks, axis=0), rhs_ref[...])
        return 0

    lax.fori_loop(0, rows // (block * size), body, 0)


def edge_term(pieces, late, hubs, slots, ids, live, hub_live, tiles, adj, acc, arrays):
    rows, depth = adj.shape
    size = tiles.shape[1]
    cells = (rows // size) * (lax.axis_size("row") * slots // size)
    return pl.pallas_call(
        functools.partial(edge_kernel, 4, pieces, late, hubs, len(arrays)),
        out_shape=[jax.ShapeDtypeStruct(acc.shape, F32), jax.ShapeDtypeStruct((rows, len(late) * slots), BF)],
        in_specs=[SMEM, SMEM, SMEM, VMEM, VMEM, VMEM] + [VMEM] * len(arrays),
        out_specs=[VMEM, VMEM],
        scratch_shapes=[pltpu.SMEM((cells,), I32), pltpu.VMEM((depth + len(pieces) * slots, acc.shape[1]), BF)],
        compiler_params=params(48),
        name="edge",
    )(ids, live, hub_live, tiles, adj, acc, *arrays)


def last_kernel(block, counts, acc_ref, late_ref, weight_ref, *refs):
    array_refs = refs[:counts]
    out_ref, stage_ref, sems = refs[counts:]
    depth = array_refs[0].shape[0]
    for m in range(acc_ref.shape[0] // block):
        span = slice(m * block, (m + 1) * block)
        total = acc_ref[span, :]
        for n in range(counts):
            total += dot(late_ref[span, n * depth : (n + 1) * depth], array_refs[n][...])
        stage_ref[span, :] = jnp.maximum(dot(total.astype(BF), weight_ref[...]), 0.0).astype(BF)
        pltpu.make_async_copy(stage_ref.at[span], out_ref.at[span], sems.at[m]).start()
    for m in range(acc_ref.shape[0] // block):
        span = slice(m * block, (m + 1) * block)
        pltpu.make_async_copy(stage_ref.at[span], out_ref.at[span], sems.at[m]).wait()


def last_term(acc, late, weight, arrays):
    block = 512
    return pl.pallas_call(
        functools.partial(last_kernel, block, len(arrays)),
        out_shape=jax.ShapeDtypeStruct(acc.shape, BF),
        in_specs=[VMEM] * (3 + len(arrays)),
        out_specs=HBM,
        scratch_shapes=[pltpu.VMEM(acc.shape, BF), pltpu.SemaphoreType.DMA((acc.shape[0] // block,))],
        compiler_params=params(32),
        name="last",
    )(acc, late, weight, *arrays)


def swap(x, axis, offset):
    return lax.ppermute(x, axis, [(i, i ^ offset) for i in range(lax.axis_size(axis))])


def join_kernel(offset_count, send_ref, count_ref, feat_ref, relayed_ref, *out_refs):
    me = lax.axis_index("row")
    slots = send_ref.shape[1]
    own_ref = out_refs[-1]
    for n, offset in enumerate(offset_count):
        out_refs[n][:slots, :] = gather_rows(send_ref, count_ref, feat_ref, me ^ offset)
        out_refs[n][slots:, :] = relayed_ref[n * slots : (n + 1) * slots, :]
    own_ref[...] = gather_rows(send_ref, count_ref, feat_ref, me)


def join(offsets, send_rows, send_count, features, relayed):
    slots, width = send_rows.shape[1], features.shape[1]
    return pl.pallas_call(
        functools.partial(join_kernel, offsets),
        out_shape=[jax.ShapeDtypeStruct((2 * slots, width), BF) for _ in offsets]
        + [jax.ShapeDtypeStruct((slots, width), BF)],
        in_specs=[VMEM, SMEM, VMEM, VMEM],
        out_specs=[VMEM] * (len(offsets) + 1),
        compiler_params=params(16),
        name="join",
    )(send_rows, send_count, features, relayed)


def per_device(
    features,
    weight,
    local_tiles,
    local_ids,
    local_live,
    send_rows,
    send_count,
    edge_tiles,
    edge_ids,
    edge_live,
    hub_feats,
    hub_adj,
    hub_live,
):
    peers, ring = lax.axis_size("row"), lax.axis_size("loop")
    slots = send_rows.shape[2]
    rows = send_rows[0]
    chips = range(2, peers, 2)
    early = [c for c in chips if c & (c - 1) == 0]
    late = [c for c in chips if c & (c - 1) != 0]
    first = pack([(c, c ^ 1) for c in early], rows, send_count, features)
    from_early = [swap(x, "row", c) for x, c in zip(first, early)]
    (relay,) = pack([tuple(c ^ 1 for c in late) + (1,)], rows, send_count, features)
    relayed = swap(relay, "row", 1)
    *second, own = join(late, rows, send_count, features, relayed)
    from_late = [swap(x, "row", c) for x, c in zip(second, late)]
    shared = [swap(x, "row", 1) for x in from_early]
    shard = hub_feats.shape[0]
    half = shard // 2
    core = lax.rem(lax.axis_index("row"), 2)
    mine = lax.dynamic_slice(hub_feats, (core * half, 0), (half, hub_feats.shape[1]))
    arrays = [hub_feats, swap(hub_feats, "loop", 1)]
    hubs = [(0, 0, shard, 0, None), (1, 0, shard, 1, None)]
    for offset in range(2, ring):
        got = swap(mine, "loop", offset)
        hubs += [(len(arrays), 0, half, offset, 0), (len(arrays) + 1, 0, half, offset, 1)]
        arrays += [got, swap(got, "row", 1)]
    pieces = [(len(arrays), 0, 0), (len(arrays) + 1, len(late) * slots, 1)]
    arrays += [own, relayed]
    for c, x, y in zip(early, from_early, shared):
        pieces += [(len(arrays), 0, c), (len(arrays) + 1, slots, c ^ 1)]
        arrays += [x, y]
    acc = local_term(local_ids, local_live, local_tiles, features)
    order = [c ^ core_bit for c in late for core_bit in (0, 1)]
    acc, late_tiles = edge_term(
        pieces, order, hubs, slots, edge_ids, edge_live, hub_live, edge_tiles, hub_adj, acc, arrays
    )
    return last_term(acc, late_tiles, weight, from_late)


def solution(mesh):
    both = ("row", "loop")
    placed = (
        P(both, None),
        P(),
        P(both, None, None),
        P(both),
        P(both),
        P(both, None, None),
        P(both, None),
        P(both, None, None),
        P(both),
        P(both),
        P("loop", None),
        P(both, None),
        P(both, None),
    )
    return jax.shard_map(per_device, mesh=mesh, in_specs=placed, out_specs=P(both, None), check_vma=False)
```

time: 172 us -> 55 us (0.32)
  matrix products: 74.4 us -> 0 us
  local copies, waits for them, and re-layouts: 71.5 us -> 12.3 us
  Pallas kernels: 0 us -> 19.6 us
  blocking collectives: 15.9 us -> 0 us
  starting transfers between devices: 5.22 us -> 15.6 us
  waiting for transfers between devices: 0.01 us -> 6.54 us
  other arithmetic: 2.74 us -> 0 us
    dot_general x7 -> x0, matrix products: 74.4 us -> none  [the longest x2 29.4 us: tile_term(): jnp.dot(row_select, products.reshape(tile_ids.shape[0], tile_size * width...]
    unnamed x22 -> x33, local copies, waits for them, and re-layouts: 38.1 us -> 11.4 us
    pallas_call x0 -> x6, Pallas kernels: none -> 19.6 us  [the longest x1 8.84 us: edge_term(): pl.pallas_call(functools.partial(edge_kernel, 4, pieces, late, hubs, len(...]
    dot_general x1 -> x0, local copies, waits for them, and re-layouts: 17.7 us -> none  [tile_term(): jnp.einsum('tab,tbf->taf', tile_set, gathered, preferred_element_type=jnp...]
    all_gather x1 -> x0, blocking collectives: 15.9 us -> none  [per_device(): lax.all_gather(hub_feats, 'loop', axis=0, tiled=True)]
    ppermute x0 -> x11, starting transfers between devices: none -> 15.6 us  [swap(): lax.ppermute(x, axis, [(i, i ^ offset) for i in range(lax.axis_size(axis))])]
    gather x1 -> x0, local copies, waits for them, and re-layouts: 8.09 us -> none  [per_device(): picked = features[send_rows[0]]]
    ppermute x0 -> x11, waiting for transfers between devices: none -> 6.54 us  [swap(): lax.ppermute(x, axis, [(i, i ^ offset) for i in range(lax.axis_size(axis))])]
  transfers between devices with their start and end apart: 1 -> 11, of which waited for: 0 -> 4; matrix products, arithmetic and copies ran while one was open for 37% -> 3% of each run, Pallas kernels for 0% -> 29%
where the time goes in v1:
time: 55 us; the launch traced here: 54 us
  Pallas kernels  19.6 us (36%)
  starting transfers between devices  15.6 us (28%)
  local copies, waits for them, and re-layouts  12.3 us (22%)
  waiting for transfers between devices  6.54 us (12%)
    ppermute x11, starting transfers between devices, swap(): lax.ppermute(x, axis, [(i, i ^ offset) for i in range(lax.axis_size(axis))])  15.6 us
    unnamed x33, local copies, waits for them, and re-layouts  11.4 us
    pallas_call x1, Pallas kernels, edge_term(): pl.pallas_call(functools.partial(edge_kernel, 4, pieces, late, hubs, len(...  8.84 us
    ppermute x11, waiting for transfers between devices, swap(): lax.ppermute(x, axis, [(i, i ^ offset) for i in range(lax.axis_size(axis))])  6.54 us
    pallas_call x1, Pallas kernels, local_term(): pl.pallas_call(functools.partial(local_kernel, 4), out_shape=jax.ShapeDty...  3.78 us
    pallas_call x2, Pallas kernels, pack(): pl.pallas_call(functools.partial(pack_kernel, offsets), out_shape=[jax.Sh...  3.16 us
    pallas_call x1, Pallas kernels, last_term(): pl.pallas_call(functools.partial(last_kernel, block, len(arrays)), out_sh...  2.46 us
    pallas_call x1, Pallas kernels, join(): pl.pallas_call(functools.partial(join_kernel, offsets), out_shape=[jax.Sh...  1.31 us
  transfers between devices with their start and end apart: 11, of which 4 were waited for; matrix products, arithmetic and copies ran while one was open for 3% of the time, Pallas kernels for 29%

profile of v1, /device:TPU:1, one launch (start us, length us, event | category | flops | bytes accessed | tf_op | source)
XLA Modules:
  0.0 54.0 jit_solution(5420204226692076469)
XLA Ops:
  0.0 1.2 %copy-done = bf16[2048,256]{1,0:T(8,128)(2,1)S(1)} copy-done((bf16[2048,256]{1,0:T(8,128)(2,1)S(1)}, bf16[2048,256]{1,0:T(8,128)(2,1)}, u32[]{:S(2)}) %copy-start) | copy-done | bytes 1048600
  1.2 0.7 %copy-done.7 = s32[1,8,256]{2,1,0:T(8,128)S(1)} copy-done((s32[1,8,256]{2,1,0:T(8,128)S(1)}, s32[1,8,256]{2,1,0:T(8,128)}, u32[]{:S(2)}) %copy-start.7) | copy-done | bytes 8216
  1.9 0.7 %copy-done.9 = s32[1,8]{1,0:T(1,128)S(1)} copy-done((s32[1,8]{1,0:T(1,128)S(1)}, s32[1,8]{1,0:T(1,128)}, u32[]{:S(2)}) %copy-start.9) | copy-done | bytes 56
  2.6 1.3 %pack.2 = bf16[512,256]{1,0:T(8,128)(2,1)S(1)} custom-call(s32[8,256]{1,0:T(8,128)S(1)} %bitcast.1, s32[1,8]{1,0:T(1,128)S(1)} %copy-done.9, bf16[2048,256]{1,0:T(8,128)(2,1)S(1)} %copy-done), custom_call_target="tpu_custom_call" | custom-call | tf_op jit(solution)/shard_map/pack/pallas_call | solution.py:55
  4.7 1.9 %pack.3 = (bf16[512,256]{1,0:T(8,128)(2,1)S(1)}, bf16[512,256]{1,0:T(8,128)(2,1)S(1)}) custom-call(s32[8,256]{1,0:T(8,128)S(1)} %bitcast.2, s32[1,8]{1,0:T(1,128)S(1)} %copy-done.10, bf16[2048,256]{1,0:T(8,128)(2,1)S(1)} %copy-done), custom_call_target="tpu_custom_call" | custom-call | tf_op jit(solution)/shard_map/pack/pallas_call | solution.py:55
  6.5 2.7 %collective-permute-start.6 = (bf16[512,256]{1,0:T(8,128)(2,1)S(1)}, bf16[512,256]{1,0:T(8,128)(2,1)S(1)}, u32[]{:S(2)}, u32[]{:S(2)}) collective-permute-start(bf16[512,256]{1,0:T(8,128)(2,1)S(1)} %get-tuple-element.12), channel_id=1, source_target_pairs={{0,8},{4,12},{8,0},{12,4},{16,24},{20,28},{24,16},{28,20},{1,9},{5... | collective-permute-start | bytes 786440 | tf_op jit(solution)/shard_map/ppermute | solution.py:199
  9.3 1.2 %collective-permute-start.8 = (bf16[512,256]{1,0:T(8,128)(2,1)S(1)}, bf16[512,256]{1,0:T(8,128)(2,1)S(1)}, u32[]{:S(2)}, u32[]{:S(2)}) collective-permute-start(bf16[512,256]{1,0:T(8,128)(2,1)S(1)} %get-tuple-element.13), channel_id=1, source_target_pairs={{0,16},{4,20},{8,24},{12,28},{16,0},{20,4},{24,8},{28,12},{1,17},{... | collective-permute-start | bytes 786440 | tf_op jit(solution)/shard_map/ppermute | solution.py:199
  10.5 1.2 %copy-done.1 = bf16[2048,256]{1,0:T(8,128)(2,1)S(1)} copy-done((bf16[2048,256]{1,0:T(8,128)(2,1)S(1)}, bf16[2048,256]{1,0:T(8,128)(2,1)}, u32[]{:S(2)}) %copy-start.1) | copy-done | bytes 1048600
  11.7 0.7 %copy-done.8 = s32[1,8,256]{2,1,0:T(8,128)S(1)} copy-done((s32[1,8,256]{2,1,0:T(8,128)S(1)}, s32[1,8,256]{2,1,0:T(8,128)}, u32[]{:S(2)}) %copy-start.8) | copy-done | bytes 8216
  13.1 1.3 %join.1 = (bf16[512,256]{1,0:T(8,128)(2,1)S(1)}, bf16[256,256]{1,0:T(8,128)(2,1)S(1)}) custom-call(s32[8,256]{1,0:T(8,128)S(1)} %bitcast.3, s32[1,8]{1,0:T(1,128)S(1)} %copy-done.11, bf16[2048,256]{1,0:T(8,128)(2,1)S(1)} %copy-done.1, bf16[512,256]{1,0:T(8,128)(2,1)S(1)} %collective-permute-done.5.relayed_ref.refs_13_), custom_call_target="tpu_custom_call" | custom-call | tf_op jit(solution)/shard_map/join/pallas_call | solution.py:214
  14.5 1.4 %collective-permute-done.6.refs_14_ = bf16[512,256]{1,0:T(8,128)(2,1)S(1)} collective-permute-done((bf16[512,256]{1,0:T(8,128)(2,1)S(1)}, bf16[512,256]{1,0:T(8,128)(2,1)S(1)}, u32[]{:S(2)}, u32[]{:S(2)}) %collective-permute-start.6) | collective-permute-done | bytes 262176 | tf_op jit(solution)/shard_map/ppermute | solution.py:199
  16.9 5.8 %collective-permute-start.9 = (bf16[512,256]{1,0:T(8,128)(2,1)S(1)}, bf16[512,256]{1,0:T(8,128)(2,1)S(1)}, u32[]{:S(2)}, u32[]{:S(2)}) collective-permute-start(bf16[512,256]{1,0:T(8,128)(2,1)S(1)} %collective-permute-done.8.refs_16_), channel_id=1, source_target_pairs={{0,4},{4,0},{8,12},{12,8},{16,20},{20,16},{24,28},{28,24},{1,5},{5... | collective-permute-start | bytes 786440 | tf_op jit(solution)/shard_map/ppermute | solution.py:199
  22.7 0.8 %constant_dynamic-slice_fusion = bf16[128,256]{1,0:T(8,128)(2,1)S(1)} fusion(bf16[256,256]{1,0:T(8,128)(2,1)} %refs_6_.1, s32[]{:T(128)S(6)} %select_n.3), kind=kLoop, calls=%fused_computation | loop fusion | bytes 131076 | tf_op jit(solution)/shard_map/dynamic_slice | solution.py:256
  23.5 3.3 %collective-permute-start.3 = (bf16[128,256]{1,0:T(8,128)(2,1)S(1)}, bf16[128,256]{1,0:T(8,128)(2,1)S(1)}, u32[]{:S(2)}, u32[]{:S(2)}) collective-permute-start(bf16[128,256]{1,0:T(8,128)(2,1)S(1)} %constant_dynamic-slice_fusion), channel_id=1, source_target_pairs={{0,3},{1,2},{2,1},{3,0},{4,7},{5,6},{6,5},{7,4},{8,11},{9,10},{10,... | collective-permute-start | bytes 196616 | tf_op jit(solution)/shard_map/ppermute | solution.py:199
  26.8 2.4 %collective-permute-done.3.refs_10_ = bf16[128,256]{1,0:T(8,128)(2,1)S(1)} collective-permute-done((bf16[128,256]{1,0:T(8,128)(2,1)S(1)}, bf16[128,256]{1,0:T(8,128)(2,1)S(1)}, u32[]{:S(2)}, u32[]{:S(2)}) %collective-permute-start.3) | collective-permute-done | bytes 65568 | tf_op jit(solution)/shard_map/ppermute | solution.py:199
  29.2 0.9 %collective-permute-start.4 = (bf16[128,256]{1,0:T(8,128)(2,1)S(1)}, bf16[128,256]{1,0:T(8,128)(2,1)S(1)}, u32[]{:S(2)}, u32[]{:S(2)}) collective-permute-start(bf16[128,256]{1,0:T(8,128)(2,1)S(1)} %collective-permute-done.3.refs_10_), channel_id=1, source_target_pairs={{0,4},{4,0},{8,12},{12,8},{16,20},{20,16},{24,28},{28,24},{1,5},{5... | collective-permute-start | bytes 196616 | tf_op jit(solution)/shard_map/ppermute | solution.py:199
  30.1 2.4 %collective-permute-done.1.refs_8_ = bf16[128,256]{1,0:T(8,128)(2,1)S(1)} collective-permute-done((bf16[128,256]{1,0:T(8,128)(2,1)S(1)}, bf16[128,256]{1,0:T(8,128)(2,1)S(1)}, u32[]{:S(2)}, u32[]{:S(2)}) %collective-permute-start.1) | collective-permute-done | bytes 65568 | tf_op jit(solution)/shard_map/ppermute | solution.py:199
  32.6 0.7 %collective-permute-start.2 = (bf16[128,256]{1,0:T(8,128)(2,1)S(1)}, bf16[128,256]{1,0:T(8,128)(2,1)S(1)}, u32[]{:S(2)}, u32[]{:S(2)}) collective-permute-start(bf16[128,256]{1,0:T(8,128)(2,1)S(1)} %collective-permute-done.1.refs_8_), channel_id=1, source_target_pairs={{0,4},{4,0},{8,12},{12,8},{16,20},{20,16},{24,28},{28,24},{1,5},{5... | collective-permute-start | bytes 196616 | tf_op jit(solution)/shard_map/ppermute | solution.py:199
  33.3 0.8 %copy.14.refs_2_ = s32[16,8]{1,0:T(8,128)S(1)} copy(s32[16,8]{0,1:T(8,128)} %param.25) | data formatting | bytes 1024 | tf_op args[12]
  34.0 2.2 %copy-done.4 = bf16[128,128,128]{2,1,0:T(8,128)(2,1)S(1)} copy-done((bf16[128,128,128]{2,1,0:T(8,128)(2,1)S(1)}, bf16[128,128,128]{2,1,0:T(8,128)(2,1)}, u32[]{:S(2)}) %copy-start.4) | copy-done | bytes 4194328
  37.5 3.8 %local.1.refs_5_ = f32[2048,256]{1,0:T(8,128)S(1)} custom-call(s32[128]{0:T(128)S(1)} %copy-done.14, s32[128]{0:T(128)S(1)} %copy-done.15, bf16[128,128,128]{2,1,0:T(8,128)(2,1)S(1)} %copy-done.4, bf16[2048,256]{1,0:T(8,128)(2,1)S(1)} %copy-done.2), custom_call_target="tpu_custom_call" | custom-call | tf_op jit(solution)/shard_map/local/pallas_call | solution.py:96
  41.3 1.3 %copy-done.3 = f32[2048,256]{1,0:T(8,128)} copy-done((f32[2048,256]{1,0:T(8,128)}, f32[2048,256]{1,0:T(8,128)S(1)}, u32[]{:S(2)}) %copy-start.3) | copy-done | bytes 2097176
  42.7 8.8 %edge.1 = (f32[2048,256]{1,0:T(8,128)S(1)}, bf16[2048,512]{1,0:T(8,128)(2,1)S(1)}) custom-call(s32[144]{0:T(256)S(1)} %copy-done.12, s32[144]{0:T(256)S(1)} %copy-done.13, s32[16,8]{1,0:T(8,128)S(1)} %copy.14.refs_2_, bf16[144,128,128]{2,1,0:T(8,128)(2,1)} %refs_3_.1, bf16[2048,1024]{1,0:T(8,128)(2,1)} %refs_4_.1, f32[2048,256]{1,0:T(8,128)} %copy-done.3, ...), custom_call_target="tpu_custom_call" | custom-call | tf_op jit(solution)/shard_map/edge/pallas_call | solution.py:158
  51.6 2.5 %last.1 = bf16[2048,256]{1,0:T(8,128)(2,1)} custom-call(f32[2048,256]{1,0:T(8,128)S(1)} %get-tuple-element.14.acc_ref, bf16[2048,512]{1,0:T(8,128)(2,1)S(1)} %get-tuple-element.15.late_ref, bf16[256,256]{1,0:T(8,128)(2,1)S(1)} %copy-done.6, bf16[512,256]{1,0:T(8,128)(2,1)S(1)} %collective-permute-done.10.refs_0_), custom_call_target="tpu_custom_call" | custom-call | tf_op jit(solution)/shard_map/last/pallas_call | solution.py:187
  (38 shorter events, 3.9 us)
Async XLA Ops:
  0.0 1.2 %copy-start = (bf16[2048,256]{1,0:T(8,128)(2,1)S(1)}, bf16[2048,256]{1,0:T(8,128)(2,1)}, u32[]{:S(2)}) copy-start(bf16[2048,256]{1,0:T(8,128)(2,1)} %feat_ref.7) | copy-start | bytes 3145732
  1.2 0.7 %copy-start.7 = (s32[1,8,256]{2,1,0:T(8,128)S(1)}, s32[1,8,256]{2,1,0:T(8,128)}, u32[]{:S(2)}) copy-start(s32[1,8,256]{2,1,0:T(8,128)} %param.18) | copy-start | bytes 24580
  2.6 31.4 %copy-start.2 = (bf16[2048,256]{1,0:T(8,128)(2,1)S(1)}, bf16[2048,256]{1,0:T(8,128)(2,1)}, u32[]{:S(2)}) copy-start(bf16[2048,256]{1,0:T(8,128)(2,1)} %feat_ref.7) | copy-start | bytes 3145732
  3.9 6.6 %collective-permute-start.5 = (bf16[512,256]{1,0:T(8,128)(2,1)S(1)}, bf16[512,256]{1,0:T(8,128)(2,1)S(1)}, u32[]{:S(2)}, u32[]{:S(2)}) collective-permute-start(bf16[512,256]{1,0:T(8,128)(2,1)S(1)} %pack.2), channel_id=1, source_target_pairs={{0,4},{4,0},{8,12},{12,8},{16,20},{20,16},{24,28},{28,24},{1,5},{5... | collective-permute-start | bytes 786440 | tf_op jit(solution)/shard_map/ppermute | solution.py:199
  4.0 0.7 %copy-start.10 = (s32[1,8]{1,0:T(1,128)S(1)}, s32[1,8]{1,0:T(1,128)}, u32[]{:S(2)}) copy-start(s32[1,8]{1,0:T(1,128)} %count_ref.5) | copy-start | bytes 100
  6.5 9.4 %collective-permute-start.6 = (bf16[512,256]{1,0:T(8,128)(2,1)S(1)}, bf16[512,256]{1,0:T(8,128)(2,1)S(1)}, u32[]{:S(2)}, u32[]{:S(2)}) collective-permute-start(bf16[512,256]{1,0:T(8,128)(2,1)S(1)} %get-tuple-element.12), channel_id=1, source_target_pairs={{0,8},{4,12},{8,0},{12,4},{16,24},{20,28},{24,16},{28,20},{1,9},{5... | collective-permute-start | bytes 786440 | tf_op jit(solution)/shard_map/ppermute | solution.py:199
  9.3 7.6 %collective-permute-start.8 = (bf16[512,256]{1,0:T(8,128)(2,1)S(1)}, bf16[512,256]{1,0:T(8,128)(2,1)S(1)}, u32[]{:S(2)}, u32[]{:S(2)}) collective-permute-start(bf16[512,256]{1,0:T(8,128)(2,1)S(1)} %get-tuple-element.13), channel_id=1, source_target_pairs={{0,16},{4,20},{8,24},{12,28},{16,0},{20,4},{24,8},{28,12},{1,17},{... | collective-permute-start | bytes 786440 | tf_op jit(solution)/shard_map/ppermute | solution.py:199
  10.5 1.2 %copy-start.1 = (bf16[2048,256]{1,0:T(8,128)(2,1)S(1)}, bf16[2048,256]{1,0:T(8,128)(2,1)}, u32[]{:S(2)}) copy-start(bf16[2048,256]{1,0:T(8,128)(2,1)} %feat_ref.7) | copy-start | bytes 3145732
  11.7 0.7 %copy-start.8 = (s32[1,8,256]{2,1,0:T(8,128)S(1)}, s32[1,8,256]{2,1,0:T(8,128)}, u32[]{:S(2)}) copy-start(s32[1,8,256]{2,1,0:T(8,128)} %param.18) | copy-start | bytes 24580
  13.1 29.6 %copy-start.5 = (bf16[256,256]{1,0:T(8,128)(2,1)S(1)}, bf16[256,256]{1,0:T(8,128)(2,1)}, u32[]{:S(2)}) copy-start(bf16[256,256]{1,0:T(8,128)(2,1)} %refs_6_.1) | copy-start | bytes 393220
  13.1 29.6 %copy-start.12 = (s32[144]{0:T(256)S(1)}, s32[144]{0:T(256)}, u32[]{:S(2)}) copy-start(s32[144]{0:T(256)} %refs_0_.1) | copy-start | bytes 1732
  13.1 29.6 %copy-start.13 = (s32[144]{0:T(256)S(1)}, s32[144]{0:T(256)}, u32[]{:S(2)}) copy-start(s32[144]{0:T(256)} %refs_1_.1) | copy-start | bytes 1732
  14.4 37.1 %collective-permute-start.10 = (bf16[512,256]{1,0:T(8,128)(2,1)S(1)}, bf16[512,256]{1,0:T(8,128)(2,1)S(1)}, u32[]{:S(2)}, u32[]{:S(2)}) collective-permute-start(bf16[512,256]{1,0:T(8,128)(2,1)S(1)} %get-tuple-element.16), channel_id=1, source_target_pairs={{0,24},{4,28},{8,16},{12,20},{16,8},{20,12},{24,0},{28,4},{1,25},{... | collective-permute-start | bytes 786440 | tf_op jit(solution)/shard_map/ppermute | solution.py:199
  15.9 26.7 %collective-permute-start.7 = (bf16[512,256]{1,0:T(8,128)(2,1)S(1)}, bf16[512,256]{1,0:T(8,128)(2,1)S(1)}, u32[]{:S(2)}, u32[]{:S(2)}) collective-permute-start(bf16[512,256]{1,0:T(8,128)(2,1)S(1)} %collective-permute-done.6.refs_14_), channel_id=1, source_target_pairs={{0,4},{4,0},{8,12},{12,8},{16,20},{20,16},{24,28},{28,24},{1,5},{5... | collective-permute-start | bytes 786440 | tf_op jit(solution)/shard_map/ppermute | solution.py:199
  16.9 25.8 %collective-permute-start.9 = (bf16[512,256]{1,0:T(8,128)(2,1)S(1)}, bf16[512,256]{1,0:T(8,128)(2,1)S(1)}, u32[]{:S(2)}, u32[]{:S(2)}) collective-permute-start(bf16[512,256]{1,0:T(8,128)(2,1)S(1)} %collective-permute-done.8.refs_16_), channel_id=1, source_target_pairs={{0,4},{4,0},{8,12},{12,8},{16,20},{20,16},{24,28},{28,24},{1,5},{5... | collective-permute-start | bytes 786440 | tf_op jit(solution)/shard_map/ppermute | solution.py:199
  23.5 5.7 %collective-permute-start.3 = (bf16[128,256]{1,0:T(8,128)(2,1)S(1)}, bf16[128,256]{1,0:T(8,128)(2,1)S(1)}, u32[]{:S(2)}, u32[]{:S(2)}) collective-permute-start(bf16[128,256]{1,0:T(8,128)(2,1)S(1)} %constant_dynamic-slice_fusion), channel_id=1, source_target_pairs={{0,3},{1,2},{2,1},{3,0},{4,7},{5,6},{6,5},{7,4},{8,11},{9,10},{10,... | collective-permute-start | bytes 196616 | tf_op jit(solution)/shard_map/ppermute | solution.py:199
  26.8 5.6 %collective-permute-start.1 = (bf16[128,256]{1,0:T(8,128)(2,1)S(1)}, bf16[128,256]{1,0:T(8,128)(2,1)S(1)}, u32[]{:S(2)}, u32[]{:S(2)}) collective-permute-start(bf16[128,256]{1,0:T(8,128)(2,1)S(1)} %constant_dynamic-slice_fusion), channel_id=1, source_target_pairs={{0,2},{1,3},{2,0},{3,1},{4,6},{5,7},{6,4},{7,5},{8,10},{9,11},{10,... | collective-permute-start | bytes 196616 | tf_op jit(solution)/shard_map/ppermute | solution.py:199
  29.2 3.3 %collective-permute-start.4 = (bf16[128,256]{1,0:T(8,128)(2,1)S(1)}, bf16[128,256]{1,0:T(8,128)(2,1)S(1)}, u32[]{:S(2)}, u32[]{:S(2)}) collective-permute-start(bf16[128,256]{1,0:T(8,128)(2,1)S(1)} %collective-permute-done.3.refs_10_), channel_id=1, source_target_pairs={{0,4},{4,0},{8,12},{12,8},{16,20},{20,16},{24,28},{28,24},{1,5},{5... | collective-permute-start | bytes 196616 | tf_op jit(solution)/shard_map/ppermute | solution.py:199
  32.5 10.2 %collective-permute-start = (bf16[256,256]{1,0:T(8,128)(2,1)}, bf16[256,256]{1,0:T(8,128)(2,1)S(1)}, u32[]{:S(2)}, u32[]{:S(2)}) collective-permute-start(bf16[256,256]{1,0:T(8,128)(2,1)} %refs_6_.1), channel_id=1, source_target_pairs={{0,1},{1,0},{2,3},{3,2},{4,5},{5,4},{6,7},{7,6},{8,9},{9,8},{10,11... | collective-permute-start | bytes 393224 | tf_op jit(solution)/shard_map/ppermute | solution.py:199
  32.6 10.1 %collective-permute-start.2 = (bf16[128,256]{1,0:T(8,128)(2,1)S(1)}, bf16[128,256]{1,0:T(8,128)(2,1)S(1)}, u32[]{:S(2)}, u32[]{:S(2)}) collective-permute-start(bf16[128,256]{1,0:T(8,128)(2,1)S(1)} %collective-permute-done.1.refs_8_), channel_id=1, source_target_pairs={{0,4},{4,0},{8,12},{12,8},{16,20},{20,16},{24,28},{28,24},{1,5},{5... | collective-permute-start | bytes 196616 | tf_op jit(solution)/shard_map/ppermute | solution.py:199
  34.0 2.2 %copy-start.4 = (bf16[128,128,128]{2,1,0:T(8,128)(2,1)S(1)}, bf16[128,128,128]{2,1,0:T(8,128)(2,1)}, u32[]{:S(2)}) copy-start(bf16[128,128,128]{2,1,0:T(8,128)(2,1)} %tiles_ref.1) | copy-start | bytes 12582916
  36.9 0.7 %copy-start.15 = (s32[128]{0:T(128)S(1)}, s32[128]{0:T(128)}, u32[]{:S(2)}) copy-start(s32[128]{0:T(128)} %live_ref.1) | copy-start | bytes 1540
  41.3 1.3 %copy-start.3 = (f32[2048,256]{1,0:T(8,128)}, f32[2048,256]{1,0:T(8,128)S(1)}, u32[]{:S(2)}) copy-start(f32[2048,256]{1,0:T(8,128)S(1)} %local.1.refs_5_) | copy-start | bytes 6291460
  42.7 8.9 %copy-start.6 = (bf16[256,256]{1,0:T(8,128)(2,1)S(1)}, bf16[256,256]{1,0:T(8,128)(2,1)}, u32[]{:S(2)}) copy-start(bf16[256,256]{1,0:T(8,128)(2,1)} %weight_ref.1) | copy-start | bytes 393220
  (3 other events, 2.0 us)

commit v2 on v1

v2 whole, which is shorter than its diff:
```python
import functools

import jax
import jax.numpy as jnp
from jax import lax
from jax.experimental import pallas as pl
from jax.experimental.pallas import tpu as pltpu
from jax.sharding import PartitionSpec as P

BF = jnp.bfloat16
F32 = jnp.float32
I32 = jnp.int32
VMEM = pl.BlockSpec(memory_space=pltpu.VMEM)
SMEM = pl.BlockSpec(memory_space=pltpu.SMEM)
HBM = pl.BlockSpec(memory_space=pltpu.HBM)
MIB = 1 << 20


def params(mib):
    return pltpu.CompilerParams(vmem_limit_bytes=mib * MIB)


def hbm(*arrays):
    return [pltpu.with_memory_space_constraint(x, pltpu.HBM) for x in arrays]


def dot(a, b):
    return jnp.dot(a, b, preferred_element_type=F32)


def gather_rows(send_ref, count_ref, feat_ref, peer):
    slots = send_ref.shape[1]
    rows = feat_ref.shape[0]
    index = send_ref[pl.ds(peer, 1), :]
    slot = lax.broadcasted_iota(I32, (1, slots), 1)
    index = jnp.where(slot < count_ref[0, peer], index, -1)
    lane = lax.broadcasted_iota(I32, (128, 128), 1)
    picks = []
    for part in range(slots // 128):
        column = jnp.broadcast_to(index[:, part * 128 : (part + 1) * 128], (128, 128)).T
        picks.append(
            jnp.concatenate(
                [jnp.where(column == lane + c * 128, 1.0, 0.0).astype(BF) for c in range(rows // 128)], axis=1
            )
        )
    return dot(jnp.concatenate(picks, axis=0), feat_ref[...]).astype(BF)


def pack_kernel(offsets, *refs):
    send_hbm, count_hbm, feat_hbm, hub_hbm, tiles_hbm = refs[:5]
    table_hbm = refs[5:10]
    feat_ref, hub_ref, tiles_ref, local_map, edge_map, hub_live_ref = refs[10:16]
    packed = refs[16 : 16 + len(offsets)]
    send_ref, count_ref, *tables, sems = refs[16 + len(offsets) :]
    local_ids, local_live, edge_ids, edge_live = tables
    copies = [
        pltpu.make_async_copy(source, target, sems.at[n])
        for n, (source, target) in enumerate(
            [
                (feat_hbm, feat_ref),
                (send_hbm, send_ref),
                (count_hbm, count_ref),
                (hub_hbm, hub_ref),
                *zip(table_hbm, (local_ids, local_live, edge_ids, edge_live, hub_live_ref)),
                (tiles_hbm, tiles_ref),
            ]
        )
    ]
    for copy in copies[:-1]:
        copy.start()
    for copy in copies[:-1]:
        copy.wait()
    copies[-1].start()
    me = lax.axis_index("row")
    slots = send_ref.shape[1]
    for n, group in enumerate(offsets):
        for k, offset in enumerate(group):
            packed[n][k * slots : (k + 1) * slots, :] = gather_rows(send_ref, count_ref, feat_ref, me ^ offset)
    fill_map(local_ids, local_live, local_map)
    fill_map(edge_ids, edge_live, edge_map)
    copies[-1].wait()


def pack(offsets, send_rows, send_count, features, hub_feats, local_tiles, tables, cells):
    slots, width = send_rows.shape[1], features.shape[1]
    total = sum(len(group) for group in offsets) * slots
    local_cells, edge_cells = cells
    return pl.pallas_call(
        functools.partial(pack_kernel, offsets),
        out_shape=[
            jax.ShapeDtypeStruct(features.shape, BF),
            jax.ShapeDtypeStruct(hub_feats.shape, BF),
            jax.ShapeDtypeStruct(local_tiles.shape, BF),
            jax.ShapeDtypeStruct((local_cells,), I32),
            jax.ShapeDtypeStruct((edge_cells,), I32),
            jax.ShapeDtypeStruct(tables[-1].shape, I32),
        ]
        + [jax.ShapeDtypeStruct((len(group) * slots, width), BF) for group in offsets],
        in_specs=[HBM] * 10,
        out_specs=[VMEM, VMEM, VMEM, SMEM, SMEM, SMEM] + [VMEM] * len(offsets),
        scratch_shapes=[pltpu.VMEM(send_rows.shape, I32), pltpu.SMEM(send_count.shape, I32)]
        + [pltpu.SMEM(table.shape, I32) for table in tables[:-1]]
        + [pltpu.SemaphoreType.DMA((10,))],
        compiler_params=params(16),
        cost_estimate=pl.CostEstimate(flops=0, bytes_accessed=0, transcendentals=0),
        name="pack",
    )(*hbm(send_rows, send_count, features, hub_feats, local_tiles, *tables))


def fill_map(ids_ref, live_ref, map_ref):
    for cell in range(map_ref.shape[0]):
        map_ref[cell] = -1
    for t in range(ids_ref.shape[0]):
        map_ref[ids_ref[t]] = jnp.where(live_ref[t] > 0, t, -1)


def cell_tile(tiles_ref, map_ref, cell):
    slot = map_ref[cell]
    tile = tiles_ref[jnp.maximum(slot, 0)]
    return jnp.where(slot >= 0, tile, jnp.zeros_like(tile))


def local_kernel(block, map_ref, tiles_ref, feat_ref, edge_hbm, adj_hbm, out_ref, edge_ref, adj_ref, sems):
    copies = [
        pltpu.make_async_copy(adj_hbm, adj_ref, sems.at[0]),
        pltpu.make_async_copy(edge_hbm, edge_ref, sems.at[1]),
    ]
    for copy in copies:
        copy.start()
    size = tiles_ref.shape[1]
    cols = feat_ref.shape[0] // size

    def body(m, _):
        rows = [
            jnp.concatenate([cell_tile(tiles_ref, map_ref, (m * block + i) * cols + j) for j in range(cols)], axis=1)
            for i in range(block)
        ]
        start = pl.multiple_of(m * block * size, block * size)
        out_ref[pl.ds(start, block * size), :] = dot(jnp.concatenate(rows, axis=0), feat_ref[...])
        return 0

    lax.fori_loop(0, out_ref.shape[0] // (block * size), body, 0)
    for copy in copies:
        copy.wait()


def local_term(local_map, tiles, features, edge_tiles, adj):
    return pl.pallas_call(
        functools.partial(local_kernel, 4),
        out_shape=[
            jax.ShapeDtypeStruct(features.shape, F32),
            jax.ShapeDtypeStruct(edge_tiles.shape, BF),
            jax.ShapeDtypeStruct(adj.shape, BF),
        ],
        in_specs=[SMEM, VMEM, VMEM, HBM, HBM],
        out_specs=[VMEM] * 3,
        scratch_shapes=[pltpu.SemaphoreType.DMA((2,))],
        compiler_params=params(16),
        cost_estimate=pl.CostEstimate(flops=0, bytes_accessed=0, transcendentals=0),
        name="local",
    )(local_map, tiles, features, *hbm(edge_tiles, adj))


def edge_kernel(block, pieces, late, hubs, counts, *refs):
    map_ref, hub_live_ref, tiles_ref, adj_ref, acc_ref = refs[:5]
    array_refs = refs[5 : 5 + counts]
    out_ref, late_ref, rhs_ref = refs[5 + counts :]
    me, loop = lax.axis_index("row"), lax.axis_index("loop")
    core = lax.rem(me, 2)
    size = tiles_ref.shape[1]
    rows, depth = adj_ref.shape
    cols = map_ref.shape[0] // (rows // size)
    slots = late_ref.shape[1] // len(late)
    per = slots // size
    for array, even, odd in hubs:
        shard = array_refs[array].shape[0]
        owner = loop ^ jnp.where(core == 0, even, odd)
        rhs_ref[pl.ds(pl.multiple_of(owner * shard, shard), shard), :] = array_refs[array][...]
    for n, (array, first, offset) in enumerate(pieces):
        rhs_ref[depth + n * slots : depth + (n + 1) * slots, :] = array_refs[array][first : first + slots, :]

    def body(m, _):
        blocks = []
        for i in range(block):
            row = m * block + i
            start = pl.multiple_of(row * size, size)
            line = []
            for b in range(depth // size):
                cell = adj_ref[pl.ds(start, size), b * size : (b + 1) * size]
                line.append(jnp.where(hub_live_ref[b, row] > 0, cell, jnp.zeros_like(cell)))
            for array, first, offset in pieces:
                for j in range(per):
                    line.append(cell_tile(tiles_ref, map_ref, row * cols + (me ^ offset) * per + j))
            blocks.append(jnp.concatenate(line, axis=1))
            for n, offset in enumerate(late):
                for j in range(per):
                    at = n * slots + j * size
                    late_ref[pl.ds(start, size), at : at + size] = cell_tile(
                        tiles_ref, map_ref, row * cols + (me ^ offset) * per + j
                    )
        span = pl.ds(pl.multiple_of(m * block * size, block * size), block * size)
        out_ref[span, :] = acc_ref[span, :] + dot(jnp.concatenate(blocks, axis=0), rhs_ref[...])
        return 0

    lax.fori_loop(0, rows // (block * size), body, 0)


def edge_term(pieces, late, hubs, slots, edge_map, hub_live, tiles, adj, acc, arrays):
    rows, depth = adj.shape
    deep = depth + len(pieces) * slots
    return pl.pallas_call(
        functools.partial(edge_kernel, 4, pieces, late, hubs, len(arrays)),
        out_shape=[jax.ShapeDtypeStruct(acc.shape, F32), jax.ShapeDtypeStruct((rows, len(late) * slots), BF)],
        in_specs=[SMEM, SMEM, VMEM, VMEM, VMEM] + [VMEM] * len(arrays),
        out_specs=[VMEM, VMEM],
        scratch_shapes=[pltpu.VMEM((deep, acc.shape[1]), BF)],
        compiler_params=params(16),
        cost_estimate=pl.CostEstimate(flops=0, bytes_accessed=0, transcendentals=0),
        name="edge",
    )(edge_map, hub_live, tiles, adj, acc, *arrays)


def last_kernel(block, counts, acc_ref, late_ref, weight_ref, *refs):
    array_refs = refs[:counts]
    out_ref, stage_ref, sems = refs[counts:]
    depth = array_refs[0].shape[0]
    for m in range(acc_ref.shape[0] // block):
        span = slice(m * block, (m + 1) * block)
        total = acc_ref[span, :]
        for n in range(counts):
            total += dot(late_ref[span, n * depth : (n + 1) * depth], array_refs[n][...])
        stage_ref[span, :] = jnp.maximum(dot(total.astype(BF), weight_ref[...]), 0.0).astype(BF)
        pltpu.make_async_copy(stage_ref.at[span], out_ref.at[span], sems.at[m]).start()
    for m in range(acc_ref.shape[0] // block):
        span = slice(m * block, (m + 1) * block)
        pltpu.make_async_copy(stage_ref.at[span], out_ref.at[span], sems.at[m]).wait()


def last_term(acc, late, weight, arrays):
    block = 512
    return pl.pallas_call(
        functools.partial(last_kernel, block, len(arrays)),
        out_shape=jax.ShapeDtypeStruct(acc.shape, BF),
        in_specs=[VMEM] * (3 + len(arrays)),
        out_specs=HBM,
        scratch_shapes=[pltpu.VMEM(acc.shape, BF), pltpu.SemaphoreType.DMA((acc.shape[0] // block,))],
        compiler_params=params(16),
        cost_estimate=pl.CostEstimate(flops=0, bytes_accessed=0, transcendentals=0),
        name="last",
    )(acc, late, weight, *arrays)


def swap(x, axis, offset):
    return lax.ppermute(x, axis, [(i, i ^ offset) for i in range(lax.axis_size(axis))])


def swap_by_core(x, even, odd):
    peers, ring = lax.axis_size("row"), lax.axis_size("loop")
    pairs = [(r * ring + l, r * ring + (l ^ (odd if r % 2 else even))) for r in range(peers) for l in range(ring)]
    return lax.ppermute(x, ("row", "loop"), pairs)


def per_device(
    features,
    weight,
    local_tiles,
    local_ids,
    local_live,
    send_rows,
    send_count,
    edge_tiles,
    edge_ids,
    edge_live,
    hub_feats,
    hub_adj,
    hub_live,
):
    peers, ring = lax.axis_size("row"), lax.axis_size("loop")
    slots = send_rows.shape[2]
    size = local_tiles.shape[1]
    tile_rows = features.shape[0] // size
    chips = range(2, peers, 2)
    early = [c for c in chips if c & (c - 1) == 0]
    late = [c ^ bit for c in chips if c & (c - 1) != 0 for bit in (0, 1)]
    offsets = [(c, c ^ 1) for c in early] + [(c,) for c in late] + [(1,), (0,)]
    feat, hub, tiles, local_map, edge_map, live, *packed = pack(
        offsets,
        send_rows[0],
        send_count,
        features,
        hub_feats,
        local_tiles,
        (local_ids, local_live, edge_ids, edge_live, hub_live.T),
        (tile_rows * tile_rows, tile_rows * (peers * slots // size)),
    )
    from_early = [swap(x, "row", c) for x, c in zip(packed, early)]
    from_late = [swap(x, "row", c) for x, c in zip(packed[len(early) :], late)]
    from_core, own = swap(packed[-2], "row", 1), packed[-1]
    arrays = [hub, swap(hub, "loop", 1)]
    hubs = [(0, 0, 0), (1, 1, 1)]
    halves = [swap_by_core(hub, offset, offset + 1) for offset in range(2, ring, 2)]
    acc, edges, adj = local_term(local_map, tiles, feat, edge_tiles, hub_adj)
    acc, *from_early = lax.optimization_barrier((acc, *from_early))
    shared = [swap(x, "row", 1) for x in from_early]
    acc, *halves = lax.optimization_barrier((acc, *halves))
    for n, got in enumerate(halves):
        hubs += [(len(arrays), 2 * n + 2, 2 * n + 3), (len(arrays) + 1, 2 * n + 3, 2 * n + 2)]
        arrays += [got, swap(got, "row", 1)]
    pieces = [(len(arrays), 0, 0), (len(arrays) + 1, 0, 1)]
    arrays += [own, from_core]
    for c, x, y in zip(early, from_early, shared):
        pieces += [(len(arrays), 0, c), (len(arrays) + 1, slots, c ^ 1)]
        arrays += [x, y]
    acc, late_tiles = edge_term(pieces, late, hubs, slots, edge_map, live, edges, adj, acc, arrays)
    return last_term(acc, late_tiles, weight, from_late)


def solution(mesh):
    both = ("row", "loop")
    placed = (
        P(both, None),
        P(),
        P(both, None, None),
        P(both),
        P(both),
        P(both, None, None),
        P(both, None),
        P(both, None, None),
        P(both),
        P(both),
        P("loop", None),
        P(both, None),
        P(both, None),
    )
    return jax.shard_map(per_device, mesh=mesh, in_specs=placed, out_specs=P(both, None), check_vma=False)
```

time: 55 us -> 33.9 us (0.62); the launches traced: 54 us -> 33.8 us
  local copies, waits for them, and re-layouts: 12.3 us -> 0.01 us
  waiting for transfers between devices: 6.54 us -> 3.32 us
  starting transfers between devices: 15.6 us -> 13.1 us
  Pallas kernels: 19.6 us -> 17.2 us
    unnamed x33 -> x2, local copies, waits for them, and re-layouts: 11.4 us -> 0.01 us
    ppermute x11 -> x9, starting transfers between devices: 15.6 us -> 9.81 us  [swap(): lax.ppermute(x, axis, [(i, i ^ offset) for i in range(lax.axis_size(axis))])]
    pallas_call x1, Pallas kernels: 8.84 us -> 4.73 us  [edge_term(): pl.pallas_call(functools.partial(edge_kernel, 4, pieces, late, hubs, len(...]
    ppermute x0 -> x1, starting transfers between devices: none -> 3.32 us  [swap_by_core(): return lax.ppermute(x, ('row', 'loop'), pairs)]
    ppermute x11 -> x9, waiting for transfers between devices: 6.54 us -> 3.32 us  [swap(): lax.ppermute(x, axis, [(i, i ^ offset) for i in range(lax.axis_size(axis))])]
    pallas_call x2 -> x1, Pallas kernels: 3.16 us -> 5.87 us  [pack(): pl.pallas_call(functools.partial(pack_kernel, offsets), out_shape=[jax.Sh...]
    pallas_call x2 -> x1, Pallas kernels: 5.09 us -> 4.18 us  [local_term(): pl.pallas_call(functools.partial(local_kernel, 4), out_shape=[jax.ShapeDt...]
    dynamic_slice x1 -> x0, local copies, waits for them, and re-layouts: 0.84 us -> none  [per_device(): lax.dynamic_slice(hub_feats, (core * half, 0), (half, hub_feats.shape[1]))]
  transfers between devices with their start and end apart: 11 -> 10, of which waited for: 4 -> 2; matrix products, arithmetic and copies ran while one was open for 3% -> 0% of each run, Pallas kernels for 29% -> 26%
where the time goes in v2:
time: 33.9 us; the launch traced here: 33.8 us
  Pallas kernels  17.2 us (51%)
  starting transfers between devices  13.1 us (39%)
  waiting for transfers between devices  3.32 us (10%)
    ppermute x9, starting transfers between devices, swap(): lax.ppermute(x, axis, [(i, i ^ offset) for i in range(lax.axis_size(axis))])  9.81 us
    pallas_call x1, Pallas kernels, pack(): pl.pallas_call(functools.partial(pack_kernel, offsets), out_shape=[jax.Sh...  5.87 us
    pallas_call x1, Pallas kernels, edge_term(): pl.pallas_call(functools.partial(edge_kernel, 4, pieces, late, hubs, len(...  4.73 us
    pallas_call x1, Pallas kernels, local_term(): pl.pallas_call(functools.partial(local_kernel, 4), out_shape=[jax.ShapeDt...  4.18 us
    ppermute x1, starting transfers between devices, swap_by_core(): return lax.ppermute(x, ('row', 'loop'), pairs)  3.32 us
    ppermute x9, waiting for transfers between devices, swap(): lax.ppermute(x, axis, [(i, i ^ offset) for i in range(lax.axis_size(axis))])  3.32 us
    pallas_call x1, Pallas kernels, last_term(): pl.pallas_call(functools.partial(last_kernel, block, len(arrays)), out_sh...  2.46 us
  transfers between devices with their start and end apart: 10, of which 2 were waited for; matrix products, arithmetic and copies ran while one was open for 0% of the time, Pallas kernels for 26%

profile of v2, /device:TPU:1, one launch (start us, length us, event | category | flops | bytes accessed | tf_op | source)
XLA Modules:
  0.0 33.8 jit_solution(95259477879423621)
XLA Ops:
  0.0 5.9 %pack.1 = (bf16[2048,256]{1,0:T(8,128)(2,1)S(1)}, bf16[256,256]{1,0:T(8,128)(2,1)S(1)}, bf16[128,128,128]{2,1,0:T(8,128)(2,1)S(1)}, s32[256]{0:T(256)S(1)}, s32[...) custom-call(s32[8,256]{1,0:T(8,128)} %bitcast.2, ...), custom_call_target="tpu_custom_call" | custom-call | tf_op jit(solution)/shard_map/pack/pallas_call | solution.py:88
  5.9 2.1 %collective-permute-start = (bf16[512,256]{1,0:T(8,128)(2,1)S(1)}, bf16[512,256]{1,0:T(8,128)(2,1)S(1)}, u32[]{:S(2)}, u32[]{:S(2)}) collective-permute-start(bf16[512,256]{1,0:T(8,128)(2,1)S(1)} %get-tuple-element.35), channel_id=1, source_target_pairs={{0,8},{4,12},{8,0},{12,4},{16,24},{20,28},{24,16},{28,20},{1,9},{5... | collective-permute-start | bytes 786440 | tf_op jit(solution)/shard_map/ppermute | solution.py:254
  8.0 1.2 %collective-permute-start.1 = (bf16[512,256]{1,0:T(8,128)(2,1)S(1)}, bf16[512,256]{1,0:T(8,128)(2,1)S(1)}, u32[]{:S(2)}, u32[]{:S(2)}) collective-permute-start(bf16[512,256]{1,0:T(8,128)(2,1)S(1)} %get-tuple-element.36), channel_id=1, source_target_pairs={{0,16},{4,20},{8,24},{12,28},{16,0},{20,4},{24,8},{28,12},{1,17},{... | collective-permute-start | bytes 786440 | tf_op jit(solution)/shard_map/ppermute | solution.py:254
  9.2 3.3 %collective-permute-start.2 = (bf16[256,256]{1,0:T(8,128)(2,1)S(1)}, bf16[256,256]{1,0:T(8,128)(2,1)S(1)}, u32[]{:S(2)}, u32[]{:S(2)}) collective-permute-start(bf16[256,256]{1,0:T(8,128)(2,1)S(1)} %get-tuple-element.38.refs_5_), channel_id=1, source_target_pairs={{0,2},{1,3},{2,0},{3,1},{4,7},{5,6},{6,5},{7,4},{8,10},{9,11},{10,... | collective-permute-start | bytes 393224 | tf_op jit(solution)/shard_map/ppermute | solution.py:260
  12.6 4.2 %local.1 = (f32[2048,256]{1,0:T(8,128)S(1)}, bf16[144,128,128]{2,1,0:T(8,128)(2,1)S(1)}, bf16[2048,1024]{1,0:T(8,128)(2,1)S(1)}) custom-call(s32[256]{0:T(256)S(1)} %get-tuple-element.29.map_ref, bf16[128,128,128]{2,1,0:T(8,128)(2,1)S(1)} %get-tuple-element.30.tiles_ref, bf16[2048,256]{1,0:T(8,128)(2,1)S(1)} %get-tuple-element.31.feat_ref, ...), custom_call_target="tpu_custom_call" | custom-call | tf_op jit(solution)/shard_map/local/pallas_call | solution.py:148
  16.7 0.0 collective-permute-done.refs_11_
  16.7 0.0 collective-permute-done.1.refs_13_
  16.8 0.6 %collective-permute-start.6 = (bf16[512,256]{1,0:T(8,128)(2,1)S(1)}, bf16[512,256]{1,0:T(8,128)(2,1)S(1)}, u32[]{:S(2)}, u32[]{:S(2)}) collective-permute-start(bf16[512,256]{1,0:T(8,128)(2,1)S(1)} %collective-permute-done.refs_11_), channel_id=1, source_target_pairs={{0,4},{4,0},{8,12},{12,8},{16,20},{20,16},{24,28},{28,24},{1,5},{5... | collective-permute-start | bytes 786440 | tf_op jit(solution)/shard_map/ppermute | solution.py:254
  17.3 0.1 collective-permute-start.7
  17.4 1.3 %collective-permute-start.3 = (bf16[256,256]{1,0:T(8,128)(2,1)S(1)}, bf16[256,256]{1,0:T(8,128)(2,1)S(1)}, u32[]{:S(2)}, u32[]{:S(2)}) collective-permute-start(bf16[256,256]{1,0:T(8,128)(2,1)S(1)} %get-tuple-element.38.refs_5_), channel_id=1, source_target_pairs={{0,1},{1,0},{2,3},{3,2},{4,5},{5,4},{6,7},{7,6},{8,9},{9,8},{10,11... | collective-permute-start | bytes 393224 | tf_op jit(solution)/shard_map/ppermute | solution.py:254
  18.7 0.7 %collective-permute-start.5 = (bf16[256,256]{1,0:T(8,128)(2,1)S(1)}, bf16[256,256]{1,0:T(8,128)(2,1)S(1)}, u32[]{:S(2)}, u32[]{:S(2)}) collective-permute-start(bf16[256,256]{1,0:T(8,128)(2,1)S(1)} %get-tuple-element.42), channel_id=1, source_target_pairs={{0,4},{4,0},{8,12},{12,8},{16,20},{20,16},{24,28},{28,24},{1,5},{5... | collective-permute-start | bytes 393224 | tf_op jit(solution)/shard_map/ppermute | solution.py:254
  19.4 0.0 collective-permute-done.2.refs_7_
  19.4 0.0 collective-permute-start.4
  19.4 2.6 %collective-permute-done.3.refs_6_ = bf16[256,256]{1,0:T(8,128)(2,1)S(1)} collective-permute-done((bf16[256,256]{1,0:T(8,128)(2,1)S(1)}, bf16[256,256]{1,0:T(8,128)(2,1)S(1)}, u32[]{:S(2)}, u32[]{:S(2)}) %collective-permute-start.3) | collective-permute-done | bytes 131104 | tf_op jit(solution)/shard_map/ppermute | solution.py:254
  22.0 0.4 %collective-permute-start.8 = (bf16[256,256]{1,0:T(8,128)(2,1)S(1)}, bf16[256,256]{1,0:T(8,128)(2,1)S(1)}, u32[]{:S(2)}, u32[]{:S(2)}) collective-permute-start(bf16[256,256]{1,0:T(8,128)(2,1)S(1)} %get-tuple-element.47), channel_id=1, source_target_pairs={{0,24},{4,28},{8,16},{12,20},{16,8},{20,12},{24,0},{28,4},{1,25},{... | collective-permute-start | bytes 393224 | tf_op jit(solution)/shard_map/ppermute | solution.py:254
  22.5 0.0 collective-permute-done.5.refs_10_
  22.5 3.4 %collective-permute-start.9 = (bf16[256,256]{1,0:T(8,128)(2,1)S(1)}, bf16[256,256]{1,0:T(8,128)(2,1)S(1)}, u32[]{:S(2)}, u32[]{:S(2)}) collective-permute-start(bf16[256,256]{1,0:T(8,128)(2,1)S(1)} %get-tuple-element.48), channel_id=1, source_target_pairs={{0,28},{4,24},{8,20},{12,16},{16,12},{20,8},{24,4},{28,0},{1,29},{... | collective-permute-start | bytes 393224 | tf_op jit(solution)/shard_map/ppermute | solution.py:254
  25.9 0.0 collective-permute-done.6.refs_12_
  25.9 0.0 collective-permute-done.7.refs_14_
  25.9 0.0 copy-start
  25.9 4.7 %edge.1 = (f32[2048,256]{1,0:T(8,128)S(1)}, bf16[2048,512]{1,0:T(8,128)(2,1)S(1)}) custom-call(s32[256]{0:T(256)S(1)} %get-tuple-element.27.refs_0_, s32[8,16]{1,0:T(8,128)S(1)} %get-tuple-element.28.refs_1_, bf16[144,128,128]{2,1,0:T(8,128)(2,1)S(1)} %get-tuple-element.32.refs_2_, bf16[2048,1024]{1,0:T(8,128)(2,1)S(1)} %get-tuple-element.33.refs_3_, ...), custom_call_target="tpu_custom_call" | custom-call | tf_op jit(solution)/shard_map/edge/pallas_call | solution.py:211
  30.6 0.0 collective-permute-done.8.refs_0_
  30.6 0.7 %collective-permute-done.9.refs_1_ = bf16[256,256]{1,0:T(8,128)(2,1)S(1)} collective-permute-done((bf16[256,256]{1,0:T(8,128)(2,1)S(1)}, bf16[256,256]{1,0:T(8,128)(2,1)S(1)}, u32[]{:S(2)}, u32[]{:S(2)}) %collective-permute-start.9) | collective-permute-done | bytes 131104 | tf_op jit(solution)/shard_map/ppermute | solution.py:254
  31.3 2.5 %last.1 = bf16[2048,256]{1,0:T(8,128)(2,1)} custom-call(f32[2048,256]{1,0:T(8,128)S(1)} %get-tuple-element.45.acc_ref, bf16[2048,512]{1,0:T(8,128)(2,1)S(1)} %get-tuple-element.46.late_ref, bf16[256,256]{1,0:T(8,128)(2,1)S(1)} %copy-done, bf16[256,256]{1,0:T(8,128)(2,1)S(1)} %collective-permute-done.8.refs_0_, ...), custom_call_target="tpu_custom_call" | custom-call | tf_op jit(solution)/shard_map/last/pallas_call | solution.py:241
  (2 shorter events, 0.0 us)
Async XLA Ops:
  5.9 10.9 %collective-permute-start = (bf16[512,256]{1,0:T(8,128)(2,1)S(1)}, bf16[512,256]{1,0:T(8,128)(2,1)S(1)}, u32[]{:S(2)}, u32[]{:S(2)}) collective-permute-start(bf16[512,256]{1,0:T(8,128)(2,1)S(1)} %get-tuple-element.35), channel_id=1, source_target_pairs={{0,8},{4,12},{8,0},{12,4},{16,24},{20,28},{24,16},{28,20},{1,9},{5... | collective-permute-start | bytes 786440 | tf_op jit(solution)/shard_map/ppermute | solution.py:254
  8.0 8.8 %collective-permute-start.1 = (bf16[512,256]{1,0:T(8,128)(2,1)S(1)}, bf16[512,256]{1,0:T(8,128)(2,1)S(1)}, u32[]{:S(2)}, u32[]{:S(2)}) collective-permute-start(bf16[512,256]{1,0:T(8,128)(2,1)S(1)} %get-tuple-element.36), channel_id=1, source_target_pairs={{0,16},{4,20},{8,24},{12,28},{16,0},{20,4},{24,8},{28,12},{1,17},{... | collective-permute-start | bytes 786440 | tf_op jit(solution)/shard_map/ppermute | solution.py:254
  9.2 10.2 %collective-permute-start.2 = (bf16[256,256]{1,0:T(8,128)(2,1)S(1)}, bf16[256,256]{1,0:T(8,128)(2,1)S(1)}, u32[]{:S(2)}, u32[]{:S(2)}) collective-permute-start(bf16[256,256]{1,0:T(8,128)(2,1)S(1)} %get-tuple-element.38.refs_5_), channel_id=1, source_target_pairs={{0,2},{1,3},{2,0},{3,1},{4,7},{5,6},{6,5},{7,4},{8,10},{9,11},{10,... | collective-permute-start | bytes 393224 | tf_op jit(solution)/shard_map/ppermute | solution.py:260
  16.8 9.1 %collective-permute-start.6 = (bf16[512,256]{1,0:T(8,128)(2,1)S(1)}, bf16[512,256]{1,0:T(8,128)(2,1)S(1)}, u32[]{:S(2)}, u32[]{:S(2)}) collective-permute-start(bf16[512,256]{1,0:T(8,128)(2,1)S(1)} %collective-permute-done.refs_11_), channel_id=1, source_target_pairs={{0,4},{4,0},{8,12},{12,8},{16,20},{20,16},{24,28},{28,24},{1,5},{5... | collective-permute-start | bytes 786440 | tf_op jit(solution)/shard_map/ppermute | solution.py:254
  17.3 8.5 %collective-permute-start.7 = (bf16[512,256]{1,0:T(8,128)(2,1)S(1)}, bf16[512,256]{1,0:T(8,128)(2,1)S(1)}, u32[]{:S(2)}, u32[]{:S(2)}) collective-permute-start(bf16[512,256]{1,0:T(8,128)(2,1)S(1)} %collective-permute-done.1.refs_13_), channel_id=1, source_target_pairs={{0,4},{4,0},{8,12},{12,8},{16,20},{20,16},{24,28},{28,24},{1,5},{5... | collective-permute-start | bytes 786440 | tf_op jit(solution)/shard_map/ppermute | solution.py:254
  17.4 4.6 %collective-permute-start.3 = (bf16[256,256]{1,0:T(8,128)(2,1)S(1)}, bf16[256,256]{1,0:T(8,128)(2,1)S(1)}, u32[]{:S(2)}, u32[]{:S(2)}) collective-permute-start(bf16[256,256]{1,0:T(8,128)(2,1)S(1)} %get-tuple-element.38.refs_5_), channel_id=1, source_target_pairs={{0,1},{1,0},{2,3},{3,2},{4,5},{5,4},{6,7},{7,6},{8,9},{9,8},{10,11... | collective-permute-start | bytes 393224 | tf_op jit(solution)/shard_map/ppermute | solution.py:254
  18.7 3.8 %collective-permute-start.5 = (bf16[256,256]{1,0:T(8,128)(2,1)S(1)}, bf16[256,256]{1,0:T(8,128)(2,1)S(1)}, u32[]{:S(2)}, u32[]{:S(2)}) collective-permute-start(bf16[256,256]{1,0:T(8,128)(2,1)S(1)} %get-tuple-element.42), channel_id=1, source_target_pairs={{0,4},{4,0},{8,12},{12,8},{16,20},{20,16},{24,28},{28,24},{1,5},{5... | collective-permute-start | bytes 393224 | tf_op jit(solution)/shard_map/ppermute | solution.py:254
  19.4 6.4 %collective-permute-start.4 = (bf16[256,256]{1,0:T(8,128)(2,1)S(1)}, bf16[256,256]{1,0:T(8,128)(2,1)S(1)}, u32[]{:S(2)}, u32[]{:S(2)}) collective-permute-start(bf16[256,256]{1,0:T(8,128)(2,1)S(1)} %collective-permute-done.2.refs_7_), channel_id=1, source_target_pairs={{0,4},{4,0},{8,12},{12,8},{16,20},{20,16},{24,28},{28,24},{1,5},{5... | collective-permute-start | bytes 393224 | tf_op jit(solution)/shard_map/ppermute | solution.py:254
  22.0 8.6 %collective-permute-start.8 = (bf16[256,256]{1,0:T(8,128)(2,1)S(1)}, bf16[256,256]{1,0:T(8,128)(2,1)S(1)}, u32[]{:S(2)}, u32[]{:S(2)}) collective-permute-start(bf16[256,256]{1,0:T(8,128)(2,1)S(1)} %get-tuple-element.47), channel_id=1, source_target_pairs={{0,24},{4,28},{8,16},{12,20},{16,8},{20,12},{24,0},{28,4},{1,25},{... | collective-permute-start | bytes 393224 | tf_op jit(solution)/shard_map/ppermute | solution.py:254
  22.5 8.8 %collective-permute-start.9 = (bf16[256,256]{1,0:T(8,128)(2,1)S(1)}, bf16[256,256]{1,0:T(8,128)(2,1)S(1)}, u32[]{:S(2)}, u32[]{:S(2)}) collective-permute-start(bf16[256,256]{1,0:T(8,128)(2,1)S(1)} %get-tuple-element.48), channel_id=1, source_target_pairs={{0,28},{4,24},{8,20},{12,16},{16,12},{20,8},{24,4},{28,0},{1,29},{... | collective-permute-start | bytes 393224 | tf_op jit(solution)/shard_map/ppermute | solution.py:254
  25.9 5.4 %copy-start = (bf16[256,256]{1,0:T(8,128)(2,1)S(1)}, bf16[256,256]{1,0:T(8,128)(2,1)}, u32[]{:S(2)}) copy-start(bf16[256,256]{1,0:T(8,128)(2,1)} %weight_ref.1) | copy-start | bytes 393220

commit v3 on v0

v3 whole, which is shorter than its diff:
```python
import functools

import jax
import jax.numpy as jnp
from jax import lax
from jax.experimental import pallas as pl
from jax.experimental.pallas import tpu as pltpu
from jax.sharding import PartitionSpec as P

BF = jnp.bfloat16
F32 = jnp.float32
I32 = jnp.int32
VMEM = pl.BlockSpec(memory_space=pltpu.VMEM)
SMEM = pl.BlockSpec(memory_space=pltpu.SMEM)
HBM = pl.BlockSpec(memory_space=pltpu.HBM)
ANY = pl.BlockSpec(memory_space=pl.ANY)
MIB = 1 << 20
FREE = pl.CostEstimate(flops=0, bytes_accessed=0, transcendentals=0)
LONG = pl.CostEstimate(flops=1 << 35, bytes_accessed=0, transcendentals=0)


def params(mib):
    return pltpu.CompilerParams(vmem_limit_bytes=mib * MIB)


def hbm(*arrays):
    return [pltpu.with_memory_space_constraint(x, pltpu.HBM) for x in arrays]


def dot(a, b):
    return jnp.dot(a, b, preferred_element_type=F32)


def picks(send_ref, count_ref, rows, peer):
    slots = send_ref.shape[1]
    index = send_ref[pl.ds(peer, 1), :]
    slot = lax.broadcasted_iota(I32, (1, slots), 1)
    peers = lax.broadcasted_iota(I32, count_ref.shape, 1)
    count = jnp.sum(jnp.where(peers == peer, count_ref[...], 0), axis=1, keepdims=True)
    index = jnp.where(slot < count, index, -1)
    lane = lax.broadcasted_iota(I32, (128, 128), 1)
    blocks = []
    for part in range(slots // 128):
        column = jnp.broadcast_to(index[:, part * 128 : (part + 1) * 128], (128, 128)).T
        line = [jnp.where(column == lane + c * 128, 1.0, 0.0).astype(BF) for c in range(rows // 128)]
        blocks.append(jnp.concatenate(line, axis=1))
    return jnp.concatenate(blocks, axis=0)


def gather_groups(offsets, send_ref, count_ref, feat_ref, packed):
    me = lax.axis_index("row")
    rows = feat_ref.shape[0]
    for out_ref, group in zip(packed, offsets):
        hot = [picks(send_ref, count_ref, rows, me ^ offset) for offset in group]
        out_ref[...] = dot(jnp.concatenate(hot, axis=0), feat_ref[...]).astype(BF)


def start_all(sources, targets, sems):
    copies = [pltpu.make_async_copy(x, y, sems.at[n]) for n, (x, y) in enumerate(zip(sources, targets))]
    for copy in copies:
        copy.start()
    return copies


def wait_all(copies):
    for copy in copies:
        copy.wait()


def pack_kernel(offsets, feat_hbm, send_hbm, count_hbm, hub_hbm, tiles_hbm, *refs):
    sources = [feat_hbm, send_hbm, count_hbm, hub_hbm, tiles_hbm]
    targets, (*packed, sems) = refs[:5], refs[5:]
    copies = [pltpu.make_async_copy(x, y, sems.at[n]) for n, (x, y) in enumerate(zip(sources, targets))]
    for copy in copies[:4]:
        copy.start()
    wait_all(copies[:4])
    copies[4].start()
    feat_ref, send_ref, count_ref = targets[:3]
    gather_groups(offsets, send_ref, count_ref, feat_ref, packed)
    copies[4].wait()


def pack(offsets, features, send_rows, send_count, hub_feats, tiles):
    slots, width = send_rows.shape[1], features.shape[1]
    arrays = (features, send_rows, send_count, hub_feats, tiles)
    return pl.pallas_call(
        functools.partial(pack_kernel, offsets),
        out_shape=[jax.ShapeDtypeStruct(x.shape, x.dtype) for x in arrays]
        + [jax.ShapeDtypeStruct((len(group) * slots, width), BF) for group in offsets],
        in_specs=[HBM] * 5,
        out_specs=[VMEM] * (5 + len(offsets)),
        scratch_shapes=[pltpu.SemaphoreType.DMA((5,))],
        compiler_params=params(16),
        cost_estimate=FREE,
        name="pack",
    )(*hbm(*arrays))


def more_kernel(offsets, feat_ref, send_ref, count_ref, *packed):
    gather_groups(offsets, send_ref, count_ref, feat_ref, packed)


def pack_more(offsets, features, send_rows, send_count):
    slots, width = send_rows.shape[1], features.shape[1]
    return pl.pallas_call(
        functools.partial(more_kernel, offsets),
        out_shape=[jax.ShapeDtypeStruct((len(group) * slots, width), BF) for group in offsets],
        in_specs=[VMEM] * 3,
        out_specs=[VMEM] * len(offsets),
        compiler_params=params(16),
        cost_estimate=FREE,
        name="more",
    )(features, send_rows, send_count)


def fill_map(ids_ref, live_ref, map_ref):
    for cell in range(map_ref.shape[0]):
        map_ref[cell] = -1
    for t in range(ids_ref.shape[0]):
        map_ref[ids_ref[t]] = jnp.where(live_ref[t] > 0, t, -1)


def cell_tile(tiles_ref, map_ref, cell):
    slot = map_ref[cell]
    tile = tiles_ref[jnp.maximum(slot, 0)]
    return jnp.where(slot >= 0, tile, jnp.zeros_like(tile))


def edge_line(tiles_ref, map_ref, row, cols, sources, per):
    return [cell_tile(tiles_ref, map_ref, row * cols + source * per + j) for source in sources for j in range(per)]


def local_kernel(block, offsets, tiles_ref, feat_ref, send_ref, count_ref, near_ref, *refs):
    del near_ref
    sources, (out_ref, edge_ref, adj_ref, map_hbm, *refs) = refs[:6], refs[6:]
    packed = refs[: len(offsets)]
    *tables, local_map, edge_map, sems = refs[len(offsets) :]
    copies = start_all(sources, [*tables, edge_ref, adj_ref], sems)
    gather_groups(offsets, send_ref, count_ref, feat_ref, packed)
    wait_all(copies[:4])
    fill_map(tables[0], tables[1], local_map)
    fill_map(tables[2], tables[3], edge_map)
    copies.append(pltpu.make_async_copy(edge_map, map_hbm, sems.at[6]))
    copies[6].start()
    size = tiles_ref.shape[1]
    rows = feat_ref.shape[0]
    cols = rows // size

    def body(m, _):
        blocks = []
        for i in range(block):
            row = m * block + i
            line = [cell_tile(tiles_ref, local_map, row * cols + j) for j in range(cols)]
            blocks.append(jnp.concatenate(line, axis=1))
        span = pl.ds(pl.multiple_of(m * block * size, block * size), block * size)
        out_ref[span, :] = dot(jnp.concatenate(blocks, axis=0), feat_ref[...])
        return 0

    lax.fori_loop(0, rows // (block * size), body, 0)
    wait_all(copies[4:])


def local_term(offsets, tiles, features, send_rows, send_count, near, tables, edges, adj):
    rows, width = features.shape
    peers, slots = send_rows.shape
    size = tiles.shape[1]
    local_cells, edge_cells = (rows // size) ** 2, (rows // size) * (peers * slots // size)
    return pl.pallas_call(
        functools.partial(local_kernel, 8, offsets),
        out_shape=[jax.ShapeDtypeStruct(features.shape, F32)]
        + [jax.ShapeDtypeStruct(x.shape, BF) for x in (edges, adj)]
        + [jax.ShapeDtypeStruct((edge_cells,), I32)]
        + [jax.ShapeDtypeStruct((len(group) * slots, width), BF) for group in offsets],
        in_specs=[VMEM] * 5 + [HBM] * 6,
        out_specs=[VMEM] * 3 + [ANY] + [VMEM] * len(offsets),
        scratch_shapes=[pltpu.SMEM(x.shape, I32) for x in tables]
        + [pltpu.SMEM((local_cells,), I32), pltpu.SMEM((edge_cells,), I32), pltpu.SemaphoreType.DMA((7,))],
        compiler_params=params(16),
        cost_estimate=FREE,
        name="local",
    )(tiles, features, send_rows, send_count, near, *hbm(*tables, edges, adj))


def stack_kernel(*refs):
    out_ref, at = refs[-1], 0
    for ref in refs[:-1]:
        out_ref[at : at + ref.shape[0], :] = ref[...]
        at += ref.shape[0]


def stack(arrays):
    return pl.pallas_call(
        stack_kernel,
        out_shape=jax.ShapeDtypeStruct((sum(x.shape[0] for x in arrays), arrays[0].shape[1]), BF),
        in_specs=[VMEM] * len(arrays),
        out_specs=VMEM,
        compiler_params=params(16),
        cost_estimate=LONG,
        name="stack",
    )(*arrays)


def last_kernel(block, pieces, hubs, counts, *refs):
    map_hbm, live_hbm, edge_ref, adj_ref, acc_ref, weight_ref = refs[:6]
    array_refs = refs[6 : 6 + counts]
    out_ref, edge_map, live_ref, rhs_ref, stage_ref, sems = refs[6 + counts :]
    size = edge_ref.shape[1]
    rows, depth = adj_ref.shape
    steps = rows // (block * size)
    tables = [
        pltpu.make_async_copy(map_hbm, edge_map, sems.at[steps]),
        pltpu.make_async_copy(live_hbm, live_ref, sems.at[steps + 1]),
    ]
    for copy in tables:
        copy.start()
    me, loop = lax.axis_index("row"), lax.axis_index("loop")
    core = lax.rem(me, 2)
    slots = (rhs_ref.shape[0] - depth) // len(pieces)
    cols = edge_map.shape[0] // (rows // size)
    for array, even, odd in hubs:
        shard = array_refs[array].shape[0]
        owner = loop ^ jnp.where(core == 0, even, odd)
        rhs_ref[pl.ds(pl.multiple_of(owner * shard, shard), shard), :] = array_refs[array][...]
    for n, (array, first, _) in enumerate(pieces):
        rhs_ref[depth + n * slots : depth + (n + 1) * slots, :] = array_refs[array][first : first + slots, :]
    sources = [me ^ offset for _, _, offset in pieces]
    wait_all(tables)

    def write(m):
        span = pl.ds(pl.multiple_of(m * block * size, block * size), block * size)
        return pltpu.make_async_copy(stage_ref.at[span], out_ref.at[span], sems.at[m])

    def body(m, _):
        blocks = []
        for i in range(block):
            row = m * block + i
            start = pl.multiple_of(row * size, size)
            line = []
            for b in range(depth // size):
                cell = adj_ref[pl.ds(start, size), b * size : (b + 1) * size]
                line.append(jnp.where(live_ref[b, row] > 0, cell, jnp.zeros_like(cell)))
            line += edge_line(edge_ref, edge_map, row, cols, sources, slots // size)
            blocks.append(jnp.concatenate(line, axis=1))
        span = pl.ds(pl.multiple_of(m * block * size, block * size), block * size)
        total = (acc_ref[span, :] + dot(jnp.concatenate(blocks, axis=0), rhs_ref[...])).astype(BF)
        stage_ref[span, :] = jnp.maximum(dot(total, weight_ref[...]), 0.0).astype(BF)
        write(m).start()
        return 0

    lax.fori_loop(0, steps, body, 0)
    for m in range(steps):
        write(m).wait()


def last_term(pieces, hubs, slots, edge_map, hub_live, edges, adj, acc, weight, arrays):
    block = 8
    rows, width = acc.shape
    return pl.pallas_call(
        functools.partial(last_kernel, block, pieces, hubs, len(arrays)),
        out_shape=jax.ShapeDtypeStruct(acc.shape, BF),
        in_specs=[ANY, HBM] + [VMEM] * (4 + len(arrays)),
        out_specs=HBM,
        scratch_shapes=[
            pltpu.SMEM(edge_map.shape, I32),
            pltpu.SMEM(hub_live.shape, I32),
            pltpu.VMEM((adj.shape[1] + len(pieces) * slots, width), BF),
            pltpu.VMEM(acc.shape, BF),
            pltpu.SemaphoreType.DMA((rows // (block * edges.shape[1]) + 2,)),
        ],
        compiler_params=params(16),
        cost_estimate=FREE,
        name="last",
    )(edge_map, *hbm(hub_live), edges, adj, acc, weight, *arrays)


def swap(x, axis, offset):
    return lax.ppermute(x, axis, [(i, i ^ offset) for i in range(lax.axis_size(axis))])


def swap_by_core(x, even, odd):
    peers, ring = lax.axis_size("row"), lax.axis_size("loop")
    pairs = [(r * ring + l, r * ring + (l ^ (odd if r % 2 else even))) for r in range(peers) for l in range(ring)]
    return lax.ppermute(x, ("row", "loop"), pairs)


def per_device(
    features,
    weight,
    local_tiles,
    local_ids,
    local_live,
    send_rows,
    send_count,
    edge_tiles,
    edge_ids,
    edge_live,
    hub_feats,
    hub_adj,
    hub_live,
):
    peers, ring = lax.axis_size("row"), lax.axis_size("loop")
    slots = send_rows.shape[2]
    size = local_tiles.shape[1]
    tile_rows = features.shape[0] // size
    chips = range(2, peers, 2)
    early = [c for c in chips if c & (c - 1) == 0]
    late = [c ^ bit for c in chips if c not in early for bit in (0, 1)]
    feat, sends, counts, hub, tiles, *packed = pack(
        [(c, c ^ 1) for c in early], features, send_rows[0], send_count, hub_feats, local_tiles
    )
    from_early = [swap(x, "row", c) for x, c in zip(packed, early)]
    packed = pack_more([(c,) for c in late], feat, sends, counts)
    from_late = [swap(x, "row", c) for x, c in zip(packed, late)]
    near = swap(hub, "loop", 1)
    far = [swap_by_core(hub, offset, offset + 1) for offset in range(2, ring, 2)]
    acc, edges, adj, edge_map, to_core, own = local_term(
        [(1,), (0,)],
        tiles,
        feat,
        sends,
        counts,
        near,
        (local_ids, local_live, edge_ids, edge_live),
        edge_tiles,
        hub_adj,
    )
    from_core = swap(to_core, "row", 1)
    from_early = lax.optimization_barrier(tuple(from_early))
    acc, *ready = lax.optimization_barrier((acc, *from_early, *far))
    from_early, far = ready[: len(early)], ready[len(early) :]
    pieces, arrays = [(0, 0, 0), (1, 0, 1)], [own, from_core]
    for c, x in zip(early, from_early):
        pieces += [(len(arrays), 0, c), (len(arrays) + 1, slots, c ^ 1)]
        arrays += [x, swap(x, "row", 1)]
    pieces += [(len(arrays), n * slots, c) for n, c in enumerate(late)]
    arrays.append(stack(from_late))
    hubs = [(len(arrays), 0, 0), (len(arrays) + 1, 1, 1)]
    arrays += [hub, near]
    for n, x in enumerate(far):
        hubs += [(len(arrays), 2 * n + 2, 2 * n + 3), (len(arrays) + 1, 2 * n + 3, 2 * n + 2)]
        arrays += [x, swap(x, "row", 1)]
    return last_term(pieces, hubs, slots, edge_map, hub_live.T, edges, adj, acc, weight, arrays)


def solution(mesh):
    both = ("row", "loop")
    placed = (
        P(both, None),
        P(),
        P(both, None, None),
        P(both),
        P(both),
        P(both, None, None),
        P(both, None),
        P(both, None, None),
        P(both),
        P(both),
        P("loop", None),
        P(both, None),
        P(both, None),
    )
    return jax.shard_map(per_device, mesh=mesh, in_specs=placed, out_specs=P(both, None), check_vma=False)
```

time: 172 us -> 28.6 us (0.17)
  matrix products: 74.4 us -> 0 us
  local copies, waits for them, and re-layouts: 71.5 us -> 0.01 us
  blocking collectives: 15.9 us -> 0 us
  Pallas kernels: 0 us -> 14.3 us
  starting transfers between devices: 5.22 us -> 12.5 us
  other arithmetic: 2.74 us -> 0 us
    dot_general x7 -> x0, matrix products: 74.4 us -> none  [the longest x2 29.4 us: tile_term(): jnp.dot(row_select, products.reshape(tile_ids.shape[0], tile_size * width...]
    unnamed x22 -> x2, local copies, waits for them, and re-layouts: 38.1 us -> 0.01 us
    dot_general x1 -> x0, local copies, waits for them, and re-layouts: 17.7 us -> none  [tile_term(): jnp.einsum('tab,tbf->taf', tile_set, gathered, preferred_element_type=jnp...]
    all_gather x1 -> x0, blocking collectives: 15.9 us -> none  [per_device(): lax.all_gather(hub_feats, 'loop', axis=0, tiled=True)]
    pallas_call x0 -> x5, Pallas kernels: none -> 14.3 us  [the longest x1 5.7 us: last_term(): pl.pallas_call(functools.partial(last_kernel, block, pieces, hubs, len(ar...]
    ppermute x0 -> x10, starting transfers between devices: none -> 12.5 us  [the longest x9 10.3 us: swap(): lax.ppermute(x, axis, [(i, i ^ offset) for i in range(lax.axis_size(axis))])]
    gather x1 -> x0, local copies, waits for them, and re-layouts: 8.09 us -> none  [per_device(): picked = features[send_rows[0]]]
    all_to_all x1 -> x0, starting transfers between devices: 5.22 us -> none  [per_device(): lax.all_to_all(outgoing, 'row', split_axis=0, concat_axis=0, tiled=True)]
  transfers between devices with their start and end apart: 1 -> 10, of which waited for: 0 -> 2; matrix products, arithmetic and copies ran while one was open for 37% -> 0% of each run, Pallas kernels for 0% -> 18%
where the time goes in v3:
time: 28.6 us; the launch traced here: 28.1 us
  Pallas kernels  14.3 us (50%)
  starting transfers between devices  12.5 us (44%)
  waiting for transfers between devices  1.2 us (4%)
    ppermute x9, starting transfers between devices, swap(): lax.ppermute(x, axis, [(i, i ^ offset) for i in range(lax.axis_size(axis))])  10.3 us
    pallas_call x1, Pallas kernels, last_term(): pl.pallas_call(functools.partial(last_kernel, block, pieces, hubs, len(ar...  5.7 us
    pallas_call x1, Pallas kernels, local_term(): pl.pallas_call(functools.partial(local_kernel, 8, offsets), out_shape=[ja...  4.24 us
    pallas_call x1, Pallas kernels, pack(): pl.pallas_call(functools.partial(pack_kernel, offsets), out_shape=[jax.Sh...  3.5 us
    ppermute x1, starting transfers between devices, swap_by_core(): return lax.ppermute(x, ('row', 'loop'), pairs)  2.19 us
    ppermute x9, waiting for transfers between devices, swap(): lax.ppermute(x, axis, [(i, i ^ offset) for i in range(lax.axis_size(axis))])  1.2 us
    pallas_call x1, Pallas kernels, pack_more(): pl.pallas_call(functools.partial(more_kernel, offsets), out_shape=[jax.Sh...  0.85 us
  transfers between devices with their start and end apart: 10, of which 2 were waited for; matrix products, arithmetic and copies ran while one was open for 0% of the time, Pallas kernels for 18%

profile of v3, /device:TPU:1, one launch (start us, length us, event | category | flops | bytes accessed | tf_op | source)
XLA Modules:
  0.0 28.1 jit_solution(8110381809708689381)
XLA Ops:
  0.0 3.5 %pack.1 = (bf16[2048,256]{1,0:T(8,128)(2,1)S(1)}, s32[8,256]{1,0:T(8,128)S(1)}, s32[1,8]{1,0:T(1,128)S(1)}, bf16[256,256]{1,0:T(8,128)(2,1)S(1)}, bf16[128,128,1...) custom-call(bf16[2048,256]{1,0:T(8,128)(2,1)} %feat_hbm.1, s32[8,256]{1,0:T(8,128)} %bitcast.2, ...), custom_call_target="tpu_custom_call" | custom-call | tf_op jit(solution)/shard_map/pack/pallas_call | solution.py:86
  3.5 2.1 %collective-permute-start.1 = (bf16[512,256]{1,0:T(8,128)(2,1)S(1)}, bf16[512,256]{1,0:T(8,128)(2,1)S(1)}, u32[]{:S(2)}, u32[]{:S(2)}) collective-permute-start(bf16[512,256]{1,0:T(8,128)(2,1)S(1)} %get-tuple-element.35), channel_id=1, source_target_pairs={{0,8},{4,12},{8,0},{12,4},{16,24},{20,28},{24,16},{28,20},{1,9},{5... | collective-permute-start | bytes 786440 | tf_op jit(solution)/shard_map/ppermute | solution.py:277
  5.6 1.2 %collective-permute-start.2 = (bf16[512,256]{1,0:T(8,128)(2,1)S(1)}, bf16[512,256]{1,0:T(8,128)(2,1)S(1)}, u32[]{:S(2)}, u32[]{:S(2)}) collective-permute-start(bf16[512,256]{1,0:T(8,128)(2,1)S(1)} %get-tuple-element.36), channel_id=1, source_target_pairs={{0,16},{4,20},{8,24},{12,28},{16,0},{20,4},{24,8},{28,12},{1,17},{... | collective-permute-start | bytes 786440 | tf_op jit(solution)/shard_map/ppermute | solution.py:277
  6.9 1.3 %collective-permute-start = (bf16[256,256]{1,0:T(8,128)(2,1)S(1)}, bf16[256,256]{1,0:T(8,128)(2,1)S(1)}, u32[]{:S(2)}, u32[]{:S(2)}) collective-permute-start(bf16[256,256]{1,0:T(8,128)(2,1)S(1)} %get-tuple-element.30.refs_13_), channel_id=1, source_target_pairs={{0,1},{1,0},{2,3},{3,2},{4,5},{5,4},{6,7},{7,6},{8,9},{9,8},{10,11... | collective-permute-start | bytes 393224 | tf_op jit(solution)/shard_map/ppermute | solution.py:277
  8.1 2.2 %collective-permute-start.3 = (bf16[256,256]{1,0:T(8,128)(2,1)S(1)}, bf16[256,256]{1,0:T(8,128)(2,1)S(1)}, u32[]{:S(2)}, u32[]{:S(2)}) collective-permute-start(bf16[256,256]{1,0:T(8,128)(2,1)S(1)} %get-tuple-element.30.refs_13_), channel_id=1, source_target_pairs={{0,2},{1,3},{2,0},{3,1},{4,7},{5,6},{6,5},{7,4},{8,10},{9,11},{10,... | collective-permute-start | bytes 393224 | tf_op jit(solution)/shard_map/ppermute | solution.py:283
  10.3 0.8 %more.1 = (bf16[256,256]{1,0:T(8,128)(2,1)S(1)}, bf16[256,256]{1,0:T(8,128)(2,1)S(1)}) custom-call(bf16[2048,256]{1,0:T(8,128)(2,1)S(1)} %get-tuple-element.27.feat_ref, s32[8,256]{1,0:T(8,128)S(1)} %get-tuple-element.28.send_ref, s32[1,8]{1,0:T(1,128)S(1)} %get-tuple-element.29.count_ref), custom_call_target="tpu_custom_call" | custom-call | tf_op jit(solution)/shard_map/more/pallas_call | solution.py:105
  11.2 0.3 collective-permute-start.7
  11.5 0.0 collective-permute-done.near_ref.refs_14_
  11.5 4.2 %collective-permute-start.8 = (bf16[256,256]{1,0:T(8,128)(2,1)S(1)}, bf16[256,256]{1,0:T(8,128)(2,1)S(1)}, u32[]{:S(2)}, u32[]{:S(2)}) collective-permute-start(bf16[256,256]{1,0:T(8,128)(2,1)S(1)} %get-tuple-element.45), channel_id=1, source_target_pairs={{0,28},{4,24},{8,20},{12,16},{16,12},{20,8},{24,4},{28,0},{1,29},{... | collective-permute-start | bytes 393224 | tf_op jit(solution)/shard_map/ppermute | solution.py:277
  15.7 4.2 %local.1 = (f32[2048,256]{1,0:T(8,128)S(1)}, bf16[144,128,128]{2,1,0:T(8,128)(2,1)S(1)}, bf16[2048,1024]{1,0:T(8,128)(2,1)S(1)}, s32[256]{0:T(256)S(1)}, bf16[25...) custom-call(bf16[128,128,128]{2,1,0:T(8,128)(2,1)S(1)} %get-tuple-element.26.tiles_ref, ...), custom_call_target="tpu_custom_call" | custom-call | tf_op jit(solution)/shard_map/local/pallas_call | solution.py:168
  20.0 0.0 collective-permute-done.1.refs_8_
  20.0 0.1 collective-permute-start.4
  20.1 0.0 collective-permute-done.2.refs_10_
  20.1 0.0 collective-permute-done.3.refs_15_
  20.1 0.0 copy-start
  20.1 0.5 %collective-permute-start.5 = (bf16[512,256]{1,0:T(8,128)(2,1)S(1)}, bf16[512,256]{1,0:T(8,128)(2,1)S(1)}, u32[]{:S(2)}, u32[]{:S(2)}) collective-permute-start(bf16[512,256]{1,0:T(8,128)(2,1)S(1)} %collective-permute-done.1.refs_8_), channel_id=1, source_target_pairs={{0,4},{4,0},{8,12},{12,8},{16,20},{20,16},{24,28},{28,24},{1,5},{5... | collective-permute-start | bytes 786440 | tf_op jit(solution)/shard_map/ppermute | solution.py:277
  20.6 0.1 collective-permute-start.6
  20.7 0.4 %collective-permute-start.9 = (bf16[256,256]{1,0:T(8,128)(2,1)S(1)}, bf16[256,256]{1,0:T(8,128)(2,1)S(1)}, u32[]{:S(2)}, u32[]{:S(2)}) collective-permute-start(bf16[256,256]{1,0:T(8,128)(2,1)S(1)} %collective-permute-done.3.refs_15_), channel_id=1, source_target_pairs={{0,4},{4,0},{8,12},{12,8},{16,20},{20,16},{24,28},{28,24},{1,5},{5... | collective-permute-start | bytes 393224 | tf_op jit(solution)/shard_map/ppermute | solution.py:277
  21.1 0.0 collective-permute-done.8.refs_1_
  21.2 0.2 collective-permute-done.4.refs_7_
  21.4 1.0 %collective-permute-done.9.refs_16_ = bf16[256,256]{1,0:T(8,128)(2,1)S(1)} collective-permute-done((bf16[256,256]{1,0:T(8,128)(2,1)S(1)}, bf16[256,256]{1,0:T(8,128)(2,1)S(1)}, u32[]{:S(2)}, u32[]{:S(2)}) %collective-permute-start.9) | collective-permute-done | bytes 131104 | tf_op jit(solution)/shard_map/ppermute | solution.py:277
  22.3 0.0 collective-permute-done.5.refs_9_
  22.4 0.0 collective-permute-done.6.refs_11_
  22.4 5.7 %last.1 = bf16[2048,256]{1,0:T(8,128)(2,1)} custom-call(s32[256]{0:T(256)S(1)} %get-tuple-element.31.refs_0_, s32[8,16]{1,0:T(8,128)} %bitcast.3, bf16[144,128,128]{2,1,0:T(8,128)(2,1)S(1)} %get-tuple-element.32.refs_2_, bf16[2048,1024]{1,0:T(8,128)(2,1)S(1)} %get-tuple-element.33.refs_3_, f32[2048,256]{1,0:T(8,128)S(1)} %get-tuple-element.39.refs_4_, ...), custom_call_target="tpu_custom_call" | custom-call | tf_op jit(solution)/shard_map/last/pallas_call | solution.py:258
  (3 shorter events, 0.0 us)
Async XLA Ops:
  3.5 16.5 %collective-permute-start.1 = (bf16[512,256]{1,0:T(8,128)(2,1)S(1)}, bf16[512,256]{1,0:T(8,128)(2,1)S(1)}, u32[]{:S(2)}, u32[]{:S(2)}) collective-permute-start(bf16[512,256]{1,0:T(8,128)(2,1)S(1)} %get-tuple-element.35), channel_id=1, source_target_pairs={{0,8},{4,12},{8,0},{12,4},{16,24},{20,28},{24,16},{28,20},{1,9},{5... | collective-permute-start | bytes 786440 | tf_op jit(solution)/shard_map/ppermute | solution.py:277
  5.6 14.4 %collective-permute-start.2 = (bf16[512,256]{1,0:T(8,128)(2,1)S(1)}, bf16[512,256]{1,0:T(8,128)(2,1)S(1)}, u32[]{:S(2)}, u32[]{:S(2)}) collective-permute-start(bf16[512,256]{1,0:T(8,128)(2,1)S(1)} %get-tuple-element.36), channel_id=1, source_target_pairs={{0,16},{4,20},{8,24},{12,28},{16,0},{20,4},{24,8},{28,12},{1,17},{... | collective-permute-start | bytes 786440 | tf_op jit(solution)/shard_map/ppermute | solution.py:277
  6.9 4.6 %collective-permute-start = (bf16[256,256]{1,0:T(8,128)(2,1)S(1)}, bf16[256,256]{1,0:T(8,128)(2,1)S(1)}, u32[]{:S(2)}, u32[]{:S(2)}) collective-permute-start(bf16[256,256]{1,0:T(8,128)(2,1)S(1)} %get-tuple-element.30.refs_13_), channel_id=1, source_target_pairs={{0,1},{1,0},{2,3},{3,2},{4,5},{5,4},{6,7},{7,6},{8,9},{9,8},{10,11... | collective-permute-start | bytes 393224 | tf_op jit(solution)/shard_map/ppermute | solution.py:277
  8.1 11.9 %collective-permute-start.3 = (bf16[256,256]{1,0:T(8,128)(2,1)S(1)}, bf16[256,256]{1,0:T(8,128)(2,1)S(1)}, u32[]{:S(2)}, u32[]{:S(2)}) collective-permute-start(bf16[256,256]{1,0:T(8,128)(2,1)S(1)} %get-tuple-element.30.refs_13_), channel_id=1, source_target_pairs={{0,2},{1,3},{2,0},{3,1},{4,7},{5,6},{6,5},{7,4},{8,10},{9,11},{10,... | collective-permute-start | bytes 393224 | tf_op jit(solution)/shard_map/ppermute | solution.py:283
  11.2 9.5 %collective-permute-start.7 = (bf16[256,256]{1,0:T(8,128)(2,1)S(1)}, bf16[256,256]{1,0:T(8,128)(2,1)S(1)}, u32[]{:S(2)}, u32[]{:S(2)}) collective-permute-start(bf16[256,256]{1,0:T(8,128)(2,1)S(1)} %get-tuple-element.44), channel_id=1, source_target_pairs={{0,24},{4,28},{8,16},{12,20},{16,8},{20,12},{24,0},{28,4},{1,25},{... | collective-permute-start | bytes 393224 | tf_op jit(solution)/shard_map/ppermute | solution.py:277
  11.5 9.7 %collective-permute-start.8 = (bf16[256,256]{1,0:T(8,128)(2,1)S(1)}, bf16[256,256]{1,0:T(8,128)(2,1)S(1)}, u32[]{:S(2)}, u32[]{:S(2)}) collective-permute-start(bf16[256,256]{1,0:T(8,128)(2,1)S(1)} %get-tuple-element.45), channel_id=1, source_target_pairs={{0,28},{4,24},{8,20},{12,16},{16,12},{20,8},{24,4},{28,0},{1,29},{... | collective-permute-start | bytes 393224 | tf_op jit(solution)/shard_map/ppermute | solution.py:277
  20.0 1.4 %collective-permute-start.4 = (bf16[256,256]{1,0:T(8,128)(2,1)S(1)}, bf16[256,256]{1,0:T(8,128)(2,1)S(1)}, u32[]{:S(2)}, u32[]{:S(2)}) collective-permute-start(bf16[256,256]{1,0:T(8,128)(2,1)S(1)} %get-tuple-element.41), channel_id=1, source_target_pairs={{0,4},{4,0},{8,12},{12,8},{16,20},{20,16},{24,28},{28,24},{1,5},{5... | collective-permute-start | bytes 393224 | tf_op jit(solution)/shard_map/ppermute | solution.py:277
  20.1 2.3 %copy-start = (bf16[256,256]{1,0:T(8,128)(2,1)S(1)}, bf16[256,256]{1,0:T(8,128)(2,1)}, u32[]{:S(2)}) copy-start(bf16[256,256]{1,0:T(8,128)(2,1)} %refs_5_.3) | copy-start | bytes 393220
  20.1 2.3 %collective-permute-start.5 = (bf16[512,256]{1,0:T(8,128)(2,1)S(1)}, bf16[512,256]{1,0:T(8,128)(2,1)S(1)}, u32[]{:S(2)}, u32[]{:S(2)}) collective-permute-start(bf16[512,256]{1,0:T(8,128)(2,1)S(1)} %collective-permute-done.1.refs_8_), channel_id=1, source_target_pairs={{0,4},{4,0},{8,12},{12,8},{16,20},{20,16},{24,28},{28,24},{1,5},{5... | collective-permute-start | bytes 786440 | tf_op jit(solution)/shard_map/ppermute | solution.py:277
  20.6 1.7 %collective-permute-start.6 = (bf16[512,256]{1,0:T(8,128)(2,1)S(1)}, bf16[512,256]{1,0:T(8,128)(2,1)S(1)}, u32[]{:S(2)}, u32[]{:S(2)}) collective-permute-start(bf16[512,256]{1,0:T(8,128)(2,1)S(1)} %collective-permute-done.2.refs_10_), channel_id=1, source_target_pairs={{0,4},{4,0},{8,12},{12,8},{16,20},{20,16},{24,28},{28,24},{1,5},{5... | collective-permute-start | bytes 786440 | tf_op jit(solution)/shard_map/ppermute | solution.py:277
  20.7 1.6 %collective-permute-start.9 = (bf16[256,256]{1,0:T(8,128)(2,1)S(1)}, bf16[256,256]{1,0:T(8,128)(2,1)S(1)}, u32[]{:S(2)}, u32[]{:S(2)}) collective-permute-start(bf16[256,256]{1,0:T(8,128)(2,1)S(1)} %collective-permute-done.3.refs_15_), channel_id=1, source_target_pairs={{0,4},{4,0},{8,12},{12,8},{16,20},{20,16},{24,28},{28,24},{1,5},{5... | collective-permute-start | bytes 393224 | tf_op jit(solution)/shard_map/ppermute | solution.py:277

commit v4 on v3

v4 whole, which is shorter than its diff:
```python
import functools

import jax
import jax.numpy as jnp
from jax import lax
from jax.experimental import pallas as pl
from jax.experimental.pallas import tpu as pltpu
from jax.sharding import PartitionSpec as P

BF = jnp.bfloat16
F32 = jnp.float32
I32 = jnp.int32
VMEM = pl.BlockSpec(memory_space=pltpu.VMEM)
SMEM = pl.BlockSpec(memory_space=pltpu.SMEM)
HBM = pl.BlockSpec(memory_space=pltpu.HBM)
ANY = pl.BlockSpec(memory_space=pl.ANY)
MIB = 1 << 20
FREE = pl.CostEstimate(flops=0, bytes_accessed=0, transcendentals=0)
VMEM = pl.BlockSpec(memory_space=pltpu.VMEM)
SMEM = pl.BlockSpec(memory_space=pltpu.SMEM)
HBM = pl.BlockSpec(memory_space=pltpu.HBM)
ANY = pl.BlockSpec(memory_space=pl.ANY)
MIB = 1 << 20
FREE = pl.CostEstimate(flops=0, bytes_accessed=0, transcendentals=0)
LONG = pl.CostEstimate(flops=1 << 35, bytes_accessed=0, transcendentals=0)


def params(mib):
    return pltpu.CompilerParams(vmem_limit_bytes=mib * MIB)


def hbm(*arrays):
    return [pltpu.with_memory_space_constraint(x, pltpu.HBM) for x in arrays]


def dot(a, b):
    return jnp.dot(a, b, preferred_element_type=F32)


def picks(send_ref, count_ref, rows, peer, scalar):
    slots = send_ref.shape[1]
    index = send_ref[pl.ds(peer, 1), :]
    slot = lax.broadcasted_iota(I32, (1, slots), 1)
    if scalar:
        count = count_ref[0, peer]
    else:
        peers = lax.broadcasted_iota(I32, count_ref.shape, 1)
        count = jnp.sum(jnp.where(peers == peer, count_ref[...], 0), axis=1, keepdims=True)
    index = jnp.where(slot < count, index, -1)
    lane = lax.broadcasted_iota(I32, (128, 128), 1)
    blocks = []
    for part in range(slots // 128):
        column = jnp.broadcast_to(index[:, part * 128 : (part + 1) * 128], (128, 128)).T
        line = [jnp.where(column == lane + c * 128, 1.0, 0.0).astype(BF) for c in range(rows // 128)]
        blocks.append(jnp.concatenate(line, axis=1))
    return jnp.concatenate(blocks, axis=0)


def gather_groups(offsets, send_ref, count_ref, feat_ref, packed, scalar=False):
    me = lax.axis_index("row")
    rows = feat_ref.shape[0]
    for out_ref, group in zip(packed, offsets):
        hot = [picks(send_ref, count_ref, rows, me ^ offset, scalar) for offset in group]
        out_ref[...] = dot(jnp.concatenate(hot, axis=0), feat_ref[...]).astype(BF)


def start_all(sources, targets, sems):
    copies = [pltpu.make_async_copy(x, y, sems.at[n]) for n, (x, y) in enumerate(zip(sources, targets))]
    for copy in copies:
        copy.start()
    return copies


def wait_all(copies):
    for copy in copies:
        copy.wait()


def pack_kernel(offsets, feat_hbm, send_hbm, count_hbm, hub_hbm, live_hbm, tiles_hbm, *refs):
    targets, (tiles_ref, *packed, scalars, sems) = refs[:5], refs[5:]
    feat_ref, send_ref = targets[:2]
    sources = [feat_hbm, send_hbm, count_hbm, hub_hbm, live_hbm, count_hbm]
    wait_all(start_all(sources, [*targets, scalars], sems))
    half = pl.ds(0, tiles_ref.shape[0] // 2)
    copy = pltpu.make_async_copy(tiles_hbm.at[half], tiles_ref.at[half], sems.at[6])
    copy.start()
    gather_groups(offsets, send_ref, scalars, feat_ref, packed, scalar=True)
    copy.wait()


def pack(offsets, features, send_rows, send_count, hub_feats, hub_live, tiles):
    slots, width = send_rows.shape[1], features.shape[1]
    arrays = (features, send_rows, send_count, hub_feats, hub_live, tiles)
    return pl.pallas_call(
        functools.partial(pack_kernel, offsets),
        out_shape=[jax.ShapeDtypeStruct(x.shape, x.dtype) for x in arrays]
        + [jax.ShapeDtypeStruct((len(group) * slots, width), BF) for group in offsets],
        in_specs=[HBM] * 6,
        out_specs=[VMEM] * (6 + len(offsets)),
        scratch_shapes=[pltpu.SMEM(send_count.shape, I32), pltpu.SemaphoreType.DMA((7,))],
        compiler_params=params(16),
        cost_estimate=FREE,
        name="pack",
    )(*hbm(*arrays))


def more_kernel(offsets, feat_ref, send_ref, count_ref, *packed):
    gather_groups(offsets, send_ref, count_ref, feat_ref, packed)


def pack_more(offsets, features, send_rows, send_count):
    slots, width = send_rows.shape[1], features.shape[1]
    return pl.pallas_call(
        functools.partial(more_kernel, offsets),
        out_shape=[jax.ShapeDtypeStruct((len(group) * slots, width), BF) for group in offsets],
        in_specs=[VMEM] * 3,
        out_specs=[VMEM] * len(offsets),
        compiler_params=params(16),
        cost_estimate=FREE,
        name="more",
    )(features, send_rows, send_count)


def fill_map(ids_ref, live_ref, map_ref):
    for cell in range(map_ref.shape[0]):
        map_ref[cell] = -1
    for t in range(ids_ref.shape[0]):
        map_ref[ids_ref[t]] = jnp.where(live_ref[t] > 0, t, -1)


def cell_tile(tiles_ref, map_ref, cell):
    slot = map_ref[cell]
    tile = tiles_ref[jnp.maximum(slot, 0)]
    return jnp.where(slot >= 0, tile, jnp.zeros_like(tile))


def edge_line(tiles_ref, map_ref, row, cols, sources, per):
    return [cell_tile(tiles_ref, map_ref, row * cols + source * per + j) for source in sources for j in range(per)]


def hub_line(adj_ref, live_ref, row, size, owners, per):
    line = []
    for owner in owners:
        for j in range(per):
            b = owner * per + j
            cell = adj_ref[pl.ds(pl.multiple_of(row * size, size), size), pl.ds(pl.multiple_of(b * size, size), size)]
            line.append(jnp.where(live_ref[b, row] > 0, cell, jnp.zeros_like(cell)))
    return line


def local_kernel(block, feat_ref, send_ref, count_ref, hub_ref, live_vmem, begun_ref, *refs):
    del begun_ref
    sources, (out_ref, tiles_ref, edge_ref, adj_ref, map_hbm, core_ref, *refs) = list(refs[:7]), refs[7:]
    *tables, local_map, edge_map, live_ref, own_ref, rhs_ref, sems = refs
    half = pl.ds(tiles_ref.shape[0] // 2, tiles_ref.shape[0] // 2)
    sources[4] = sources[4].at[half]
    copies = start_all([*sources, live_vmem], [*tables, tiles_ref.at[half], edge_ref, adj_ref, live_ref], sems)
    gather_groups([(1,), (0,)], send_ref, count_ref, feat_ref, [core_ref, own_ref])
    wait_all(copies[:4])
    fill_map(tables[0], tables[1], local_map)
    fill_map(tables[2], tables[3], edge_map)
    copies.append(pltpu.make_async_copy(edge_map, map_hbm, sems.at[8]))
    copies[8].start()
    copies[4].wait()
    size = tiles_ref.shape[1]
    rows = feat_ref.shape[0]
    cols, edge_cols = rows // size, edge_map.shape[0] // (rows // size)
    steps = rows // (block * size)

    def span(m):
        return pl.ds(pl.multiple_of(m * block * size, block * size), block * size)

    def local_body(m, _):
        blocks = []
        for i in range(block):
            row = m * block + i
            line = [cell_tile(tiles_ref, local_map, row * cols + j) for j in range(cols)]
            blocks.append(jnp.concatenate(line, axis=1))
        out_ref[span(m), :] = dot(jnp.concatenate(blocks, axis=0), feat_ref[...])
        return 0

    lax.fori_loop(0, steps, local_body, 0)
    wait_all(copies[5:])
    me, loop = lax.axis_index("row"), lax.axis_index("loop")
    shard, slots = hub_ref.shape[0], own_ref.shape[0]
    rhs_ref[:shard, :] = hub_ref[...]
    rhs_ref[shard:, :] = own_ref[...]

    def here_body(m, _):
        blocks = []
        for i in range(block):
            row = m * block + i
            line = hub_line(adj_ref, live_ref, row, size, [loop], shard // size)
            line += edge_line(edge_ref, edge_map, row, edge_cols, [me], slots // size)
            blocks.append(jnp.concatenate(line, axis=1))
        out_ref[span(m), :] += dot(jnp.concatenate(blocks, axis=0), rhs_ref[...])
        return 0

    lax.fori_loop(0, steps, here_body, 0)


def local_term(features, send_rows, send_count, hub, hub_live, begun, tables, tiles, edges, adj):
    rows, width = features.shape
    peers, slots = send_rows.shape
    size = tiles.shape[1]
    local_cells, edge_cells = (rows // size) ** 2, (rows // size) * (peers * slots // size)
    return pl.pallas_call(
        functools.partial(local_kernel, 8),
        out_shape=[
            jax.ShapeDtypeStruct(features.shape, F32),
            *[jax.ShapeDtypeStruct(x.shape, BF) for x in (tiles, edges, adj)],
            jax.ShapeDtypeStruct((edge_cells,), I32),
            jax.ShapeDtypeStruct((slots, width), BF),
        ],
        in_specs=[VMEM] * 6 + [HBM] * 7,
        out_specs=[VMEM] * 4 + [ANY, VMEM],
        scratch_shapes=[pltpu.SMEM(x.shape, I32) for x in tables]
        + [pltpu.SMEM((local_cells,), I32), pltpu.SMEM((edge_cells,), I32), pltpu.SMEM(hub_live.shape, I32)]
        + [pltpu.VMEM((slots, width), BF), pltpu.VMEM((hub.shape[0] + slots, width), BF)]
        + [pltpu.SemaphoreType.DMA((9,))],
        input_output_aliases={5: 1},
        compiler_params=params(16),
        cost_estimate=FREE,
        name="local",
    )(features, send_rows, send_count, hub, hub_live, begun, *hbm(*tables, tiles, edges, adj))


def sum_kernel(block, pieces, hubs, shard, counts, map_ref, live_vmem, edge_ref, adj_ref, acc_ref, *refs):
    array_refs, refs = refs[:counts], refs[counts:]
    last = len(refs) == 7
    if last:
        weight_ref, out_ref, edge_map, live_ref, rhs_ref, sems, stage_ref = refs
    else:
        out_ref, edge_map, live_ref, rhs_ref, sems = refs
    size = edge_ref.shape[1]
    rows = adj_ref.shape[0]
    steps = rows // (block * size)
    tables = [
        pltpu.make_async_copy(map_ref, edge_map, sems.at[steps]),
        pltpu.make_async_copy(live_vmem, live_ref, sems.at[steps + 1]),
    ]
    for copy in tables:
        copy.start()
    me, loop = lax.axis_index("row"), lax.axis_index("loop")
    core = lax.rem(me, 2)
    cols = edge_map.shape[0] // (rows // size)
    owners = [loop ^ jnp.where(core == 0, even, odd) for _, _, even, odd in hubs]
    sources = [me ^ offset for _, _, offset in pieces]
    at = 0
    for array, first, _, _ in hubs:
        rhs_ref[at : at + shard, :] = array_refs[array][first : first + shard, :]
        at += shard
    slots = (rhs_ref.shape[0] - at) // len(pieces)
    for array, first, _ in pieces:
        rhs_ref[at : at + slots, :] = array_refs[array][first : first + slots, :]
        at += slots
    wait_all(tables)

    def write(m):
        span = pl.ds(pl.multiple_of(m * block * size, block * size), block * size)
        return pltpu.make_async_copy(stage_ref.at[span], out_ref.at[span], sems.at[m])

    def body(m, _):
        blocks = []
        for i in range(block):
            row = m * block + i
            line = hub_line(adj_ref, live_ref, row, size, owners, shard // size)
            line += edge_line(edge_ref, edge_map, row, cols, sources, slots // size)
            blocks.append(jnp.concatenate(line, axis=1))
        span = pl.ds(pl.multiple_of(m * block * size, block * size), block * size)
        total = acc_ref[span, :] + dot(jnp.concatenate(blocks, axis=0), rhs_ref[...])
        if last:
            stage_ref[span, :] = jnp.maximum(dot(total.astype(BF), weight_ref[...]), 0.0).astype(BF)
            write(m).start()
        else:
            out_ref[span, :] = total
        return 0

    lax.fori_loop(0, steps, body, 0)
    if last:
        for m in range(steps):
            write(m).wait()


def sum_term(name, pieces, hubs, shard, slots, edge_map, hub_live, edges, adj, acc, arrays, weight=None):
    block = 8
    rows, width = acc.shape
    last = weight is not None
    deep = len(pieces) * slots + len(hubs) * shard
    return pl.pallas_call(
        functools.partial(sum_kernel, block, pieces, hubs, shard, len(arrays)),
        out_shape=jax.ShapeDtypeStruct(acc.shape, BF if last else F32),
        in_specs=[ANY] + [VMEM] * (4 + len(arrays) + last),
        out_specs=HBM if last else VMEM,
        scratch_shapes=[
            pltpu.SMEM(edge_map.shape, I32),
            pltpu.SMEM(hub_live.shape, I32),
            pltpu.VMEM((deep, width), BF),
            pltpu.SemaphoreType.DMA((rows // (block * edges.shape[1]) + 2,)),
        ]
        + [pltpu.VMEM(acc.shape, BF)] * last,
        compiler_params=params(16),
        cost_estimate=FREE,
        name=name,
    )(edge_map, hub_live, edges, adj, acc, *arrays, *([weight] if last else []))


def swap(x, axis, offset):
    return lax.ppermute(x, axis, [(i, i ^ offset) for i in range(lax.axis_size(axis))])


def swap_by_core(x, even, odd):
    peers, ring = lax.axis_size("row"), lax.axis_size("loop")
    pairs = [(r * ring + l, r * ring + (l ^ (odd if r % 2 else even))) for r in range(peers) for l in range(ring)]
    return lax.ppermute(x, ("row", "loop"), pairs)


def per_device(
    features,
    weight,
    local_tiles,
    local_ids,
    local_live,
    send_rows,
    send_count,
    edge_tiles,
    edge_ids,
    edge_live,
    hub_feats,
    hub_adj,
    hub_live,
):
    peers, ring = lax.axis_size("row"), lax.axis_size("loop")
    slots = send_rows.shape[2]
    size = local_tiles.shape[1]
    tile_rows = features.shape[0] // size
    chips = range(2, peers, 2)
    early = [c for c in chips if c & (c - 1) == 0]
    late = [c for c in chips if c not in early]
    feat, sends, counts, hub, live, tiles, *packed = pack(
        [(c, c ^ 1) for c in early], features, send_rows[0], send_count, hub_feats, hub_live.T, local_tiles
    )
    from_early = [swap(x, "row", c) for x, c in zip(packed, early)]
    packed = pack_more([(c, c ^ 1) for c in late], feat, sends, counts)
    from_late = [swap(x, "row", c) for x, c in zip(packed, late)]
    near = swap(hub, "loop", 1)
    far = [swap_by_core(hub, offset, offset + 1) for offset in range(2, ring, 2)]
    acc, _, edges, adj, edge_map, to_core = local_term(
        feat,
        sends,
        counts,
        hub,
        live,
        tiles,
        (local_ids, local_live, edge_ids, edge_live),
        local_tiles,
        edge_tiles,
        hub_adj,
    )
    from_core = swap(to_core, "row", 1)
    from_early = lax.optimization_barrier(tuple(from_early))
    acc, near, *ready = lax.optimization_barrier((acc, near, *from_early, *from_late, *far))
    arrived, far = ready[: len(chips)], ready[len(chips) :]
    shared = [swap(x, "row", 1) for x in arrived]
    far_shared = [swap(x, "row", 1) for x in far]
    common = (hub.shape[0], slots, edge_map, live, edges, adj)
    order = early + late
    pieces = [(n, 0, c) for n, c in enumerate(order)]
    acc = sum_term("middle", pieces, [(len(chips), 0, 1, 1)], *common, acc, [*arrived, near])
    arrays = [from_core, *shared, *far, *far_shared]
    pieces = [(0, 0, 1)] + [(1 + n, slots, c ^ 1) for n, c in enumerate(order)]
    at = len(pieces)
    hubs = [(at + n, 0, 2 * n + 2, 2 * n + 3) for n in range(len(far))]
    hubs += [(at + len(far) + n, 0, 2 * n + 3, 2 * n + 2) for n in range(len(far))]
    return sum_term("last", pieces, hubs, *common, acc, arrays, weight)


def solution(mesh):
    both = ("row", "loop")
    placed = (
        P(both, None),
        P(),
        P(both, None, None),
        P(both),
        P(both),
        P(both, None, None),
        P(both, None),
        P(both, None, None),
        P(both),
        P(both),
        P("loop", None),
        P(both, None),
        P(both, None),
    )
    return jax.shard_map(per_device, mesh=mesh, in_specs=placed, out_specs=P(both, None), check_vma=False)
```

time: 28.6 us -> 26.9 us (0.941); the launches traced: 28.1 us -> 26.7 us
  starting transfers between devices: 12.5 us -> 9.95 us
  Pallas kernels: 14.3 us -> 15.1 us
  waiting for transfers between devices: 1.2 us -> 1.5 us
    ppermute x9, starting transfers between devices: 10.3 us -> 7.75 us  [swap(): lax.ppermute(x, axis, [(i, i ^ offset) for i in range(lax.axis_size(axis))])]
    pallas_call x3, Pallas kernels: 9.96 us -> 11.3 us  [the longest x2 6.13 us: sum_term(): pl.pallas_call(functools.partial(sum_kernel, block, pieces, hubs, shard,...]
    pallas_call x1, Pallas kernels: 3.5 us -> 2.93 us  [pack(): pl.pallas_call(functools.partial(pack_kernel, offsets), out_shape=[jax.Sh...]
    ppermute x9, waiting for transfers between devices: 1.2 us -> 1.49 us  [swap(): lax.ppermute(x, axis, [(i, i ^ offset) for i in range(lax.axis_size(axis))])]
  transfers between devices with their start and end apart: 10 -> 10, of which waited for: 2 -> 1; matrix products, arithmetic and copies ran while one was open for 0% -> 0% of each run, Pallas kernels for 18% -> 31%
where the time goes in v4:
time: 26.9 us; the launch traced here: 26.7 us
  Pallas kernels  15.1 us (56%)
  starting transfers between devices  9.95 us (37%)
  waiting for transfers between devices  1.5 us (6%)
    ppermute x9, starting transfers between devices, swap(): lax.ppermute(x, axis, [(i, i ^ offset) for i in range(lax.axis_size(axis))])  7.75 us
    pallas_call x2, Pallas kernels, sum_term(): pl.pallas_call(functools.partial(sum_kernel, block, pieces, hubs, shard,...  6.13 us
    pallas_call x1, Pallas kernels, local_term(): pl.pallas_call(functools.partial(local_kernel, 8), out_shape=[jax.ShapeDt...  5.22 us
    pallas_call x1, Pallas kernels, pack(): pl.pallas_call(functools.partial(pack_kernel, offsets), out_shape=[jax.Sh...  2.93 us
    ppermute x1, starting transfers between devices, swap_by_core(): return lax.ppermute(x, ('row', 'loop'), pairs)  2.2 us
    ppermute x9, waiting for transfers between devices, swap(): lax.ppermute(x, axis, [(i, i ^ offset) for i in range(lax.axis_size(axis))])  1.49 us
    pallas_call x1, Pallas kernels, pack_more(): pl.pallas_call(functools.partial(more_kernel, offsets), out_shape=[jax.Sh...  0.85 us
  transfers between devices with their start and end apart: 10, of which 1 were waited for; matrix products, arithmetic and copies ran while one was open for 0% of the time, Pallas kernels for 31%

profile of v4, /device:TPU:1, one launch (start us, length us, event | category | flops | bytes accessed | tf_op | source)
XLA Modules:
  0.0 26.7 jit_solution(12839693082105159695)
XLA Ops:
  0.0 2.9 %pack.1 = (bf16[2048,256]{1,0:T(8,128)(2,1)S(1)}, s32[8,256]{1,0:T(8,128)S(1)}, s32[1,8]{1,0:T(1,128)S(1)}, bf16[256,256]{1,0:T(8,128)(2,1)S(1)}, s32[8,16]{1,0:...) custom-call(bf16[2048,256]{1,0:T(8,128)(2,1)} %feat_hbm.1, ...), custom_call_target="tpu_custom_call" | custom-call | tf_op jit(solution)/shard_map/pack/pallas_call | solution.py:94
  2.9 2.1 %collective-permute-start.1 = (bf16[512,256]{1,0:T(8,128)(2,1)S(1)}, bf16[512,256]{1,0:T(8,128)(2,1)S(1)}, u32[]{:S(2)}, u32[]{:S(2)}) collective-permute-start(bf16[512,256]{1,0:T(8,128)(2,1)S(1)} %get-tuple-element.36), channel_id=1, source_target_pairs={{0,8},{4,12},{8,0},{12,4},{16,24},{20,28},{24,16},{28,20},{1,9},{5... | collective-permute-start | bytes 786440 | tf_op jit(solution)/shard_map/ppermute | solution.py:309
  5.0 1.2 %collective-permute-start.2 = (bf16[512,256]{1,0:T(8,128)(2,1)S(1)}, bf16[512,256]{1,0:T(8,128)(2,1)S(1)}, u32[]{:S(2)}, u32[]{:S(2)}) collective-permute-start(bf16[512,256]{1,0:T(8,128)(2,1)S(1)} %get-tuple-element.37), channel_id=1, source_target_pairs={{0,16},{4,20},{8,24},{12,28},{16,0},{20,4},{24,8},{28,12},{1,17},{... | collective-permute-start | bytes 786440 | tf_op jit(solution)/shard_map/ppermute | solution.py:309
  6.3 0.8 %more.1 = bf16[512,256]{1,0:T(8,128)(2,1)S(1)} custom-call(bf16[2048,256]{1,0:T(8,128)(2,1)S(1)} %get-tuple-element.26.feat_ref, s32[8,256]{1,0:T(8,128)S(1)} %get-tuple-element.27.send_ref, s32[1,8]{1,0:T(1,128)S(1)} %get-tuple-element.28.count_ref), custom_call_target="tpu_custom_call" | custom-call | tf_op jit(solution)/shard_map/more/pallas_call | solution.py:113
  7.1 0.1 collective-permute-start.3
  7.2 1.5 %collective-permute-start = (bf16[256,256]{1,0:T(8,128)(2,1)S(1)}, bf16[256,256]{1,0:T(8,128)(2,1)S(1)}, u32[]{:S(2)}, u32[]{:S(2)}) collective-permute-start(bf16[256,256]{1,0:T(8,128)(2,1)S(1)} %get-tuple-element.29.hub_ref), channel_id=1, source_target_pairs={{0,1},{1,0},{2,3},{3,2},{4,5},{5,4},{6,7},{7,6},{8,9},{9,8},{10,11... | collective-permute-start | bytes 393224 | tf_op jit(solution)/shard_map/ppermute | solution.py:309
  8.7 2.2 %collective-permute-start.4 = (bf16[256,256]{1,0:T(8,128)(2,1)S(1)}, bf16[256,256]{1,0:T(8,128)(2,1)S(1)}, u32[]{:S(2)}, u32[]{:S(2)}) collective-permute-start(bf16[256,256]{1,0:T(8,128)(2,1)S(1)} %get-tuple-element.29.hub_ref), channel_id=1, source_target_pairs={{0,2},{1,3},{2,0},{3,1},{4,7},{5,6},{6,5},{7,4},{8,10},{9,11},{10,... | collective-permute-start | bytes 393224 | tf_op jit(solution)/shard_map/ppermute | solution.py:315
  10.9 5.2 %local.1 = (f32[2048,256]{1,0:T(8,128)S(1)}, bf16[128,128,128]{2,1,0:T(8,128)(2,1)S(1)}, bf16[144,128,128]{2,1,0:T(8,128)(2,1)S(1)}, bf16[2048,1024]{1,0:T(8,128...) custom-call(bf16[2048,256]{1,0:T(8,128)(2,1)S(1)} %get-tuple-element.26.feat_ref, ...), custom_call_target="tpu_custom_call", output_to_operand_aliasing={{1}: (5, {})} | custom-call | tf_op jit(solution)/shard_map/local/pallas_call | solution.py:207
  16.1 0.0 collective-permute-done.1.refs_0_
  16.1 0.0 collective-permute-done.2.refs_1_
  16.1 0.0 collective-permute-done.refs_3_
  16.1 0.0 collective-permute-done.4.refs_4_
  16.2 1.5 %collective-permute-done.3.refs_2_ = bf16[512,256]{1,0:T(8,128)(2,1)S(1)} collective-permute-done((bf16[512,256]{1,0:T(8,128)(2,1)S(1)}, bf16[512,256]{1,0:T(8,128)(2,1)S(1)}, u32[]{:S(2)}, u32[]{:S(2)}) %collective-permute-start.3) | collective-permute-done | bytes 262176 | tf_op jit(solution)/shard_map/ppermute | solution.py:309
  17.6 1.8 %collective-permute-start.6 = (bf16[512,256]{1,0:T(8,128)(2,1)S(1)}, bf16[512,256]{1,0:T(8,128)(2,1)S(1)}, u32[]{:S(2)}, u32[]{:S(2)}) collective-permute-start(bf16[512,256]{1,0:T(8,128)(2,1)S(1)} %collective-permute-done.1.refs_0_), channel_id=1, source_target_pairs={{0,4},{4,0},{8,12},{12,8},{16,20},{20,16},{24,28},{28,24},{1,5},{5... | collective-permute-start | bytes 786440 | tf_op jit(solution)/shard_map/ppermute | solution.py:309
  19.5 0.1 collective-permute-start.7
  19.5 0.4 %collective-permute-start.8 = (bf16[512,256]{1,0:T(8,128)(2,1)S(1)}, bf16[512,256]{1,0:T(8,128)(2,1)S(1)}, u32[]{:S(2)}, u32[]{:S(2)}) collective-permute-start(bf16[512,256]{1,0:T(8,128)(2,1)S(1)} %collective-permute-done.3.refs_2_), channel_id=1, source_target_pairs={{0,4},{4,0},{8,12},{12,8},{16,20},{20,16},{24,28},{28,24},{1,5},{5... | collective-permute-start | bytes 786440 | tf_op jit(solution)/shard_map/ppermute | solution.py:309
  20.0 0.1 collective-permute-start.5
  20.1 0.4 %collective-permute-start.9 = (bf16[256,256]{1,0:T(8,128)(2,1)S(1)}, bf16[256,256]{1,0:T(8,128)(2,1)S(1)}, u32[]{:S(2)}, u32[]{:S(2)}) collective-permute-start(bf16[256,256]{1,0:T(8,128)(2,1)S(1)} %collective-permute-done.4.refs_4_), channel_id=1, source_target_pairs={{0,4},{4,0},{8,12},{12,8},{16,20},{20,16},{24,28},{28,24},{1,5},{5... | collective-permute-start | bytes 393224 | tf_op jit(solution)/shard_map/ppermute | solution.py:309
  20.5 2.1 %middle.1.acc_ref = f32[2048,256]{1,0:T(8,128)S(1)} custom-call(s32[256]{0:T(256)S(1)} %get-tuple-element.32.map_ref, s32[8,16]{1,0:T(8,128)S(1)} %get-tuple-element.30.live_vmem, bf16[144,128,128]{2,1,0:T(8,128)(2,1)S(1)} %get-tuple-element.33.edge_ref, bf16[2048,1024]{1,0:T(8,128)(2,1)S(1)} %get-tuple-element.34.adj_ref, ...), custom_call_target="tpu_custom_call" | custom-call | tf_op jit(solution)/shard_map/middle/pallas_call | solution.py:290
  22.6 0.0 collective-permute-done.5.refs_0_
  22.6 0.0 collective-permute-done.9.refs_5_
  22.7 0.0 collective-permute-done.7.refs_2_
  22.7 0.0 collective-permute-done.8.refs_3_
  22.7 4.0 %last.1 = bf16[2048,256]{1,0:T(8,128)(2,1)} custom-call(s32[256]{0:T(256)S(1)} %get-tuple-element.32.map_ref, s32[8,16]{1,0:T(8,128)S(1)} %get-tuple-element.30.live_vmem, bf16[144,128,128]{2,1,0:T(8,128)(2,1)S(1)} %get-tuple-element.33.edge_ref, bf16[2048,1024]{1,0:T(8,128)(2,1)S(1)} %get-tuple-element.34.adj_ref, f32[2048,256]{1,0:T(8,128)S(1)} %middle.1.acc_ref, ...), custom_call_target="tpu_custom_call" | custom-call | tf_op jit(solution)/shard_map/last/pallas_call | solution.py:290
  (3 shorter events, 0.0 us)
Async XLA Ops:
  2.9 13.2 %collective-permute-start.1 = (bf16[512,256]{1,0:T(8,128)(2,1)S(1)}, bf16[512,256]{1,0:T(8,128)(2,1)S(1)}, u32[]{:S(2)}, u32[]{:S(2)}) collective-permute-start(bf16[512,256]{1,0:T(8,128)(2,1)S(1)} %get-tuple-element.36), channel_id=1, source_target_pairs={{0,8},{4,12},{8,0},{12,4},{16,24},{20,28},{24,16},{28,20},{1,9},{5... | collective-permute-start | bytes 786440 | tf_op jit(solution)/shard_map/ppermute | solution.py:309
  5.0 11.1 %collective-permute-start.2 = (bf16[512,256]{1,0:T(8,128)(2,1)S(1)}, bf16[512,256]{1,0:T(8,128)(2,1)S(1)}, u32[]{:S(2)}, u32[]{:S(2)}) collective-permute-start(bf16[512,256]{1,0:T(8,128)(2,1)S(1)} %get-tuple-element.37), channel_id=1, source_target_pairs={{0,16},{4,20},{8,24},{12,28},{16,0},{20,4},{24,8},{28,12},{1,17},{... | collective-permute-start | bytes 786440 | tf_op jit(solution)/shard_map/ppermute | solution.py:309
  7.1 10.5 %collective-permute-start.3 = (bf16[512,256]{1,0:T(8,128)(2,1)S(1)}, bf16[512,256]{1,0:T(8,128)(2,1)S(1)}, u32[]{:S(2)}, u32[]{:S(2)}) collective-permute-start(bf16[512,256]{1,0:T(8,128)(2,1)S(1)} %more.1), channel_id=1, source_target_pairs={{0,24},{4,28},{8,16},{12,20},{16,8},{20,12},{24,0},{28,4},{1,25},{... | collective-permute-start | bytes 786440 | tf_op jit(solution)/shard_map/ppermute | solution.py:309
  7.2 8.9 %collective-permute-start = (bf16[256,256]{1,0:T(8,128)(2,1)S(1)}, bf16[256,256]{1,0:T(8,128)(2,1)S(1)}, u32[]{:S(2)}, u32[]{:S(2)}) collective-permute-start(bf16[256,256]{1,0:T(8,128)(2,1)S(1)} %get-tuple-element.29.hub_ref), channel_id=1, source_target_pairs={{0,1},{1,0},{2,3},{3,2},{4,5},{5,4},{6,7},{7,6},{8,9},{9,8},{10,11... | collective-permute-start | bytes 393224 | tf_op jit(solution)/shard_map/ppermute | solution.py:309
  8.7 7.5 %collective-permute-start.4 = (bf16[256,256]{1,0:T(8,128)(2,1)S(1)}, bf16[256,256]{1,0:T(8,128)(2,1)S(1)}, u32[]{:S(2)}, u32[]{:S(2)}) collective-permute-start(bf16[256,256]{1,0:T(8,128)(2,1)S(1)} %get-tuple-element.29.hub_ref), channel_id=1, source_target_pairs={{0,2},{1,3},{2,0},{3,1},{4,7},{5,6},{6,5},{7,4},{8,10},{9,11},{10,... | collective-permute-start | bytes 393224 | tf_op jit(solution)/shard_map/ppermute | solution.py:315
  17.6 5.0 %collective-permute-start.6 = (bf16[512,256]{1,0:T(8,128)(2,1)S(1)}, bf16[512,256]{1,0:T(8,128)(2,1)S(1)}, u32[]{:S(2)}, u32[]{:S(2)}) collective-permute-start(bf16[512,256]{1,0:T(8,128)(2,1)S(1)} %collective-permute-done.1.refs_0_), channel_id=1, source_target_pairs={{0,4},{4,0},{8,12},{12,8},{16,20},{20,16},{24,28},{28,24},{1,5},{5... | collective-permute-start | bytes 786440 | tf_op jit(solution)/shard_map/ppermute | solution.py:309
  19.5 3.2 %collective-permute-start.7 = (bf16[512,256]{1,0:T(8,128)(2,1)S(1)}, bf16[512,256]{1,0:T(8,128)(2,1)S(1)}, u32[]{:S(2)}, u32[]{:S(2)}) collective-permute-start(bf16[512,256]{1,0:T(8,128)(2,1)S(1)} %collective-permute-done.2.refs_1_), channel_id=1, source_target_pairs={{0,4},{4,0},{8,12},{12,8},{16,20},{20,16},{24,28},{28,24},{1,5},{5... | collective-permute-start | bytes 786440 | tf_op jit(solution)/shard_map/ppermute | solution.py:309
  19.5 3.1 %collective-permute-start.8 = (bf16[512,256]{1,0:T(8,128)(2,1)S(1)}, bf16[512,256]{1,0:T(8,128)(2,1)S(1)}, u32[]{:S(2)}, u32[]{:S(2)}) collective-permute-start(bf16[512,256]{1,0:T(8,128)(2,1)S(1)} %collective-permute-done.3.refs_2_), channel_id=1, source_target_pairs={{0,4},{4,0},{8,12},{12,8},{16,20},{20,16},{24,28},{28,24},{1,5},{5... | collective-permute-start | bytes 786440 | tf_op jit(solution)/shard_map/ppermute | solution.py:309
  20.0 2.6 %collective-permute-start.5 = (bf16[256,256]{1,0:T(8,128)(2,1)S(1)}, bf16[256,256]{1,0:T(8,128)(2,1)S(1)}, u32[]{:S(2)}, u32[]{:S(2)}) collective-permute-start(bf16[256,256]{1,0:T(8,128)(2,1)S(1)} %get-tuple-element.45), channel_id=1, source_target_pairs={{0,4},{4,0},{8,12},{12,8},{16,20},{20,16},{24,28},{28,24},{1,5},{5... | collective-permute-start | bytes 393224 | tf_op jit(solution)/shard_map/ppermute | solution.py:309
  20.1 2.6 %collective-permute-start.9 = (bf16[256,256]{1,0:T(8,128)(2,1)S(1)}, bf16[256,256]{1,0:T(8,128)(2,1)S(1)}, u32[]{:S(2)}, u32[]{:S(2)}) collective-permute-start(bf16[256,256]{1,0:T(8,128)(2,1)S(1)} %collective-permute-done.4.refs_4_), channel_id=1, source_target_pairs={{0,4},{4,0},{8,12},{12,8},{16,20},{20,16},{24,28},{28,24},{1,5},{5... | collective-permute-start | bytes 393224 | tf_op jit(solution)/shard_map/ppermute | solution.py:309
  20.5 2.2 %copy-start = (bf16[256,256]{1,0:T(8,128)(2,1)S(1)}, bf16[256,256]{1,0:T(8,128)(2,1)}, u32[]{:S(2)}) copy-start(bf16[256,256]{1,0:T(8,128)(2,1)} %refs_6_.3) | copy-start | bytes 393220

commit v5 on v4

v5 whole, which is shorter than its diff:
```python
import functools

import jax
import jax.numpy as jnp
from jax import lax
from jax.experimental import pallas as pl
from jax.experimental.pallas import tpu as pltpu
from jax.sharding import PartitionSpec as P

BF = jnp.bfloat16
F32 = jnp.float32
I32 = jnp.int32
LONG = pl.CostEstimate(flops=1 << 35, bytes_accessed=0, transcendentals=0)
VMEM = pl.BlockSpec(memory_space=pltpu.VMEM)
SMEM = pl.BlockSpec(memory_space=pltpu.SMEM)
HBM = pl.BlockSpec(memory_space=pltpu.HBM)
ANY = pl.BlockSpec(memory_space=pl.ANY)
MIB = 1 << 20
FREE = pl.CostEstimate(flops=0, bytes_accessed=0, transcendentals=0)
VMEM = pl.BlockSpec(memory_space=pltpu.VMEM)
SMEM = pl.BlockSpec(memory_space=pltpu.SMEM)
HBM = pl.BlockSpec(memory_space=pltpu.HBM)
ANY = pl.BlockSpec(memory_space=pl.ANY)
MIB = 1 << 20
FREE = pl.CostEstimate(flops=0, bytes_accessed=0, transcendentals=0)
LONG = pl.CostEstimate(flops=1 << 35, bytes_accessed=0, transcendentals=0)


def params(mib):
    return pltpu.CompilerParams(vmem_limit_bytes=mib * MIB)


def hbm(*arrays):
    return [pltpu.with_memory_space_constraint(x, pltpu.HBM) for x in arrays]


def dot(a, b):
    return jnp.dot(a, b, preferred_element_type=F32)


def picks(send_ref, count_ref, rows, peer, scalar):
    slots = send_ref.shape[1]
    index = send_ref[pl.ds(peer, 1), :]
    slot = lax.broadcasted_iota(I32, (1, slots), 1)
    if scalar:
        count = count_ref[0, peer]
    else:
        peers = lax.broadcasted_iota(I32, count_ref.shape, 1)
        count = jnp.sum(jnp.where(peers == peer, count_ref[...], 0), axis=1, keepdims=True)
    index = jnp.where(slot < count, index, -1)
    lane = lax.broadcasted_iota(I32, (128, 128), 1)
    blocks = []
    for part in range(slots // 128):
        column = jnp.broadcast_to(index[:, part * 128 : (part + 1) * 128], (128, 128)).T
        line = [jnp.where(column == lane + c * 128, 1.0, 0.0).astype(BF) for c in range(rows // 128)]
        blocks.append(jnp.concatenate(line, axis=1))
    return jnp.concatenate(blocks, axis=0)


def gather_groups(offsets, send_ref, count_ref, feat_ref, packed, scalar=False):
    me = lax.axis_index("row")
    rows = feat_ref.shape[0]
    for out_ref, group in zip(packed, offsets):
        hot = [picks(send_ref, count_ref, rows, me ^ offset, scalar) for offset in group]
        out_ref[...] = dot(jnp.concatenate(hot, axis=0), feat_ref[...]).astype(BF)


def start_all(sources, targets, sems):
    copies = [pltpu.make_async_copy(x, y, sems.at[n]) for n, (x, y) in enumerate(zip(sources, targets))]
    for copy in copies:
        copy.start()
    return copies


def wait_all(copies):
    for copy in copies:
        copy.wait()


def pack_kernel(offsets, feat_hbm, send_hbm, count_hbm, hub_hbm, live_hbm, *refs):
    targets, (*packed, scalars, sems) = refs[:5], refs[5:]
    feat_ref, send_ref = targets[:2]
    sources = [feat_hbm, send_hbm, count_hbm, hub_hbm, live_hbm, count_hbm]
    copies = start_all(sources, [*targets, scalars], sems)
    wait_all(copies[:2] + copies[5:])
    gather_groups(offsets, send_ref, scalars, feat_ref, packed, scalar=True)
    wait_all(copies[2:5])


def pack(offsets, features, send_rows, send_count, hub_feats, hub_live):
    slots, width = send_rows.shape[1], features.shape[1]
    arrays = (features, send_rows, send_count, hub_feats, hub_live)
    return pl.pallas_call(
        functools.partial(pack_kernel, offsets),
        out_shape=[jax.ShapeDtypeStruct(x.shape, x.dtype) for x in arrays]
        + [jax.ShapeDtypeStruct((len(group) * slots, width), BF) for group in offsets],
        in_specs=[HBM] * 5,
        out_specs=[VMEM] * (5 + len(offsets)),
        scratch_shapes=[pltpu.SMEM(send_count.shape, I32), pltpu.SemaphoreType.DMA((6,))],
        compiler_params=params(16),
        cost_estimate=FREE,
        name="pack",
    )(*hbm(*arrays))


def more_kernel(offsets, feat_ref, send_ref, count_ref, tiles_hbm, tiles_ref, *refs):
    *packed, sem = refs
    half = pl.ds(0, tiles_ref.shape[0] // 2)
    copy = pltpu.make_async_copy(tiles_hbm.at[half], tiles_ref.at[half], sem)
    copy.start()
    gather_groups(offsets, send_ref, count_ref, feat_ref, packed)
    copy.wait()


def pack_more(offsets, features, send_rows, send_count, tiles):
    slots, width = send_rows.shape[1], features.shape[1]
    return pl.pallas_call(
        functools.partial(more_kernel, offsets),
        out_shape=[jax.ShapeDtypeStruct(tiles.shape, BF)]
        + [jax.ShapeDtypeStruct((len(group) * slots, width), BF) for group in offsets],
        in_specs=[VMEM] * 3 + [HBM],
        out_specs=[VMEM] * (1 + len(offsets)),
        scratch_shapes=[pltpu.SemaphoreType.DMA],
        compiler_params=params(16),
        cost_estimate=FREE,
        name="more",
    )(features, send_rows, send_count, *hbm(tiles))


def clear_map(map_ref):
    for cell in range(map_ref.shape[0]):
        map_ref[cell] = -1


def fill_map(ids_ref, live_ref, map_ref, first, count):
    for n in range(count):
        t = first + n
        map_ref[ids_ref[t]] = jnp.where(live_ref[t] > 0, t, -1)


def cell_tile(tiles_ref, map_ref, cell):
    slot = map_ref[cell]
    tile = tiles_ref[jnp.maximum(slot, 0)]
    return jnp.where(slot >= 0, tile, jnp.zeros_like(tile))


def edge_line(tiles_ref, map_ref, row, cols, sources, per):
    return [cell_tile(tiles_ref, map_ref, row * cols + source * per + j) for source in sources for j in range(per)]


def local_kernel(block, feat_ref, send_ref, count_ref, begun_ref, *refs):
    del begun_ref
    sources, (out_ref, tiles_ref, edge_ref, adj_ref, map_hbm, core_ref, *refs) = list(refs[:7]), refs[7:]
    *tables, local_map, edge_map, own_ref, sems = refs
    half = pl.ds(tiles_ref.shape[0] // 2, tiles_ref.shape[0] // 2)
    sources[4] = sources[4].at[half]
    copies = start_all(sources, [*tables, tiles_ref.at[half], edge_ref, adj_ref], sems)
    gather_groups([(1,)], send_ref, count_ref, feat_ref, [core_ref])
    wait_all(copies[:4])
    clear_map(local_map)
    fill_map(tables[0], tables[1], local_map, 0, tables[0].shape[0])
    clear_map(edge_map)
    gather_groups([(0,)], send_ref, count_ref, feat_ref, [own_ref])
    copies[4].wait()
    size = tiles_ref.shape[1]
    rows = feat_ref.shape[0]
    cols, edge_cols = rows // size, edge_map.shape[0] // (rows // size)
    steps = rows // (block * size)
    share = tables[2].shape[0] // steps

    def span(m):
        return pl.ds(pl.multiple_of(m * block * size, block * size), block * size)

    def local_body(m, _):
        blocks = []
        for i in range(block):
            row = m * block + i
            line = [cell_tile(tiles_ref, local_map, row * cols + j) for j in range(cols)]
            blocks.append(jnp.concatenate(line, axis=1))
        out_ref[span(m), :] = dot(jnp.concatenate(blocks, axis=0), feat_ref[...])
        fill_map(tables[2], tables[3], edge_map, m * share, share)
        return 0

    lax.fori_loop(0, steps, local_body, 0)
    fill_map(tables[2], tables[3], edge_map, steps * share, tables[2].shape[0] - steps * share)
    copies.append(pltpu.make_async_copy(edge_map, map_hbm, sems.at[7]))
    copies[7].start()
    copies[5].wait()
    me = lax.axis_index("row")
    per = own_ref.shape[0] // size

    def own_body(m, _):
        lines = [edge_line(edge_ref, edge_map, m * block + i, edge_cols, [me], per) for i in range(block)]
        own_tiles = jnp.concatenate([jnp.concatenate(line, axis=1) for line in lines], axis=0)
        out_ref[span(m), :] += dot(own_tiles, own_ref[...])
        return 0

    lax.fori_loop(0, steps, own_body, 0)
    wait_all(copies[6:])


def local_term(features, send_rows, send_count, begun, tables, tiles, edges, adj):
    rows, width = features.shape
    peers, slots = send_rows.shape
    size = tiles.shape[1]
    local_cells, edge_cells = (rows // size) ** 2, (rows // size) * (peers * slots // size)
    return pl.pallas_call(
        functools.partial(local_kernel, 8),
        out_shape=[
            jax.ShapeDtypeStruct(features.shape, F32),
            *[jax.ShapeDtypeStruct(x.shape, BF) for x in (tiles, edges, adj)],
            jax.ShapeDtypeStruct((edge_cells,), I32),
            jax.ShapeDtypeStruct((slots, width), BF),
        ],
        in_specs=[VMEM] * 4 + [HBM] * 7,
        out_specs=[VMEM] * 4 + [ANY, VMEM],
        scratch_shapes=[pltpu.SMEM(x.shape, I32) for x in tables]
        + [pltpu.SMEM((local_cells,), I32), pltpu.SMEM((edge_cells,), I32)]
        + [pltpu.VMEM((slots, width), BF), pltpu.SemaphoreType.DMA((8,))],
        input_output_aliases={3: 1},
        compiler_params=params(16),
        cost_estimate=FREE,
        name="local",
    )(features, send_rows, send_count, begun, *hbm(*tables, tiles, edges, adj))


def masked_line(adj_ref, mask_ref, row, size, columns):
    span = pl.ds(pl.multiple_of(row * size, size), size)
    line = []
    for column in columns:
        mask = jnp.broadcast_to(mask_ref[pl.ds(row, 1), column], (size, column.size)).astype(BF)
        line.append(adj_ref[span, column] * mask)
    return jnp.concatenate(line, axis=1)


def hub_kernel(block, hubs, waited, live_ref, adj_ref, acc_ref, *refs):
    *array_refs, out_ref, mask_ref, rhs_ref = refs[waited:]
    core, loop = lax.rem(lax.axis_index("row"), 2), lax.axis_index("loop")
    shard = array_refs[0].shape[0]
    tiles, rows = live_ref.shape
    size = adj_ref.shape[0] // rows
    columns = []
    for n, (array_ref, (even, odd)) in enumerate(zip(array_refs, hubs)):
        owner = loop ^ jnp.where(core == 0, even, odd)
        columns.append(pl.ds(pl.multiple_of(owner * shard, shard), shard))
        rhs_ref[n * shard : (n + 1) * shard, :] = array_ref[...]
    lane = lax.broadcasted_iota(I32, (tiles, adj_ref.shape[1]), 1)
    first = lax.broadcasted_iota(I32, (tiles, adj_ref.shape[1]), 0) * size
    inside = (lane >= first) & (lane < first + size)
    live = live_ref[...]
    for row in range(rows):
        hit = jnp.where(inside & (live[:, row : row + 1] > 0), 1.0, 0.0)
        mask_ref[row : row + 1, :] = jnp.sum(hit, axis=0, keepdims=True)

    def body(m, _):
        blocks = [masked_line(adj_ref, mask_ref, m * block + i, size, columns) for i in range(block)]
        span = pl.ds(pl.multiple_of(m * block * size, block * size), block * size)
        out_ref[span, :] = acc_ref[span, :] + dot(jnp.concatenate(blocks, axis=0), rhs_ref[...])
        return 0

    lax.fori_loop(0, rows // block, body, 0)


def hub_term(hubs, waited, hub_live, adj, acc, arrays):
    shard, width = arrays[0].shape
    return pl.pallas_call(
        functools.partial(hub_kernel, 8, hubs, len(waited)),
        out_shape=[
            jax.ShapeDtypeStruct(acc.shape, F32),
            jax.ShapeDtypeStruct((hub_live.shape[1], adj.shape[1]), F32),
        ],
        in_specs=[VMEM] * (3 + len(waited) + len(arrays)),
        out_specs=[VMEM] * 2,
        scratch_shapes=[pltpu.VMEM((len(hubs) * shard, width), BF)],
        compiler_params=params(16),
        cost_estimate=LONG,
        name="hub",
    )(hub_live, adj, acc, *waited, *arrays)


def last_kernel(block, pieces, map_ref, edge_ref, adj_ref, mask_ref, acc_ref, weight_ref, near_ref, *refs):
    *array_refs, out_ref, edge_map, rhs_ref, total_ref, stage_ref, sems = refs
    size = edge_ref.shape[1]
    rows = acc_ref.shape[0]
    steps = rows // (block * size)
    table = pltpu.make_async_copy(map_ref, edge_map, sems.at[steps])
    table.start()
    me, loop = lax.axis_index("row"), lax.axis_index("loop")
    cols = edge_map.shape[0] // (rows // size)
    slots = rhs_ref.shape[0] // len(pieces)
    shard = near_ref.shape[0]
    for n, (array, first, _) in enumerate(pieces):
        rhs_ref[n * slots : (n + 1) * slots, :] = array_refs[array][first : first + slots, :]
    sources = [me ^ offset for _, _, offset in pieces]
    columns = [pl.ds(pl.multiple_of((loop ^ 1) * shard, shard), shard)]

    def span(m):
        return pl.ds(pl.multiple_of(m * block * size, block * size), block * size)

    def write(m):
        return pltpu.make_async_copy(stage_ref.at[span(m)], out_ref.at[span(m)], sems.at[m])

    def near_body(m, _):
        blocks = [masked_line(adj_ref, mask_ref, m * block + i, size, columns) for i in range(block)]
        total_ref[span(m), :] = acc_ref[span(m), :] + dot(jnp.concatenate(blocks, axis=0), near_ref[...])
        return 0

    lax.fori_loop(0, steps, near_body, 0)
    table.wait()

    def body(m, _):
        lines = [
            edge_line(edge_ref, edge_map, m * block + i, cols, sources, slots // size) for i in range(block)
        ]
        tiles = jnp.concatenate([jnp.concatenate(line, axis=1) for line in lines], axis=0)
        total = total_ref[span(m), :] + dot(tiles, rhs_ref[...])
        stage_ref[span(m), :] = jnp.maximum(dot(total.astype(BF), weight_ref[...]), 0.0).astype(BF)
        write(m).start()
        return 0

    lax.fori_loop(0, steps, body, 0)
    for m in range(steps):
        write(m).wait()


def last_term(pieces, slots, edge_map, edges, adj, mask, acc, weight, near, arrays):
    block = 8
    rows, width = acc.shape
    return pl.pallas_call(
        functools.partial(last_kernel, block, pieces),
        out_shape=jax.ShapeDtypeStruct(acc.shape, BF),
        in_specs=[ANY] + [VMEM] * (6 + len(arrays)),
        out_specs=HBM,
        scratch_shapes=[
            pltpu.SMEM(edge_map.shape, I32),
            pltpu.VMEM((len(pieces) * slots, width), BF),
            pltpu.VMEM(acc.shape, F32),
            pltpu.VMEM(acc.shape, BF),
            pltpu.SemaphoreType.DMA((rows // (block * edges.shape[1]) + 1,)),
        ],
        compiler_params=params(16),
        cost_estimate=FREE,
        name="last",
    )(edge_map, edges, adj, mask, acc, weight, near, *arrays)


def swap(x, axis, offset):
    return lax.ppermute(x, axis, [(i, i ^ offset) for i in range(lax.axis_size(axis))])


def swap_by_core(x, even, odd):
    peers, ring = lax.axis_size("row"), lax.axis_size("loop")
    pairs = [(r * ring + l, r * ring + (l ^ (odd if r % 2 else even))) for r in range(peers) for l in range(ring)]
    return lax.ppermute(x, ("row", "loop"), pairs)


def per_device(
    features,
    weight,
    local_tiles,
    local_ids,
    local_live,
    send_rows,
    send_count,
    edge_tiles,
    edge_ids,
    edge_live,
    hub_feats,
    hub_adj,
    hub_live,
):
    peers, ring = lax.axis_size("row"), lax.axis_size("loop")
    slots = send_rows.shape[2]
    size = local_tiles.shape[1]
    tile_rows = features.shape[0] // size
    chips = range(2, peers, 2)
    near_chips = [c for c in chips if c & (c - 1) == 0]
    far_chips = [c for c in chips if c not in near_chips]
    feat, sends, counts, hub, live, *packed = pack(
        [(c, c ^ 1) for c in far_chips], features, send_rows[0], send_count, hub_feats, hub_live.T
    )
    from_far = [swap(x, "row", c) for x, c in zip(packed, far_chips)]
    tiles, *packed = pack_more([(c, c ^ 1) for c in near_chips], feat, sends, counts, local_tiles)
    from_near = [swap(x, "row", c) for x, c in zip(packed, near_chips)]
    near = swap(hub, "loop", 1)
    far = [swap_by_core(hub, offset, offset + 1) for offset in range(2, ring, 2)]
    acc, _, edges, adj, edge_map, to_core = local_term(
        feat,
        sends,
        counts,
        tiles,
        (local_ids, local_live, edge_ids, edge_live),
        local_tiles,
        edge_tiles,
        hub_adj,
    )
    from_core = swap(to_core, "row", 1)
    acc, near, *far = lax.optimization_barrier((acc, near, *far))
    from_far = lax.optimization_barrier(tuple(from_far))
    acc, *arrived = lax.optimization_barrier((acc, *from_far, *from_near))
    shared = [swap(x, "row", 1) for x in arrived]
    far_shared = [swap(x, "row", 1) for x in far]
    hubs, arrays = [(0, 0)], [hub]
    for n, (x, y) in enumerate(zip(far, far_shared)):
        hubs += [(2 * n + 2, 2 * n + 3), (2 * n + 3, 2 * n + 2)]
        arrays += [x, y]
    acc, mask = hub_term(hubs, [from_core], live, adj, acc, arrays)
    pieces = [(0, 0, 1)]
    for n, c in enumerate(far_chips + near_chips):
        pieces += [(1 + n, 0, c), (1 + len(chips) + n, slots, c ^ 1)]
    return last_term(pieces, slots, edge_map, edges, adj, mask, acc, weight, near, [from_core, *arrived, *shared])


def solution(mesh):
    both = ("row", "loop")
    placed = (
        P(both, None),
        P(),
        P(both, None, None),
        P(both),
        P(both),
        P(both, None, None),
        P(both, None),
        P(both, None, None),
        P(both),
        P(both),
        P("loop", None),
        P(both, None),
        P(both, None),
    )
    return jax.shard_map(per_device, mesh=mesh, in_specs=placed, out_specs=P(both, None), check_vma=False)
```

time: 26.9 us -> 25.5 us (0.948)
  waiting for transfers between devices: 1.5 us -> 0.27 us
  Pallas kernels: 15.1 us -> 14.3 us
  starting transfers between devices: 9.95 us -> 10.4 us
    ppermute x9, waiting for transfers between devices: 1.49 us -> 0.27 us  [swap(): lax.ppermute(x, axis, [(i, i ^ offset) for i in range(lax.axis_size(axis))])]
    pallas_call x1, Pallas kernels: 2.93 us -> 2.06 us  [pack(): pl.pallas_call(functools.partial(pack_kernel, offsets), out_shape=[jax.Sh...]
    pallas_call x1, Pallas kernels: 0.85 us -> 1.61 us  [pack_more(): pl.pallas_call(functools.partial(more_kernel, offsets), out_shape=[jax.Sh...]
    ppermute x9, starting transfers between devices: 7.75 us -> 8.25 us  [swap(): lax.ppermute(x, axis, [(i, i ^ offset) for i in range(lax.axis_size(axis))])]
    pallas_call x2, Pallas kernels: 6.13 us -> 5.72 us  [the longest x1 4.25 us: last_term(): pl.pallas_call(functools.partial(last_kernel, block, pieces), out_shape=j...]
    pallas_call x1, Pallas kernels: 5.22 us -> 4.9 us  [local_term(): pl.pallas_call(functools.partial(local_kernel, 8), out_shape=[jax.ShapeDt...]
  transfers between devices with their start and end apart: 10 -> 10, of which waited for: 1 -> 1; matrix products, arithmetic and copies ran while one was open for 0% -> 0% of each run, Pallas kernels for 31% -> 32%
where the time goes in v5:
time: 25.5 us; the launch traced here: 25.1 us
  Pallas kernels  14.3 us (56%)
  starting transfers between devices  10.4 us (41%)
  waiting for transfers between devices  0.27 us (1%)
    ppermute x9, starting transfers between devices, swap(): lax.ppermute(x, axis, [(i, i ^ offset) for i in range(lax.axis_size(axis))])  8.25 us
    pallas_call x1, Pallas kernels, local_term(): pl.pallas_call(functools.partial(local_kernel, 8), out_shape=[jax.ShapeDt...  4.9 us
    pallas_call x1, Pallas kernels, last_term(): pl.pallas_call(functools.partial(last_kernel, block, pieces), out_shape=j...  4.25 us
    ppermute x1, starting transfers between devices, swap_by_core(): return lax.ppermute(x, ('row', 'loop'), pairs)  2.2 us
    pallas_call x1, Pallas kernels, pack(): pl.pallas_call(functools.partial(pack_kernel, offsets), out_shape=[jax.Sh...  2.06 us
    pallas_call x1, Pallas kernels, pack_more(): pl.pallas_call(functools.partial(more_kernel, offsets), out_shape=[jax.Sh...  1.61 us
    pallas_call x1, Pallas kernels, hub_term(): pl.pallas_call(functools.partial(hub_kernel, 8, hubs, len(waited)), out_s...  1.47 us
  transfers between devices with their start and end apart: 10, of which 1 were waited for; matrix products, arithmetic and copies ran while one was open for 0% of the time, Pallas kernels for 32%

profile of v5, /device:TPU:1, one launch (start us, length us, event | category | flops | bytes accessed | tf_op | source)
XLA Modules:
  0.0 25.1 jit_solution(6666457539533319723)
XLA Ops:
  0.0 2.1 %pack.1 = (bf16[2048,256]{1,0:T(8,128)(2,1)S(1)}, s32[8,256]{1,0:T(8,128)S(1)}, s32[1,8]{1,0:T(1,128)S(1)}, bf16[256,256]{1,0:T(8,128)(2,1)S(1)}, s32[8,16]{1,0:T(8,128)S(1)}, /*index=5*/bf16[512,256]{1,0:T(8,128)(2,1)S(1)}) custom-call(bf16[2048,256]{1,0:T(8,128)(2,1)} %feat_hbm.1, s32[8,256]{1,0:T(8,128)} %bitcast.2, s32[1,8]{1,0:T(1,128)} %count_hbm.1, ...), custom_call_target="tpu_custom_call" | custom-call | tf_op jit(solution)/shard_map/pack/pallas_call | solution.py:93
  2.1 3.1 %collective-permute-start.2 = (bf16[512,256]{1,0:T(8,128)(2,1)S(1)}, bf16[512,256]{1,0:T(8,128)(2,1)S(1)}, u32[]{:S(2)}, u32[]{:S(2)}) collective-permute-start(bf16[512,256]{1,0:T(8,128)(2,1)S(1)} %get-tuple-element.39), channel_id=1, source_target_pairs={{0,24},{4,28},{8,16},{12,20},{16,8},{20,12},{24,0},{28,4},{1,25},{... | collective-permute-start | bytes 786440 | tf_op jit(solution)/shard_map/ppermute | solution.py:348
  5.1 1.6 %more.1 = (bf16[128,128,128]{2,1,0:T(8,128)(2,1)S(1)}, bf16[512,256]{1,0:T(8,128)(2,1)S(1)}, bf16[512,256]{1,0:T(8,128)(2,1)S(1)}) custom-call(bf16[2048,256]{1,0:T(8,128)(2,1)S(1)} %get-tuple-element.28.feat_ref, s32[8,256]{1,0:T(8,128)S(1)} %get-tuple-element.29.send_ref, s32[1,8]{1,0:T(1,128)S(1)} %get-tuple-element.30.count_ref, ...), custom_call_target="tpu_custom_call" | custom-call | tf_op jit(solution)/shard_map/more/pallas_call | solution.py:117
  6.8 0.3 %collective-permute-start.3 = (bf16[512,256]{1,0:T(8,128)(2,1)S(1)}, bf16[512,256]{1,0:T(8,128)(2,1)S(1)}, u32[]{:S(2)}, u32[]{:S(2)}) collective-permute-start(bf16[512,256]{1,0:T(8,128)(2,1)S(1)} %get-tuple-element.40), channel_id=1, source_target_pairs={{0,8},{4,12},{8,0},{12,4},{16,24},{20,28},{24,16},{28,20},{1,9},{5... | collective-permute-start | bytes 786440 | tf_op jit(solution)/shard_map/ppermute | solution.py:348
  7.1 0.1 collective-permute-start.4
  7.1 1.5 %collective-permute-start = (bf16[256,256]{1,0:T(8,128)(2,1)S(1)}, bf16[256,256]{1,0:T(8,128)(2,1)S(1)}, u32[]{:S(2)}, u32[]{:S(2)}) collective-permute-start(bf16[256,256]{1,0:T(8,128)(2,1)S(1)} %get-tuple-element.37.refs_1_), channel_id=1, source_target_pairs={{0,1},{1,0},{2,3},{3,2},{4,5},{5,4},{6,7},{7,6},{8,9},{9,8},{10,11... | collective-permute-start | bytes 393224 | tf_op jit(solution)/shard_map/ppermute | solution.py:348
  8.6 2.2 %collective-permute-start.1 = (bf16[256,256]{1,0:T(8,128)(2,1)S(1)}, bf16[256,256]{1,0:T(8,128)(2,1)S(1)}, u32[]{:S(2)}, u32[]{:S(2)}) collective-permute-start(bf16[256,256]{1,0:T(8,128)(2,1)S(1)} %get-tuple-element.37.refs_1_), channel_id=1, source_target_pairs={{0,2},{1,3},{2,0},{3,1},{4,7},{5,6},{6,5},{7,4},{8,10},{9,11},{10,... | collective-permute-start | bytes 393224 | tf_op jit(solution)/shard_map/ppermute | solution.py:354
  10.8 4.9 %local.1 = (f32[2048,256]{1,0:T(8,128)S(1)}, bf16[128,128,128]{2,1,0:T(8,128)(2,1)S(1)}, bf16[144,128,128]{2,1,0:T(8,128)(2,1)S(1)}, bf16[2048,1024]{1,0:T(8,128...) custom-call(bf16[2048,256]{1,0:T(8,128)(2,1)S(1)} %get-tuple-element.28.feat_ref, ...), custom_call_target="tpu_custom_call", output_to_operand_aliasing={{1}: (3, {})} | custom-call | tf_op jit(solution)/shard_map/local/pallas_call | solution.py:207
  15.7 0.0 collective-permute-done.near_ref
  15.7 2.3 %collective-permute-start.5 = (bf16[256,256]{1,0:T(8,128)(2,1)S(1)}, bf16[256,256]{1,0:T(8,128)(2,1)S(1)}, u32[]{:S(2)}, u32[]{:S(2)}) collective-permute-start(bf16[256,256]{1,0:T(8,128)(2,1)S(1)} %get-tuple-element.43), channel_id=1, source_target_pairs={{0,4},{4,0},{8,12},{12,8},{16,20},{20,16},{24,28},{28,24},{1,5},{5... | collective-permute-start | bytes 393224 | tf_op jit(solution)/shard_map/ppermute | solution.py:348
  18.0 0.0 collective-permute-done.1.refs_2_
  18.0 0.3 %collective-permute-start.6 = (bf16[256,256]{1,0:T(8,128)(2,1)S(1)}, bf16[256,256]{1,0:T(8,128)(2,1)S(1)}, u32[]{:S(2)}, u32[]{:S(2)}) collective-permute-start(bf16[256,256]{1,0:T(8,128)(2,1)S(1)} %collective-permute-done.1.refs_2_), channel_id=1, source_target_pairs={{0,4},{4,0},{8,12},{12,8},{16,20},{20,16},{24,28},{28,24},{1,5},{5... | collective-permute-start | bytes 393224 | tf_op jit(solution)/shard_map/ppermute | solution.py:348
  18.2 0.0 collective-permute-done.2.refs_1_
  18.2 0.0 collective-permute-done.3.refs_2_
  18.2 0.0 collective-permute-done.4.refs_3_
  18.3 0.3 %collective-permute-start.7 = (bf16[512,256]{1,0:T(8,128)(2,1)S(1)}, bf16[512,256]{1,0:T(8,128)(2,1)S(1)}, u32[]{:S(2)}, u32[]{:S(2)}) collective-permute-start(bf16[512,256]{1,0:T(8,128)(2,1)S(1)} %collective-permute-done.2.refs_1_), channel_id=1, source_target_pairs={{0,4},{4,0},{8,12},{12,8},{16,20},{20,16},{24,28},{28,24},{1,5},{5... | collective-permute-start | bytes 786440 | tf_op jit(solution)/shard_map/ppermute | solution.py:348
  18.6 0.3 %collective-permute-start.8 = (bf16[512,256]{1,0:T(8,128)(2,1)S(1)}, bf16[512,256]{1,0:T(8,128)(2,1)S(1)}, u32[]{:S(2)}, u32[]{:S(2)}) collective-permute-start(bf16[512,256]{1,0:T(8,128)(2,1)S(1)} %collective-permute-done.3.refs_2_), channel_id=1, source_target_pairs={{0,4},{4,0},{8,12},{12,8},{16,20},{20,16},{24,28},{28,24},{1,5},{5... | collective-permute-start | bytes 786440 | tf_op jit(solution)/shard_map/ppermute | solution.py:348
  18.8 0.2 collective-permute-start.9
  19.1 0.0 collective-permute-done.5.refs_0_
  19.1 0.2 collective-permute-done.6.refs_3_
  19.3 1.5 %hub.1 = (f32[2048,256]{1,0:T(8,128)S(1)}, f32[16,1024]{1,0:T(8,128)S(1)}) custom-call(s32[8,16]{1,0:T(8,128)S(1)} %get-tuple-element.35.live_ref, bf16[2048,1024]{1,0:T(8,128)(2,1)S(1)} %get-tuple-element.34.adj_ref, f32[2048,256]{1,0:T(8,128)S(1)} %get-tuple-element.42.acc_ref, bf16[256,256]{1,0:T(8,128)(2,1)S(1)} %collective-permute-done.5.refs_0_, ...), custom_call_target="tpu_custom_call" | custom-call | flops 34359738368 | tf_op jit(solution)/shard_map/hub/pallas_call | solution.py:266
  20.8 0.0 collective-permute-done.8.refs_5_
  20.8 0.0 collective-permute-done.9.refs_6_
  20.8 4.2 %last.1 = bf16[2048,256]{1,0:T(8,128)(2,1)} custom-call(s32[256]{0:T(256)S(1)} %get-tuple-element.32.map_ref, bf16[144,128,128]{2,1,0:T(8,128)(2,1)S(1)} %get-tuple-element.33.edge_ref, bf16[2048,1024]{1,0:T(8,128)(2,1)S(1)} %get-tuple-element.34.adj_ref, f32[16,1024]{1,0:T(8,128)S(1)} %get-tuple-element.45.mask_ref, ...), custom_call_target="tpu_custom_call" | custom-call | tf_op jit(solution)/shard_map/last/pallas_call | solution.py:329
  (3 shorter events, 0.0 us)
Async XLA Ops:
  2.1 16.2 %collective-permute-start.2 = (bf16[512,256]{1,0:T(8,128)(2,1)S(1)}, bf16[512,256]{1,0:T(8,128)(2,1)S(1)}, u32[]{:S(2)}, u32[]{:S(2)}) collective-permute-start(bf16[512,256]{1,0:T(8,128)(2,1)S(1)} %get-tuple-element.39), channel_id=1, source_target_pairs={{0,24},{4,28},{8,16},{12,20},{16,8},{20,12},{24,0},{28,4},{1,25},{... | collective-permute-start | bytes 786440 | tf_op jit(solution)/shard_map/ppermute | solution.py:348
  6.8 11.5 %collective-permute-start.3 = (bf16[512,256]{1,0:T(8,128)(2,1)S(1)}, bf16[512,256]{1,0:T(8,128)(2,1)S(1)}, u32[]{:S(2)}, u32[]{:S(2)}) collective-permute-start(bf16[512,256]{1,0:T(8,128)(2,1)S(1)} %get-tuple-element.40), channel_id=1, source_target_pairs={{0,8},{4,12},{8,0},{12,4},{16,24},{20,28},{24,16},{28,20},{1,9},{5... | collective-permute-start | bytes 786440 | tf_op jit(solution)/shard_map/ppermute | solution.py:348
  7.1 11.2 %collective-permute-start.4 = (bf16[512,256]{1,0:T(8,128)(2,1)S(1)}, bf16[512,256]{1,0:T(8,128)(2,1)S(1)}, u32[]{:S(2)}, u32[]{:S(2)}) collective-permute-start(bf16[512,256]{1,0:T(8,128)(2,1)S(1)} %get-tuple-element.41), channel_id=1, source_target_pairs={{0,16},{4,20},{8,24},{12,28},{16,0},{20,4},{24,8},{28,12},{1,17},{... | collective-permute-start | bytes 786440 | tf_op jit(solution)/shard_map/ppermute | solution.py:348
  7.1 8.6 %collective-permute-start = (bf16[256,256]{1,0:T(8,128)(2,1)S(1)}, bf16[256,256]{1,0:T(8,128)(2,1)S(1)}, u32[]{:S(2)}, u32[]{:S(2)}) collective-permute-start(bf16[256,256]{1,0:T(8,128)(2,1)S(1)} %get-tuple-element.37.refs_1_), channel_id=1, source_target_pairs={{0,1},{1,0},{2,3},{3,2},{4,5},{5,4},{6,7},{7,6},{8,9},{9,8},{10,11... | collective-permute-start | bytes 393224 | tf_op jit(solution)/shard_map/ppermute | solution.py:348
  8.6 9.4 %collective-permute-start.1 = (bf16[256,256]{1,0:T(8,128)(2,1)S(1)}, bf16[256,256]{1,0:T(8,128)(2,1)S(1)}, u32[]{:S(2)}, u32[]{:S(2)}) collective-permute-start(bf16[256,256]{1,0:T(8,128)(2,1)S(1)} %get-tuple-element.37.refs_1_), channel_id=1, source_target_pairs={{0,2},{1,3},{2,0},{3,1},{4,7},{5,6},{6,5},{7,4},{8,10},{9,11},{10,... | collective-permute-start | bytes 393224 | tf_op jit(solution)/shard_map/ppermute | solution.py:354
  15.7 3.4 %collective-permute-start.5 = (bf16[256,256]{1,0:T(8,128)(2,1)S(1)}, bf16[256,256]{1,0:T(8,128)(2,1)S(1)}, u32[]{:S(2)}, u32[]{:S(2)}) collective-permute-start(bf16[256,256]{1,0:T(8,128)(2,1)S(1)} %get-tuple-element.43), channel_id=1, source_target_pairs={{0,4},{4,0},{8,12},{12,8},{16,20},{20,16},{24,28},{28,24},{1,5},{5... | collective-permute-start | bytes 393224 | tf_op jit(solution)/shard_map/ppermute | solution.py:348
  18.0 1.3 %collective-permute-start.6 = (bf16[256,256]{1,0:T(8,128)(2,1)S(1)}, bf16[256,256]{1,0:T(8,128)(2,1)S(1)}, u32[]{:S(2)}, u32[]{:S(2)}) collective-permute-start(bf16[256,256]{1,0:T(8,128)(2,1)S(1)} %collective-permute-done.1.refs_2_), channel_id=1, source_target_pairs={{0,4},{4,0},{8,12},{12,8},{16,20},{20,16},{24,28},{28,24},{1,5},{5... | collective-permute-start | bytes 393224 | tf_op jit(solution)/shard_map/ppermute | solution.py:348
  18.3 2.6 %collective-permute-start.7 = (bf16[512,256]{1,0:T(8,128)(2,1)S(1)}, bf16[512,256]{1,0:T(8,128)(2,1)S(1)}, u32[]{:S(2)}, u32[]{:S(2)}) collective-permute-start(bf16[512,256]{1,0:T(8,128)(2,1)S(1)} %collective-permute-done.2.refs_1_), channel_id=1, source_target_pairs={{0,4},{4,0},{8,12},{12,8},{16,20},{20,16},{24,28},{28,24},{1,5},{5... | collective-permute-start | bytes 786440 | tf_op jit(solution)/shard_map/ppermute | solution.py:348
  18.6 2.3 %collective-permute-start.8 = (bf16[512,256]{1,0:T(8,128)(2,1)S(1)}, bf16[512,256]{1,0:T(8,128)(2,1)S(1)}, u32[]{:S(2)}, u32[]{:S(2)}) collective-permute-start(bf16[512,256]{1,0:T(8,128)(2,1)S(1)} %collective-permute-done.3.refs_2_), channel_id=1, source_target_pairs={{0,4},{4,0},{8,12},{12,8},{16,20},{20,16},{24,28},{28,24},{1,5},{5... | collective-permute-start | bytes 786440 | tf_op jit(solution)/shard_map/ppermute | solution.py:348
  18.8 2.0 %collective-permute-start.9 = (bf16[512,256]{1,0:T(8,128)(2,1)S(1)}, bf16[512,256]{1,0:T(8,128)(2,1)S(1)}, u32[]{:S(2)}, u32[]{:S(2)}) collective-permute-start(bf16[512,256]{1,0:T(8,128)(2,1)S(1)} %collective-permute-done.4.refs_3_), channel_id=1, source_target_pairs={{0,4},{4,0},{8,12},{12,8},{16,20},{20,16},{24,28},{28,24},{1,5},{5... | collective-permute-start | bytes 786440 | tf_op jit(solution)/shard_map/ppermute | solution.py:348
  19.3 1.5 %copy-start = (bf16[256,256]{1,0:T(8,128)(2,1)S(1)}, bf16[256,256]{1,0:T(8,128)(2,1)}, u32[]{:S(2)}) copy-start(bf16[256,256]{1,0:T(8,128)(2,1)} %weight_ref.1) | copy-start | bytes 393220

commit v6 on v5

--- a/solution.py
+++ b/solution.py
@@ -10,7 +10,7 @@
 BF = jnp.bfloat16
 F32 = jnp.float32
 I32 = jnp.int32
-LONG = pl.CostEstimate(flops=1 << 35, bytes_accessed=0, transcendentals=0)
+EARLY = pl.CostEstimate(flops=1 << 35, bytes_accessed=0, transcendentals=0)
 VMEM = pl.BlockSpec(memory_space=pltpu.VMEM)
 SMEM = pl.BlockSpec(memory_space=pltpu.SMEM)
 HBM = pl.BlockSpec(memory_space=pltpu.HBM)
@@ -23,6 +23,7 @@
 ANY = pl.BlockSpec(memory_space=pl.ANY)
 MIB = 1 << 20
 FREE = pl.CostEstimate(flops=0, bytes_accessed=0, transcendentals=0)
+EARLY = pl.CostEstimate(flops=1 << 35, bytes_accessed=0, transcendentals=0)
 LONG = pl.CostEstimate(flops=1 << 35, bytes_accessed=0, transcendentals=0)
 
 
@@ -98,33 +99,26 @@
         out_specs=[VMEM] * (5 + len(offsets)),
         scratch_shapes=[pltpu.SMEM(send_count.shape, I32), pltpu.SemaphoreType.DMA((6,))],
         compiler_params=params(16),
-        cost_estimate=FREE,
+        cost_estimate=EARLY,
         name="pack",
     )(*hbm(*arrays))
 
 
-def more_kernel(offsets, feat_ref, send_ref, count_ref, tiles_hbm, tiles_ref, *refs):
-    *packed, sem = refs
-    half = pl.ds(0, tiles_ref.shape[0] // 2)
-    copy = pltpu.make_async_copy(tiles_hbm.at[half], tiles_ref.at[half], sem)
-    copy.start()
+def more_kernel(offsets, feat_ref, send_ref, count_ref, *packed):
     gather_groups(offsets, send_ref, count_ref, feat_ref, packed)
-    copy.wait()
-
-
-def pack_more(offsets, features, send_rows, send_count, tiles):
+
+
+def pack_more(offsets, features, send_rows, send_count):
     slots, width = send_rows.shape[1], features.shape[1]
     return pl.pallas_call(
         functools.partial(more_kernel, offsets),
-        out_shape=[jax.ShapeDtypeStruct(tiles.shape, BF)]
-        + [jax.ShapeDtypeStruct((len(group) * slots, width), BF) for group in offsets],
-        in_specs=[VMEM] * 3 + [HBM],
-        out_specs=[VMEM] * (1 + len(offsets)),
-        scratch_shapes=[pltpu.SemaphoreType.DMA],
-        compiler_params=params(16),
-        cost_estimate=FREE,
+        out_shape=[jax.ShapeDtypeStruct((len(group) * slots, width), BF) for group in offsets],
+        in_specs=[VMEM] * 3,
+        out_specs=[VMEM] * len(offsets),
+        compiler_params=params(16),
+        cost_estimate=EARLY,
         name="more",
-    )(features, send_rows, send_count, *hbm(tiles))
+    )(features, send_rows, send_count)
 
 
 def clear_map(map_ref):
@@ -148,20 +142,27 @@
     return [cell_tile(tiles_ref, map_ref, row * cols + source * per + j) for source in sources for j in range(per)]
 
 
-def local_kernel(block, feat_ref, send_ref, count_ref, begun_ref, *refs):
-    del begun_ref
-    sources, (out_ref, tiles_ref, edge_ref, adj_ref, map_hbm, core_ref, *refs) = list(refs[:7]), refs[7:]
-    *tables, local_map, edge_map, own_ref, sems = refs
-    half = pl.ds(tiles_ref.shape[0] // 2, tiles_ref.shape[0] // 2)
-    sources[4] = sources[4].at[half]
-    copies = start_all(sources, [*tables, tiles_ref.at[half], edge_ref, adj_ref], sems)
+def hub_line(adj_ref, live_ref, row, size, owner, per):
+    line = []
+    for b in [owner * per + j for j in range(per)]:
+        cell = adj_ref[pl.ds(pl.multiple_of(row * size, size), size), pl.ds(pl.multiple_of(b * size, size), size)]
+        line.append(jnp.where(live_ref[b, row] > 0, cell, jnp.zeros_like(cell)))
+    return line
+
+
+def local_kernel(block, feat_ref, send_ref, count_ref, tiles_ref, edge_ref, adj_ref, live_vmem, hub_ref, *refs):
+    sources, (out_ref, map_hbm, core_ref, *refs) = refs[:4], refs[4:]
+    *tables, live_ref, local_map, edge_map, rhs_ref, sems = refs
+    copies = start_all([*sources, live_vmem], [*tables, live_ref], sems)
+    shard = hub_ref.shape[0]
+    own_ref = rhs_ref.at[shard:]
+    rhs_ref[:shard, :] = hub_ref[...]
     gather_groups([(1,)], send_ref, count_ref, feat_ref, [core_ref])
-    wait_all(copies[:4])
+    wait_all(copies)
     clear_map(local_map)
     fill_map(tables[0], tables[1], local_map, 0, tables[0].shape[0])
     clear_map(edge_map)
     gather_groups([(0,)], send_ref, count_ref, feat_ref, [own_ref])
-    copies[4].wait()
     size = tiles_ref.shape[1]
     rows = feat_ref.shape[0]
     cols, edge_cols = rows // size, edge_map.shape[0] // (rows // size)
@@ -183,23 +184,26 @@
 
     lax.fori_loop(0, steps, local_body, 0)
     fill_map(tables[2], tables[3], edge_map, steps * share, tables[2].shape[0] - steps * share)
-    copies.append(pltpu.make_async_copy(edge_map, map_hbm, sems.at[7]))
-    copies[7].start()
-    copies[5].wait()
-    me = lax.axis_index("row")
+    write = pltpu.make_async_copy(edge_map, map_hbm, sems.at[5])
+    write.start()
+    me, loop = lax.axis_index("row"), lax.axis_index("loop")
     per = own_ref.shape[0] // size
 
     def own_body(m, _):
-        lines = [edge_line(edge_ref, edge_map, m * block + i, edge_cols, [me], per) for i in range(block)]
-        own_tiles = jnp.concatenate([jnp.concatenate(line, axis=1) for line in lines], axis=0)
-        out_ref[span(m), :] += dot(own_tiles, own_ref[...])
+        blocks = []
+        for i in range(block):
+            row = m * block + i
+            line = hub_line(adj_ref, live_ref, row, size, loop, shard // size)
+            line += edge_line(edge_ref, edge_map, row, edge_cols, [me], per)
+            blocks.append(jnp.concatenate(line, axis=1))
+        out_ref[span(m), :] += dot(jnp.concatenate(blocks, axis=0), rhs_ref[...])
         return 0
 
     lax.fori_loop(0, steps, own_body, 0)
-    wait_all(copies[6:])
-
-
-def local_term(features, send_rows, send_count, begun, tables, tiles, edges, adj):
+    write.wait()
+
+
+def local_term(features, send_rows, send_count, tables, tiles, edges, adj, hub_live, hub):
     rows, width = features.shape
     peers, slots = send_rows.shape
     size = tiles.shape[1]
@@ -208,20 +212,38 @@
         functools.partial(local_kernel, 8),
         out_shape=[
             jax.ShapeDtypeStruct(features.shape, F32),
-            *[jax.ShapeDtypeStruct(x.shape, BF) for x in (tiles, edges, adj)],
             jax.ShapeDtypeStruct((edge_cells,), I32),
             jax.ShapeDtypeStruct((slots, width), BF),
         ],
-        in_specs=[VMEM] * 4 + [HBM] * 7,
-        out_specs=[VMEM] * 4 + [ANY, VMEM],
+        in_specs=[VMEM] * 8 + [HBM] * 4,
+        out_specs=[VMEM, ANY, VMEM],
         scratch_shapes=[pltpu.SMEM(x.shape, I32) for x in tables]
-        + [pltpu.SMEM((local_cells,), I32), pltpu.SMEM((edge_cells,), I32)]
-        + [pltpu.VMEM((slots, width), BF), pltpu.SemaphoreType.DMA((8,))],
-        input_output_aliases={3: 1},
+        + [pltpu.SMEM(hub_live.shape, I32), pltpu.SMEM((local_cells,), I32), pltpu.SMEM((edge_cells,), I32)]
+        + [pltpu.VMEM((hub.shape[0] + slots, width), BF), pltpu.SemaphoreType.DMA((6,))],
         compiler_params=params(16),
         cost_estimate=FREE,
         name="local",
-    )(features, send_rows, send_count, begun, *hbm(*tables, tiles, edges, adj))
+    )(features, send_rows, send_count, tiles, edges, adj, hub_live, hub, *hbm(*tables))
+
+
+def stack_kernel(rows, *refs):
+    *array_refs, out_ref = refs
+    at = 0
+    for array_ref, (first, count) in zip(array_refs, rows):
+        out_ref[at : at + count, :] = array_ref[first : first + count, :]
+        at += count
+
+
+def stack(rows, arrays):
+    return pl.pallas_call(
+        functools.partial(stack_kernel, rows),
+        out_shape=jax.ShapeDtypeStruct((sum(count for _, count in rows), arrays[0].shape[1]), BF),
+        in_specs=[VMEM] * len(arrays),
+        out_specs=VMEM,
+        compiler_params=params(16),
+        cost_estimate=FREE,
+        name="stack",
+    )(*arrays)
 
 
 def masked_line(adj_ref, mask_ref, row, size, columns):
@@ -233,17 +255,24 @@
     return jnp.concatenate(line, axis=1)
 
 
-def hub_kernel(block, hubs, waited, live_ref, adj_ref, acc_ref, *refs):
-    *array_refs, out_ref, mask_ref, rhs_ref = refs[waited:]
-    core, loop = lax.rem(lax.axis_index("row"), 2), lax.axis_index("loop")
-    shard = array_refs[0].shape[0]
+def middle_kernel(block, hubs, pieces, map_ref, live_ref, adj_ref, edge_ref, acc_ref, *refs):
+    *array_refs, out_ref, mask_ref, edge_map, hub_rhs, rhs_ref, sem = refs
+    table = pltpu.make_async_copy(map_ref, edge_map, sem)
+    table.start()
+    me, loop = lax.axis_index("row"), lax.axis_index("loop")
+    core = lax.rem(me, 2)
     tiles, rows = live_ref.shape
     size = adj_ref.shape[0] // rows
+    cols = edge_map.shape[0] // rows
+    shard, slots = hub_rhs.shape[0] // len(hubs), rhs_ref.shape[0] // len(pieces)
     columns = []
-    for n, (array_ref, (even, odd)) in enumerate(zip(array_refs, hubs)):
+    for n, (even, odd) in enumerate(hubs):
         owner = loop ^ jnp.where(core == 0, even, odd)
         columns.append(pl.ds(pl.multiple_of(owner * shard, shard), shard))
-        rhs_ref[n * shard : (n + 1) * shard, :] = array_ref[...]
+        hub_rhs[n * shard : (n + 1) * shard, :] = array_refs[n][...]
+    for n in range(len(pieces)):
+        rhs_ref[n * slots : (n + 1) * slots, :] = array_refs[len(hubs) + n][:slots, :]
+    sources = [me ^ offset for offset in pieces]
     lane = lax.broadcasted_iota(I32, (tiles, adj_ref.shape[1]), 1)
     first = lax.broadcasted_iota(I32, (tiles, adj_ref.shape[1]), 0) * size
     inside = (lane >= first) & (lane < first + size)
@@ -252,47 +281,70 @@
         hit = jnp.where(inside & (live[:, row : row + 1] > 0), 1.0, 0.0)
         mask_ref[row : row + 1, :] = jnp.sum(hit, axis=0, keepdims=True)
 
-    def body(m, _):
+    def span(m):
+        return pl.ds(pl.multiple_of(m * block * size, block * size), block * size)
+
+    def hub_body(m, _):
         blocks = [masked_line(adj_ref, mask_ref, m * block + i, size, columns) for i in range(block)]
-        span = pl.ds(pl.multiple_of(m * block * size, block * size), block * size)
-        out_ref[span, :] = acc_ref[span, :] + dot(jnp.concatenate(blocks, axis=0), rhs_ref[...])
-        return 0
-
-    lax.fori_loop(0, rows // block, body, 0)
-
-
-def hub_term(hubs, waited, hub_live, adj, acc, arrays):
+        out_ref[span(m), :] = acc_ref[span(m), :] + dot(jnp.concatenate(blocks, axis=0), hub_rhs[...])
+        return 0
+
+    lax.fori_loop(0, rows // block, hub_body, 0)
+    table.wait()
+
+    def edge_body(m, _):
+        lines = [
+            edge_line(edge_ref, edge_map, m * block + i, cols, sources, slots // size) for i in range(block)
+        ]
+        found = jnp.concatenate([jnp.concatenate(line, axis=1) for line in lines], axis=0)
+        out_ref[span(m), :] += dot(found, rhs_ref[...])
+        return 0
+
+    lax.fori_loop(0, rows // block, edge_body, 0)
+
+
+def middle_term(hubs, pieces, slots, edge_map, hub_live, adj, edges, acc, arrays):
     shard, width = arrays[0].shape
     return pl.pallas_call(
-        functools.partial(hub_kernel, 8, hubs, len(waited)),
+        functools.partial(middle_kernel, 8, hubs, pieces),
         out_shape=[
             jax.ShapeDtypeStruct(acc.shape, F32),
             jax.ShapeDtypeStruct((hub_live.shape[1], adj.shape[1]), F32),
         ],
-        in_specs=[VMEM] * (3 + len(waited) + len(arrays)),
+        in_specs=[ANY] + [VMEM] * (4 + len(arrays)),
         out_specs=[VMEM] * 2,
-        scratch_shapes=[pltpu.VMEM((len(hubs) * shard, width), BF)],
-        compiler_params=params(16),
-        cost_estimate=LONG,
-        name="hub",
-    )(hub_live, adj, acc, *waited, *arrays)
-
-
-def last_kernel(block, pieces, map_ref, edge_ref, adj_ref, mask_ref, acc_ref, weight_ref, near_ref, *refs):
-    *array_refs, out_ref, edge_map, rhs_ref, total_ref, stage_ref, sems = refs
+        scratch_shapes=[
+            pltpu.SMEM(edge_map.shape, I32),
+            pltpu.VMEM((len(hubs) * shard, width), BF),
+            pltpu.VMEM((len(pieces) * slots, width), BF),
+            pltpu.SemaphoreType.DMA,
+        ],
+        compiler_params=params(16),
+        cost_estimate=FREE,
+        name="middle",
+    )(edge_map, hub_live, adj, edges, acc, *arrays)
+
+
+def last_kernel(block, pieces, hubs, map_ref, edge_ref, adj_ref, mask_ref, acc_ref, weight_ref, *refs):
+    *array_refs, out_ref, edge_map, hub_ref, rhs_ref, total_ref, stage_ref, sems = refs
     size = edge_ref.shape[1]
     rows = acc_ref.shape[0]
     steps = rows // (block * size)
     table = pltpu.make_async_copy(map_ref, edge_map, sems.at[steps])
     table.start()
     me, loop = lax.axis_index("row"), lax.axis_index("loop")
+    core = lax.rem(me, 2)
     cols = edge_map.shape[0] // (rows // size)
     slots = rhs_ref.shape[0] // len(pieces)
-    shard = near_ref.shape[0]
+    shard = hub_ref.shape[0] // len(hubs)
+    columns = []
+    for n, (array, first, even, odd) in enumerate(hubs):
+        owner = loop ^ jnp.where(core == 0, even, odd)
+        columns.append(pl.ds(pl.multiple_of(owner * shard, shard), shard))
+        hub_ref[n * shard : (n + 1) * shard, :] = array_refs[array][first : first + shard, :]
     for n, (array, first, _) in enumerate(pieces):
         rhs_ref[n * slots : (n + 1) * slots, :] = array_refs[array][first : first + slots, :]
     sources = [me ^ offset for _, _, offset in pieces]
-    columns = [pl.ds(pl.multiple_of((loop ^ 1) * shard, shard), shard)]
 
     def span(m):
         return pl.ds(pl.multiple_of(m * block * size, block * size), block * size)
@@ -300,12 +352,12 @@
     def write(m):
         return pltpu.make_async_copy(stage_ref.at[span(m)], out_ref.at[span(m)], sems.at[m])
 
-    def near_body(m, _):
+    def hub_body(m, _):
         blocks = [masked_line(adj_ref, mask_ref, m * block + i, size, columns) for i in range(block)]
-        total_ref[span(m), :] = acc_ref[span(m), :] + dot(jnp.concatenate(blocks, axis=0), near_ref[...])
-        return 0
-
-    lax.fori_loop(0, steps, near_body, 0)
+        total_ref[span(m), :] = acc_ref[span(m), :] + dot(jnp.concatenate(blocks, axis=0), hub_ref[...])
+        return 0
+
+    lax.fori_loop(0, steps, hub_body, 0)
     table.wait()
 
     def body(m, _):
@@ -323,16 +375,17 @@
         write(m).wait()
 
 
-def last_term(pieces, slots, edge_map, edges, adj, mask, acc, weight, near, arrays):
+def last_term(pieces, hubs, slots, shard, edge_map, edges, adj, mask, acc, weight, arrays):
     block = 8
     rows, width = acc.shape
     return pl.pallas_call(
-        functools.partial(last_kernel, block, pieces),
+        functools.partial(last_kernel, block, pieces, hubs),
         out_shape=jax.ShapeDtypeStruct(acc.shape, BF),
-        in_specs=[ANY] + [VMEM] * (6 + len(arrays)),
+        in_specs=[ANY] + [VMEM] * (5 + len(arrays)),
         out_specs=HBM,
         scratch_shapes=[
             pltpu.SMEM(edge_map.shape, I32),
+            pltpu.VMEM((len(hubs) * shard, width), BF),
             pltpu.VMEM((len(pieces) * slots, width), BF),
             pltpu.VMEM(acc.shape, F32),
             pltpu.VMEM(acc.shape, BF),
@@ -341,7 +394,7 @@
         compiler_params=params(16),
         cost_estimate=FREE,
         name="last",
-    )(edge_map, edges, adj, mask, acc, weight, near, *arrays)
+    )(edge_map, edges, adj, mask, acc, weight, *arrays)
 
 
 def swap(x, axis, offset):
@@ -380,35 +433,34 @@
         [(c, c ^ 1) for c in far_chips], features, send_rows[0], send_count, hub_feats, hub_live.T
     )
     from_far = [swap(x, "row", c) for x, c in zip(packed, far_chips)]
-    tiles, *packed = pack_more([(c, c ^ 1) for c in near_chips], feat, sends, counts, local_tiles)
+    packed = pack_more([(c, c ^ 1) for c in near_chips], feat, sends, counts)
     from_near = [swap(x, "row", c) for x, c in zip(packed, near_chips)]
     near = swap(hub, "loop", 1)
     far = [swap_by_core(hub, offset, offset + 1) for offset in range(2, ring, 2)]
-    acc, _, edges, adj, edge_map, to_core = local_term(
+    acc, edge_map, to_core = local_term(
         feat,
         sends,
         counts,
-        tiles,
         (local_ids, local_live, edge_ids, edge_live),
         local_tiles,
         edge_tiles,
         hub_adj,
+        live,
+        hub,
     )
-    from_core = swap(to_core, "row", 1)
-    acc, near, *far = lax.optimization_barrier((acc, near, *far))
-    from_far = lax.optimization_barrier(tuple(from_far))
-    acc, *arrived = lax.optimization_barrier((acc, *from_far, *from_near))
-    shared = [swap(x, "row", 1) for x in arrived]
-    far_shared = [swap(x, "row", 1) for x in far]
-    hubs, arrays = [(0, 0)], [hub]
-    for n, (x, y) in enumerate(zip(far, far_shared)):
-        hubs += [(2 * n + 2, 2 * n + 3), (2 * n + 3, 2 * n + 2)]
-        arrays += [x, y]
-    acc, mask = hub_term(hubs, [from_core], live, adj, acc, arrays)
-    pieces = [(0, 0, 1)]
-    for n, c in enumerate(far_chips + near_chips):
-        pieces += [(1 + n, 0, c), (1 + len(chips) + n, slots, c ^ 1)]
-    return last_term(pieces, slots, edge_map, edges, adj, mask, acc, weight, near, [from_core, *arrived, *shared])
+    arrived = from_far + from_near
+    shard = hub.shape[0]
+    rows = [(0, slots)] + [(slots, slots)] * len(arrived) + [(0, shard)] * len(far)
+    shared = swap(stack(rows, [to_core, *arrived, *far, near]), "row", 1)
+    hubs = [(1, 1)] + [(2 * n + 2, 2 * n + 3) for n in range(len(far))]
+    order = far_chips + near_chips
+    acc, mask = middle_term(
+        hubs, order, slots, edge_map, live, hub_adj, edge_tiles, acc, [near, *far, *arrived]
+    )
+    pieces = [(0, 0, 1)] + [(0, (1 + n) * slots, c ^ 1) for n, c in enumerate(order)]
+    at = len(pieces) * slots
+    hubs = [(0, at + n * shard, 2 * n + 3, 2 * n + 2) for n in range(len(far))]
+    return last_term(pieces, hubs, slots, shard, edge_map, edge_tiles, hub_adj, mask, acc, weight, [shared])
 
 
 def solution(mesh):

time: 25.5 us -> 24.6 us (0.965)
  starting transfers between devices: 10.4 us -> 7.79 us
  waiting for transfers between devices: 0.27 us -> 1.84 us
  Pallas kernels: 14.3 us -> 14.7 us
    ppermute x9 -> x5, starting transfers between devices: 8.25 us -> 4.31 us  [swap(): lax.ppermute(x, axis, [(i, i ^ offset) for i in range(lax.axis_size(axis))])]
    ppermute x9 -> x5, waiting for transfers between devices: 0.27 us -> 1.83 us  [swap(): lax.ppermute(x, axis, [(i, i ^ offset) for i in range(lax.axis_size(axis))])]
    ppermute x1, starting transfers between devices: 2.2 us -> 3.48 us  [swap_by_core(): return lax.ppermute(x, ('row', 'loop'), pairs)]
    pallas_call x1, Pallas kernels: 4.9 us -> 5.22 us  [local_term(): pl.pallas_call(functools.partial(local_kernel, 8), out_shape=[jax.ShapeDt...]
    pallas_call x2 -> x3, Pallas kernels: 5.72 us -> 5.86 us  [the longest x1 3.44 us: last_term(): pl.pallas_call(functools.partial(last_kernel, block, pieces, hubs), out_s...]
  transfers between devices with their start and end apart: 10 -> 6, of which waited for: 1 -> 3; matrix products, arithmetic and copies ran while one was open for 0% -> 0% of each run, Pallas kernels for 32% -> 37%
where the time goes in v6:
time: 24.6 us; the launch traced here: 24.4 us
  Pallas kernels  14.7 us (60%)
  starting transfers between devices  7.79 us (32%)
  waiting for transfers between devices  1.84 us (7%)
    pallas_call x1, Pallas kernels, local_term(): pl.pallas_call(functools.partial(local_kernel, 8), out_shape=[jax.ShapeDt...  5.22 us
    ppermute x5, starting transfers between devices, swap(): lax.ppermute(x, axis, [(i, i ^ offset) for i in range(lax.axis_size(axis))])  4.31 us
    ppermute x1, starting transfers between devices, swap_by_core(): return lax.ppermute(x, ('row', 'loop'), pairs)  3.48 us
    pallas_call x1, Pallas kernels, last_term(): pl.pallas_call(functools.partial(last_kernel, block, pieces, hubs), out_s...  3.44 us
    pallas_call x1, Pallas kernels, middle_term(): pl.pallas_call(functools.partial(middle_kernel, 8, hubs, pieces), out_sha...  2.38 us
    pallas_call x1, Pallas kernels, pack(): pl.pallas_call(functools.partial(pack_kernel, offsets), out_shape=[jax.Sh...  2.21 us
    ppermute x5, waiting for transfers between devices, swap(): lax.ppermute(x, axis, [(i, i ^ offset) for i in range(lax.axis_size(axis))])  1.83 us
    pallas_call x1, Pallas kernels, pack_more(): pl.pallas_call(functools.partial(more_kernel, offsets), out_shape=[jax.Sh...  1.39 us
  transfers between devices with their start and end apart: 6, of which 3 were waited for; matrix products, arithmetic and copies ran while one was open for 0% of the time, Pallas kernels for 37%

profile of v6, /device:TPU:1, one launch (start us, length us, event | category | flops | bytes accessed | tf_op | source)
XLA Modules:
  0.0 24.4 jit_solution(12247833350472065643)
XLA Ops:
  0.0 0.0 slice-start
  0.0 2.2 %pack.1 = (bf16[2048,256]{1,0:T(8,128)(2,1)S(1)}, s32[8,256]{1,0:T(8,128)S(1)}, s32[1,8]{1,0:T(1,128)S(1)}, bf16[256,256]{1,0:T(8,128)(2,1)S(1)}, s32[8,16]{1,0:T(8,128)S(1)}, /*index=5*/bf16[512,256]{1,0:T(8,128)(2,1)S(1)}) custom-call(bf16[2048,256]{1,0:T(8,128)(2,1)} %feat_hbm.1, s32[8,256]{1,0:T(8,128)} %bitcast.4, s32[1,8]{1,0:T(1,128)} %count_hbm.1, ...), custom_call_target="tpu_custom_call" | custom-call | flops 34359738368 | tf_op jit(solution)/shard_map/pack/pallas_call | solution.py:94
  2.2 3.1 %collective-permute-start.2 = (bf16[512,256]{1,0:T(8,128)(2,1)S(1)}, bf16[512,256]{1,0:T(8,128)(2,1)S(1)}, u32[]{:S(2)}, u32[]{:S(2)}) collective-permute-start(bf16[512,256]{1,0:T(8,128)(2,1)S(1)} %get-tuple-element.25), channel_id=1, source_target_pairs={{0,24},{4,28},{8,16},{12,20},{16,8},{20,12},{24,0},{28,4},{1,25},{... | collective-permute-start | bytes 786440 | tf_op jit(solution)/shard_map/ppermute | solution.py:401
  5.3 0.0 slice-start.1
  5.3 1.4 %more.1 = (bf16[512,256]{1,0:T(8,128)(2,1)S(1)}, bf16[512,256]{1,0:T(8,128)(2,1)S(1)}) custom-call(bf16[2048,256]{1,0:T(8,128)(2,1)S(1)} %get-tuple-element.18.feat_ref, s32[8,256]{1,0:T(8,128)S(1)} %get-tuple-element.19.send_ref, s32[1,8]{1,0:T(1,128)S(1)} %get-tuple-element.20.count_ref), custom_call_target="tpu_custom_call" | custom-call | flops 34359738368 | tf_op jit(solution)/shard_map/more/pallas_call | solution.py:113
  6.7 0.3 %collective-permute-start.3 = (bf16[512,256]{1,0:T(8,128)(2,1)S(1)}, bf16[512,256]{1,0:T(8,128)(2,1)S(1)}, u32[]{:S(2)}, u32[]{:S(2)}) collective-permute-start(bf16[512,256]{1,0:T(8,128)(2,1)S(1)} %get-tuple-element.26), channel_id=1, source_target_pairs={{0,8},{4,12},{8,0},{12,4},{16,24},{20,28},{24,16},{28,20},{1,9},{5... | collective-permute-start | bytes 786440 | tf_op jit(solution)/shard_map/ppermute | solution.py:401
  7.0 0.1 collective-permute-start.4
  7.1 3.5 %collective-permute-start.1 = (bf16[256,256]{1,0:T(8,128)(2,1)S(1)}, bf16[256,256]{1,0:T(8,128)(2,1)S(1)}, u32[]{:S(2)}, u32[]{:S(2)}) collective-permute-start(bf16[256,256]{1,0:T(8,128)(2,1)S(1)} %get-tuple-element.22.hub_ref), channel_id=1, source_target_pairs={{0,2},{1,3},{2,0},{3,1},{4,7},{5,6},{6,5},{7,4},{8,10},{9,11},{10,... | collective-permute-start | bytes 393224 | tf_op jit(solution)/shard_map/ppermute | solution.py:407
  10.6 0.0 collective-permute-start
  10.6 0.0 slice-done
  10.6 0.0 slice-done.1
  10.6 0.0 copy-done
  10.6 0.0 copy-done.1
  10.6 5.2 %local.1 = (f32[2048,256]{1,0:T(8,128)S(1)}, s32[256]{0:T(256)S(1)}, bf16[256,256]{1,0:T(8,128)(2,1)S(1)}) custom-call(bf16[2048,256]{1,0:T(8,128)(2,1)S(1)} %get-tuple-element.18.feat_ref, s32[8,256]{1,0:T(8,128)S(1)} %get-tuple-element.19.send_ref, s32[1,8]{1,0:T(1,128)S(1)} %get-tuple-element.20.count_ref, bf16[128,128,128]{2,1,0:T(8,128)(2,1)S(1)} %copy-done.1, ...), custom_call_target="tpu_custom_call" | custom-call | tf_op jit(solution)/shard_map/local/pallas_call | solution.py:211
  15.8 0.0 collective-permute-done.1.refs_1_.refs_4_
  15.8 0.9 %collective-permute-done.refs_0_.refs_5_ = bf16[256,256]{1,0:T(8,128)(2,1)S(1)} collective-permute-done((bf16[256,256]{1,0:T(8,128)(2,1)S(1)}, bf16[256,256]{1,0:T(8,128)(2,1)S(1)}, u32[]{:S(2)}, u32[]{:S(2)}) %collective-permute-start) | collective-permute-done | bytes 131104 | tf_op jit(solution)/shard_map/ppermute | solution.py:401
  16.7 0.0 collective-permute-done.2.refs_2_.refs_1_
  16.7 0.2 collective-permute-done.3.refs_3_.refs_2_
  16.9 0.8 %collective-permute-done.4.refs_4_.refs_3_ = bf16[512,256]{1,0:T(8,128)(2,1)S(1)} collective-permute-done((bf16[512,256]{1,0:T(8,128)(2,1)S(1)}, bf16[512,256]{1,0:T(8,128)(2,1)S(1)}, u32[]{:S(2)}, u32[]{:S(2)}) %collective-permute-start.4) | collective-permute-done | bytes 262176 | tf_op jit(solution)/shard_map/ppermute | solution.py:401
  17.7 0.9 %collective-permute-start.5 = (bf16[1280,256]{1,0:T(8,128)(2,1)S(1)}, bf16[1280,256]{1,0:T(8,128)(2,1)S(1)}, u32[]{:S(2)}, u32[]{:S(2)}) collective-permute-start(bf16[1280,256]{1,0:T(8,128)(2,1)S(1)} %stack.1), channel_id=1, source_target_pairs={{0,4},{4,0},{8,12},{12,8},{16,20},{20,16},{24,28},{28,24},{1,5},{5... | collective-permute-start | bytes 1966088 | tf_op jit(solution)/shard_map/ppermute | solution.py:401
  18.6 2.4 %middle.1 = (f32[2048,256]{1,0:T(8,128)S(1)}, f32[16,1024]{1,0:T(8,128)S(1)}) custom-call(s32[256]{0:T(256)S(1)} %get-tuple-element.23.map_ref, s32[8,16]{1,0:T(8,128)S(1)} %get-tuple-element.21.live_vmem.live_ref, bf16[2048,1024]{1,0:T(8,128)(2,1)S(1)} %copy-done, bf16[144,128,128]{2,1,0:T(8,128)(2,1)S(1)} %bitcast.3, ...), custom_call_target="tpu_custom_call" | custom-call | tf_op jit(solution)/shard_map/middle/pallas_call | solution.py:308
  21.0 0.0 collective-permute-done.5.refs_0_
  21.0 0.0 copy-done.2
  21.0 3.4 %last.1 = bf16[2048,256]{1,0:T(8,128)(2,1)} custom-call(s32[256]{0:T(256)S(1)} %get-tuple-element.23.map_ref, bf16[144,128,128]{2,1,0:T(8,128)(2,1)S(1)} %bitcast.3, bf16[2048,1024]{1,0:T(8,128)(2,1)S(1)} %copy-done, f32[16,1024]{1,0:T(8,128)S(1)} %get-tuple-element.28.mask_ref, f32[2048,256]{1,0:T(8,128)S(1)} %get-tuple-element.29.acc_ref, ...), custom_call_target="tpu_custom_call" | custom-call | tf_op jit(solution)/shard_map/last/pallas_call | solution.py:381
  (5 shorter events, 0.0 us)
Async XLA Ops:
  0.0 10.6 %slice-start = ((s8[4718592]{0:T(1024)(128)(4,1)}), s8[4194304]{0:T(1024)(128)(4,1)S(1)}, s32[]{:S(2)}) async-start(s8[4718592]{0:T(1024)(128)(4,1)} %bitcast.2), calls=%async_computation | async-start | bytes 8388608
  2.2 14.5 %collective-permute-start.2 = (bf16[512,256]{1,0:T(8,128)(2,1)S(1)}, bf16[512,256]{1,0:T(8,128)(2,1)S(1)}, u32[]{:S(2)}, u32[]{:S(2)}) collective-permute-start(bf16[512,256]{1,0:T(8,128)(2,1)S(1)} %get-tuple-element.25), channel_id=1, source_target_pairs={{0,24},{4,28},{8,16},{12,20},{16,8},{20,12},{24,0},{28,4},{1,25},{... | collective-permute-start | bytes 786440 | tf_op jit(solution)/shard_map/ppermute | solution.py:401
  5.3 5.3 %slice-start.1 = ((s8[4718592]{0:T(1024)(128)(4,1)}), s8[524288]{0:T(1024)(128)(4,1)S(1)}, s32[]{:S(2)}) async-start(s8[4718592]{0:T(1024)(128)(4,1)} %bitcast.2), calls=%async_computation.1 | async-start | bytes 1048576
  5.3 5.3 %copy-start = (bf16[2048,1024]{1,0:T(8,128)(2,1)S(1)}, bf16[2048,1024]{1,0:T(8,128)(2,1)}, u32[]{:S(2)}) copy-start(bf16[2048,1024]{1,0:T(8,128)(2,1)} %adj_ref.5) | copy-start | bytes 12582916
  5.3 5.3 %copy-start.1 = (bf16[128,128,128]{2,1,0:T(8,128)(2,1)S(1)}, bf16[128,128,128]{2,1,0:T(8,128)(2,1)}, u32[]{:S(2)}) copy-start(bf16[128,128,128]{2,1,0:T(8,128)(2,1)} %tiles_ref.1) | copy-start | bytes 12582916
  6.7 10.2 %collective-permute-start.3 = (bf16[512,256]{1,0:T(8,128)(2,1)S(1)}, bf16[512,256]{1,0:T(8,128)(2,1)S(1)}, u32[]{:S(2)}, u32[]{:S(2)}) collective-permute-start(bf16[512,256]{1,0:T(8,128)(2,1)S(1)} %get-tuple-element.26), channel_id=1, source_target_pairs={{0,8},{4,12},{8,0},{12,4},{16,24},{20,28},{24,16},{28,20},{1,9},{5... | collective-permute-start | bytes 786440 | tf_op jit(solution)/shard_map/ppermute | solution.py:401
  7.0 10.7 %collective-permute-start.4 = (bf16[512,256]{1,0:T(8,128)(2,1)S(1)}, bf16[512,256]{1,0:T(8,128)(2,1)S(1)}, u32[]{:S(2)}, u32[]{:S(2)}) collective-permute-start(bf16[512,256]{1,0:T(8,128)(2,1)S(1)} %get-tuple-element.27), channel_id=1, source_target_pairs={{0,16},{4,20},{8,24},{12,28},{16,0},{20,4},{24,8},{28,12},{1,17},{... | collective-permute-start | bytes 786440 | tf_op jit(solution)/shard_map/ppermute | solution.py:401
  7.1 8.7 %collective-permute-start.1 = (bf16[256,256]{1,0:T(8,128)(2,1)S(1)}, bf16[256,256]{1,0:T(8,128)(2,1)S(1)}, u32[]{:S(2)}, u32[]{:S(2)}) collective-permute-start(bf16[256,256]{1,0:T(8,128)(2,1)S(1)} %get-tuple-element.22.hub_ref), channel_id=1, source_target_pairs={{0,2},{1,3},{2,0},{3,1},{4,7},{5,6},{6,5},{7,4},{8,10},{9,11},{10,... | collective-permute-start | bytes 393224 | tf_op jit(solution)/shard_map/ppermute | solution.py:407
  10.6 6.2 %collective-permute-start = (bf16[256,256]{1,0:T(8,128)(2,1)S(1)}, bf16[256,256]{1,0:T(8,128)(2,1)S(1)}, u32[]{:S(2)}, u32[]{:S(2)}) collective-permute-start(bf16[256,256]{1,0:T(8,128)(2,1)S(1)} %get-tuple-element.22.hub_ref), channel_id=1, source_target_pairs={{0,1},{1,0},{2,3},{3,2},{4,5},{5,4},{6,7},{7,6},{8,9},{9,8},{10,11... | collective-permute-start | bytes 393224 | tf_op jit(solution)/shard_map/ppermute | solution.py:401
  17.7 3.2 %collective-permute-start.5 = (bf16[1280,256]{1,0:T(8,128)(2,1)S(1)}, bf16[1280,256]{1,0:T(8,128)(2,1)S(1)}, u32[]{:S(2)}, u32[]{:S(2)}) collective-permute-start(bf16[1280,256]{1,0:T(8,128)(2,1)S(1)} %stack.1), channel_id=1, source_target_pairs={{0,4},{4,0},{8,12},{12,8},{16,20},{20,16},{24,28},{28,24},{1,5},{5... | collective-permute-start | bytes 1966088 | tf_op jit(solution)/shard_map/ppermute | solution.py:401
  18.6 2.4 %copy-start.2 = (bf16[256,256]{1,0:T(8,128)(2,1)S(1)}, bf16[256,256]{1,0:T(8,128)(2,1)}, u32[]{:S(2)}) copy-start(bf16[256,256]{1,0:T(8,128)(2,1)} %weight_ref.1) | copy-start | bytes 393220

commit v7 on v6

--- a/solution.py
+++ b/solution.py
@@ -23,7 +23,6 @@
 ANY = pl.BlockSpec(memory_space=pl.ANY)
 MIB = 1 << 20
 FREE = pl.CostEstimate(flops=0, bytes_accessed=0, transcendentals=0)
-EARLY = pl.CostEstimate(flops=1 << 35, bytes_accessed=0, transcendentals=0)
 LONG = pl.CostEstimate(flops=1 << 35, bytes_accessed=0, transcendentals=0)
 
 
@@ -99,7 +98,7 @@
         out_specs=[VMEM] * (5 + len(offsets)),
         scratch_shapes=[pltpu.SMEM(send_count.shape, I32), pltpu.SemaphoreType.DMA((6,))],
         compiler_params=params(16),
-        cost_estimate=EARLY,
+        cost_estimate=FREE,
         name="pack",
     )(*hbm(*arrays))
 
@@ -151,7 +150,7 @@
 
 
 def local_kernel(block, feat_ref, send_ref, count_ref, tiles_ref, edge_ref, adj_ref, live_vmem, hub_ref, *refs):
-    sources, (out_ref, map_hbm, core_ref, *refs) = refs[:4], refs[4:]
+    sources, (out_ref, map_hbm, core_ref, mask_ref, *refs) = refs[:4], refs[4:]
     *tables, live_ref, local_map, edge_map, rhs_ref, sems = refs
     copies = start_all([*sources, live_vmem], [*tables, live_ref], sems)
     shard = hub_ref.shape[0]
@@ -180,7 +179,16 @@
             blocks.append(jnp.concatenate(line, axis=1))
         out_ref[span(m), :] = dot(jnp.concatenate(blocks, axis=0), feat_ref[...])
         fill_map(tables[2], tables[3], edge_map, m * share, share)
-        return 0
+        for i in range(block):
+            row = m * block + i
+            hit = jnp.sum(jnp.where(at_row == row, live_vmem[...], 0), axis=1, keepdims=True)
+            mask_ref[pl.ds(row, 1), :] = jnp.sum(jnp.where(inside & (hit > 0), 1.0, 0.0), axis=0, keepdims=True)
+        return 0
+
+    at_row = lax.broadcasted_iota(I32, live_vmem.shape, 1)
+    cells = (live_vmem.shape[0], adj_ref.shape[1])
+    lane, first = lax.broadcasted_iota(I32, cells, 1), lax.broadcasted_iota(I32, cells, 0) * size
+    inside = (lane >= first) & (lane < first + size)
 
     lax.fori_loop(0, steps, local_body, 0)
     fill_map(tables[2], tables[3], edge_map, steps * share, tables[2].shape[0] - steps * share)
@@ -214,9 +222,10 @@
             jax.ShapeDtypeStruct(features.shape, F32),
             jax.ShapeDtypeStruct((edge_cells,), I32),
             jax.ShapeDtypeStruct((slots, width), BF),
+            jax.ShapeDtypeStruct((rows // size, adj.shape[1]), F32),
         ],
         in_specs=[VMEM] * 8 + [HBM] * 4,
-        out_specs=[VMEM, ANY, VMEM],
+        out_specs=[VMEM, ANY, VMEM, VMEM],
         scratch_shapes=[pltpu.SMEM(x.shape, I32) for x in tables]
         + [pltpu.SMEM(hub_live.shape, I32), pltpu.SMEM((local_cells,), I32), pltpu.SMEM((edge_cells,), I32)]
         + [pltpu.VMEM((hub.shape[0] + slots, width), BF), pltpu.SemaphoreType.DMA((6,))],
@@ -255,13 +264,13 @@
     return jnp.concatenate(line, axis=1)
 
 
-def middle_kernel(block, hubs, pieces, map_ref, live_ref, adj_ref, edge_ref, acc_ref, *refs):
-    *array_refs, out_ref, mask_ref, edge_map, hub_rhs, rhs_ref, sem = refs
+def middle_kernel(block, hubs, pieces, map_ref, mask_ref, adj_ref, edge_ref, acc_ref, *refs):
+    *array_refs, out_ref, edge_map, hub_rhs, rhs_ref, sem = refs
     table = pltpu.make_async_copy(map_ref, edge_map, sem)
     table.start()
     me, loop = lax.axis_index("row"), lax.axis_index("loop")
     core = lax.rem(me, 2)
-    tiles, rows = live_ref.shape
+    rows = mask_ref.shape[0]
     size = adj_ref.shape[0] // rows
     cols = edge_map.shape[0] // rows
     shard, slots = hub_rhs.shape[0] // len(hubs), rhs_ref.shape[0] // len(pieces)
@@ -273,14 +282,6 @@
     for n in range(len(pieces)):
         rhs_ref[n * slots : (n + 1) * slots, :] = array_refs[len(hubs) + n][:slots, :]
     sources = [me ^ offset for offset in pieces]
-    lane = lax.broadcasted_iota(I32, (tiles, adj_ref.shape[1]), 1)
-    first = lax.broadcasted_iota(I32, (tiles, adj_ref.shape[1]), 0) * size
-    inside = (lane >= first) & (lane < first + size)
-    live = live_ref[...]
-    for row in range(rows):
-        hit = jnp.where(inside & (live[:, row : row + 1] > 0), 1.0, 0.0)
-        mask_ref[row : row + 1, :] = jnp.sum(hit, axis=0, keepdims=True)
-
     def span(m):
         return pl.ds(pl.multiple_of(m * block * size, block * size), block * size)
 
@@ -303,16 +304,13 @@
     lax.fori_loop(0, rows // block, edge_body, 0)
 
 
-def middle_term(hubs, pieces, slots, edge_map, hub_live, adj, edges, acc, arrays):
+def middle_term(hubs, pieces, slots, edge_map, mask, adj, edges, acc, arrays):
     shard, width = arrays[0].shape
     return pl.pallas_call(
         functools.partial(middle_kernel, 8, hubs, pieces),
-        out_shape=[
-            jax.ShapeDtypeStruct(acc.shape, F32),
-            jax.ShapeDtypeStruct((hub_live.shape[1], adj.shape[1]), F32),
-        ],
+        out_shape=jax.ShapeDtypeStruct(acc.shape, F32),
         in_specs=[ANY] + [VMEM] * (4 + len(arrays)),
-        out_specs=[VMEM] * 2,
+        out_specs=VMEM,
         scratch_shapes=[
             pltpu.SMEM(edge_map.shape, I32),
             pltpu.VMEM((len(hubs) * shard, width), BF),
@@ -322,7 +320,7 @@
         compiler_params=params(16),
         cost_estimate=FREE,
         name="middle",
-    )(edge_map, hub_live, adj, edges, acc, *arrays)
+    )(edge_map, mask, adj, edges, acc, *arrays)
 
 
 def last_kernel(block, pieces, hubs, map_ref, edge_ref, adj_ref, mask_ref, acc_ref, weight_ref, *refs):
@@ -437,7 +435,7 @@
     from_near = [swap(x, "row", c) for x, c in zip(packed, near_chips)]
     near = swap(hub, "loop", 1)
     far = [swap_by_core(hub, offset, offset + 1) for offset in range(2, ring, 2)]
-    acc, edge_map, to_core = local_term(
+    acc, edge_map, to_core, mask = local_term(
         feat,
         sends,
         counts,
@@ -454,8 +452,8 @@
     shared = swap(stack(rows, [to_core, *arrived, *far, near]), "row", 1)
     hubs = [(1, 1)] + [(2 * n + 2, 2 * n + 3) for n in range(len(far))]
     order = far_chips + near_chips
-    acc, mask = middle_term(
-        hubs, order, slots, edge_map, live, hub_adj, edge_tiles, acc, [near, *far, *arrived]
+    acc = middle_term(
+        hubs, order, slots, edge_map, mask, hub_adj, edge_tiles, acc, [near, *far, *arrived]
     )
     pieces = [(0, 0, 1)] + [(0, (1 + n) * slots, c ^ 1) for n, c in enumerate(order)]
     at = len(pieces) * slots

time: 24.6 us -> 24.2 us (0.984)
  Pallas kernels: 14.7 us -> 14.3 us
  transfers between devices with their start and end apart: 6 -> 6, of which waited for: 3 -> 3; matrix products, arithmetic and copies ran while one was open for 0% -> 0% of each run, Pallas kernels for 37% -> 36%
where the time goes in v7:
time: 24.2 us; the launch traced here: 24 us
  Pallas kernels  14.3 us (59%)
  starting transfers between devices  7.79 us (32%)
  waiting for transfers between devices  1.85 us (8%)
    pallas_call x1, Pallas kernels, local_term(): pl.pallas_call(functools.partial(local_kernel, 8), out_shape=[jax.ShapeDt...  5.22 us
    ppermute x5, starting transfers between devices, swap(): lax.ppermute(x, axis, [(i, i ^ offset) for i in range(lax.axis_size(axis))])  4.31 us
    ppermute x1, starting transfers between devices, swap_by_core(): return lax.ppermute(x, ('row', 'loop'), pairs)  3.48 us
    pallas_call x1, Pallas kernels, last_term(): pl.pallas_call(functools.partial(last_kernel, block, pieces, hubs), out_s...  3.43 us
    pallas_call x1, Pallas kernels, middle_term(): pl.pallas_call(functools.partial(middle_kernel, 8, hubs, pieces), out_sha...  2.14 us
    pallas_call x1, Pallas kernels, pack(): pl.pallas_call(functools.partial(pack_kernel, offsets), out_shape=[jax.Sh...  2.06 us
    ppermute x5, waiting for transfers between devices, swap(): lax.ppermute(x, axis, [(i, i ^ offset) for i in range(lax.axis_size(axis))])  1.85 us
    pallas_call x1, Pallas kernels, pack_more(): pl.pallas_call(functools.partial(more_kernel, offsets), out_shape=[jax.Sh...  1.39 us
  transfers between devices with their start and end apart: 6, of which 3 were waited for; matrix products, arithmetic and copies ran while one was open for 0% of the time, Pallas kernels for 36%

profile of v7, /device:TPU:1, one launch (start us, length us, event | category | flops | bytes accessed | tf_op | source)
XLA Modules:
  0.0 24.0 jit_solution(12556792142129934089)
XLA Ops:
  0.0 2.1 %pack.1 = (bf16[2048,256]{1,0:T(8,128)(2,1)S(1)}, s32[8,256]{1,0:T(8,128)S(1)}, s32[1,8]{1,0:T(1,128)S(1)}, bf16[256,256]{1,0:T(8,128)(2,1)S(1)}, s32[8,16]{1,0:T(8,128)S(1)}, /*index=5*/bf16[512,256]{1,0:T(8,128)(2,1)S(1)}) custom-call(bf16[2048,256]{1,0:T(8,128)(2,1)} %feat_hbm.1, s32[8,256]{1,0:T(8,128)} %bitcast.2, s32[1,8]{1,0:T(1,128)} %count_hbm.1, ...), custom_call_target="tpu_custom_call" | custom-call | tf_op jit(solution)/shard_map/pack/pallas_call | solution.py:93
  2.1 3.1 %collective-permute-start.2 = (bf16[512,256]{1,0:T(8,128)(2,1)S(1)}, bf16[512,256]{1,0:T(8,128)(2,1)S(1)}, u32[]{:S(2)}, u32[]{:S(2)}) collective-permute-start(bf16[512,256]{1,0:T(8,128)(2,1)S(1)} %get-tuple-element.25), channel_id=1, source_target_pairs={{0,24},{4,28},{8,16},{12,20},{16,8},{20,12},{24,0},{28,4},{1,25},{... | collective-permute-start | bytes 786440 | tf_op jit(solution)/shard_map/ppermute | solution.py:399
  5.1 0.0 copy-start
  5.1 0.0 copy-start.1
  5.1 0.0 copy-start.2
  5.1 1.4 %more.1 = (bf16[512,256]{1,0:T(8,128)(2,1)S(1)}, bf16[512,256]{1,0:T(8,128)(2,1)S(1)}) custom-call(bf16[2048,256]{1,0:T(8,128)(2,1)S(1)} %get-tuple-element.17.feat_ref, s32[8,256]{1,0:T(8,128)S(1)} %get-tuple-element.18.send_ref, s32[1,8]{1,0:T(1,128)S(1)} %get-tuple-element.19.count_ref), custom_call_target="tpu_custom_call" | custom-call | flops 34359738368 | tf_op jit(solution)/shard_map/more/pallas_call | solution.py:112
  6.5 0.3 %collective-permute-start.3 = (bf16[512,256]{1,0:T(8,128)(2,1)S(1)}, bf16[512,256]{1,0:T(8,128)(2,1)S(1)}, u32[]{:S(2)}, u32[]{:S(2)}) collective-permute-start(bf16[512,256]{1,0:T(8,128)(2,1)S(1)} %get-tuple-element.26), channel_id=1, source_target_pairs={{0,8},{4,12},{8,0},{12,4},{16,24},{20,28},{24,16},{28,20},{1,9},{5... | collective-permute-start | bytes 786440 | tf_op jit(solution)/shard_map/ppermute | solution.py:399
  6.9 0.1 collective-permute-start.4
  6.9 3.5 %collective-permute-start.1 = (bf16[256,256]{1,0:T(8,128)(2,1)S(1)}, bf16[256,256]{1,0:T(8,128)(2,1)S(1)}, u32[]{:S(2)}, u32[]{:S(2)}) collective-permute-start(bf16[256,256]{1,0:T(8,128)(2,1)S(1)} %get-tuple-element.21.hub_ref), channel_id=1, source_target_pairs={{0,2},{1,3},{2,0},{3,1},{4,7},{5,6},{6,5},{7,4},{8,10},{9,11},{10,... | collective-permute-start | bytes 393224 | tf_op jit(solution)/shard_map/ppermute | solution.py:405
  10.4 0.0 collective-permute-start
  10.4 0.0 copy-done
  10.4 0.0 copy-done.1
  10.4 0.0 copy-done.2
  10.4 5.2 %local.1 = (f32[2048,256]{1,0:T(8,128)S(1)}, s32[256]{0:T(256)S(1)}, bf16[256,256]{1,0:T(8,128)(2,1)S(1)}, f32[16,1024]{1,0:T(8,128)S(1)}) custom-call(bf16[2048,256]{1,0:T(8,128)(2,1)S(1)} %get-tuple-element.17.feat_ref, s32[8,256]{1,0:T(8,128)S(1)} %get-tuple-element.18.send_ref, s32[1,8]{1,0:T(1,128)S(1)} %get-tuple-element.19.count_ref, ...), custom_call_target="tpu_custom_call" | custom-call | tf_op jit(solution)/shard_map/local/pallas_call | solution.py:219
  15.7 0.0 collective-permute-done.1.refs_1_.refs_4_
  15.7 0.9 %collective-permute-done.refs_0_.refs_5_ = bf16[256,256]{1,0:T(8,128)(2,1)S(1)} collective-permute-done((bf16[256,256]{1,0:T(8,128)(2,1)S(1)}, bf16[256,256]{1,0:T(8,128)(2,1)S(1)}, u32[]{:S(2)}, u32[]{:S(2)}) %collective-permute-start) | collective-permute-done | bytes 131104 | tf_op jit(solution)/shard_map/ppermute | solution.py:399
  16.6 0.0 collective-permute-done.2.refs_2_.refs_1_
  16.6 0.2 collective-permute-done.3.refs_3_.refs_2_
  16.7 0.8 %collective-permute-done.4.refs_4_.refs_3_ = bf16[512,256]{1,0:T(8,128)(2,1)S(1)} collective-permute-done((bf16[512,256]{1,0:T(8,128)(2,1)S(1)}, bf16[512,256]{1,0:T(8,128)(2,1)S(1)}, u32[]{:S(2)}, u32[]{:S(2)}) %collective-permute-start.4) | collective-permute-done | bytes 262176 | tf_op jit(solution)/shard_map/ppermute | solution.py:399
  17.6 0.9 %collective-permute-start.5 = (bf16[1280,256]{1,0:T(8,128)(2,1)S(1)}, bf16[1280,256]{1,0:T(8,128)(2,1)S(1)}, u32[]{:S(2)}, u32[]{:S(2)}) collective-permute-start(bf16[1280,256]{1,0:T(8,128)(2,1)S(1)} %stack.1), channel_id=1, source_target_pairs={{0,4},{4,0},{8,12},{12,8},{16,20},{20,16},{24,28},{28,24},{1,5},{5... | collective-permute-start | bytes 1966088 | tf_op jit(solution)/shard_map/ppermute | solution.py:399
  18.4 2.1 %middle.1.acc_ref = f32[2048,256]{1,0:T(8,128)S(1)} custom-call(s32[256]{0:T(256)S(1)} %get-tuple-element.22.map_ref, f32[16,1024]{1,0:T(8,128)S(1)} %get-tuple-element.23.mask_ref, bf16[2048,1024]{1,0:T(8,128)(2,1)S(1)} %copy-done.1, bf16[144,128,128]{2,1,0:T(8,128)(2,1)S(1)} %copy-done, f32[2048,256]{1,0:T(8,128)S(1)} %get-tuple-element.24.acc_ref, ...), custom_call_target="tpu_custom_call" | custom-call | tf_op jit(solution)/shard_map/middle/pallas_call | solution.py:309
  20.6 0.0 collective-permute-done.5.refs_0_
  20.6 0.0 copy-done.3
  20.6 3.4 %last.1 = bf16[2048,256]{1,0:T(8,128)(2,1)} custom-call(s32[256]{0:T(256)S(1)} %get-tuple-element.22.map_ref, bf16[144,128,128]{2,1,0:T(8,128)(2,1)S(1)} %copy-done, bf16[2048,1024]{1,0:T(8,128)(2,1)S(1)} %copy-done.1, f32[16,1024]{1,0:T(8,128)S(1)} %get-tuple-element.23.mask_ref, f32[2048,256]{1,0:T(8,128)S(1)} %middle.1.acc_ref, ...), custom_call_target="tpu_custom_call" | custom-call | tf_op jit(solution)/shard_map/last/pallas_call | solution.py:379
  (2 shorter events, 0.0 us)
Async XLA Ops:
  2.1 14.5 %collective-permute-start.2 = (bf16[512,256]{1,0:T(8,128)(2,1)S(1)}, bf16[512,256]{1,0:T(8,128)(2,1)S(1)}, u32[]{:S(2)}, u32[]{:S(2)}) collective-permute-start(bf16[512,256]{1,0:T(8,128)(2,1)S(1)} %get-tuple-element.25), channel_id=1, source_target_pairs={{0,24},{4,28},{8,16},{12,20},{16,8},{20,12},{24,0},{28,4},{1,25},{... | collective-permute-start | bytes 786440 | tf_op jit(solution)/shard_map/ppermute | solution.py:399
  5.1 5.3 %copy-start = (bf16[144,128,128]{2,1,0:T(8,128)(2,1)S(1)}, bf16[144,128,128]{2,1,0:T(8,128)(2,1)}, u32[]{:S(2)}) copy-start(bf16[144,128,128]{2,1,0:T(8,128)(2,1)} %edge_ref.5) | copy-start | bytes 14155780
  5.1 5.3 %copy-start.1 = (bf16[2048,1024]{1,0:T(8,128)(2,1)S(1)}, bf16[2048,1024]{1,0:T(8,128)(2,1)}, u32[]{:S(2)}) copy-start(bf16[2048,1024]{1,0:T(8,128)(2,1)} %adj_ref.5) | copy-start | bytes 12582916
  5.1 5.3 %copy-start.2 = (bf16[128,128,128]{2,1,0:T(8,128)(2,1)S(1)}, bf16[128,128,128]{2,1,0:T(8,128)(2,1)}, u32[]{:S(2)}) copy-start(bf16[128,128,128]{2,1,0:T(8,128)(2,1)} %tiles_ref.1) | copy-start | bytes 12582916
  6.5 10.2 %collective-permute-start.3 = (bf16[512,256]{1,0:T(8,128)(2,1)S(1)}, bf16[512,256]{1,0:T(8,128)(2,1)S(1)}, u32[]{:S(2)}, u32[]{:S(2)}) collective-permute-start(bf16[512,256]{1,0:T(8,128)(2,1)S(1)} %get-tuple-element.26), channel_id=1, source_target_pairs={{0,8},{4,12},{8,0},{12,4},{16,24},{20,28},{24,16},{28,20},{1,9},{5... | collective-permute-start | bytes 786440 | tf_op jit(solution)/shard_map/ppermute | solution.py:399
  6.9 10.7 %collective-permute-start.4 = (bf16[512,256]{1,0:T(8,128)(2,1)S(1)}, bf16[512,256]{1,0:T(8,128)(2,1)S(1)}, u32[]{:S(2)}, u32[]{:S(2)}) collective-permute-start(bf16[512,256]{1,0:T(8,128)(2,1)S(1)} %get-tuple-element.27), channel_id=1, source_target_pairs={{0,16},{4,20},{8,24},{12,28},{16,0},{20,4},{24,8},{28,12},{1,17},{... | collective-permute-start | bytes 786440 | tf_op jit(solution)/shard_map/ppermute | solution.py:399
  6.9 8.7 %collective-permute-start.1 = (bf16[256,256]{1,0:T(8,128)(2,1)S(1)}, bf16[256,256]{1,0:T(8,128)(2,1)S(1)}, u32[]{:S(2)}, u32[]{:S(2)}) collective-permute-start(bf16[256,256]{1,0:T(8,128)(2,1)S(1)} %get-tuple-element.21.hub_ref), channel_id=1, source_target_pairs={{0,2},{1,3},{2,0},{3,1},{4,7},{5,6},{6,5},{7,4},{8,10},{9,11},{10,... | collective-permute-start | bytes 393224 | tf_op jit(solution)/shard_map/ppermute | solution.py:405
  10.4 6.2 %collective-permute-start = (bf16[256,256]{1,0:T(8,128)(2,1)S(1)}, bf16[256,256]{1,0:T(8,128)(2,1)S(1)}, u32[]{:S(2)}, u32[]{:S(2)}) collective-permute-start(bf16[256,256]{1,0:T(8,128)(2,1)S(1)} %get-tuple-element.21.hub_ref), channel_id=1, source_target_pairs={{0,1},{1,0},{2,3},{3,2},{4,5},{5,4},{6,7},{7,6},{8,9},{9,8},{10,11... | collective-permute-start | bytes 393224 | tf_op jit(solution)/shard_map/ppermute | solution.py:399
  17.6 3.0 %collective-permute-start.5 = (bf16[1280,256]{1,0:T(8,128)(2,1)S(1)}, bf16[1280,256]{1,0:T(8,128)(2,1)S(1)}, u32[]{:S(2)}, u32[]{:S(2)}) collective-permute-start(bf16[1280,256]{1,0:T(8,128)(2,1)S(1)} %stack.1), channel_id=1, source_target_pairs={{0,4},{4,0},{8,12},{12,8},{16,20},{20,16},{24,28},{28,24},{1,5},{5... | collective-permute-start | bytes 1966088 | tf_op jit(solution)/shard_map/ppermute | solution.py:399
  18.4 2.2 %copy-start.3 = (bf16[256,256]{1,0:T(8,128)(2,1)S(1)}, bf16[256,256]{1,0:T(8,128)(2,1)}, u32[]{:S(2)}) copy-start(bf16[256,256]{1,0:T(8,128)(2,1)} %weight_ref.1) | copy-start | bytes 393220

commit v8 on v7

--- a/solution.py
+++ b/solution.py
@@ -17,13 +17,6 @@
 ANY = pl.BlockSpec(memory_space=pl.ANY)
 MIB = 1 << 20
 FREE = pl.CostEstimate(flops=0, bytes_accessed=0, transcendentals=0)
-VMEM = pl.BlockSpec(memory_space=pltpu.VMEM)
-SMEM = pl.BlockSpec(memory_space=pltpu.SMEM)
-HBM = pl.BlockSpec(memory_space=pltpu.HBM)
-ANY = pl.BlockSpec(memory_space=pl.ANY)
-MIB = 1 << 20
-FREE = pl.CostEstimate(flops=0, bytes_accessed=0, transcendentals=0)
-LONG = pl.CostEstimate(flops=1 << 35, bytes_accessed=0, transcendentals=0)
 
 
 def params(mib):
@@ -293,15 +286,9 @@
     lax.fori_loop(0, rows // block, hub_body, 0)
     table.wait()
 
-    def edge_body(m, _):
-        lines = [
-            edge_line(edge_ref, edge_map, m * block + i, cols, sources, slots // size) for i in range(block)
-        ]
-        found = jnp.concatenate([jnp.concatenate(line, axis=1) for line in lines], axis=0)
-        out_ref[span(m), :] += dot(found, rhs_ref[...])
-        return 0
-
-    lax.fori_loop(0, rows // block, edge_body, 0)
+    lines = [edge_line(edge_ref, edge_map, row, cols, sources, slots // size) for row in range(rows)]
+    found = jnp.concatenate([jnp.concatenate(line, axis=1) for line in lines], axis=0)
+    out_ref[...] += dot(found, rhs_ref[...])
 
 
 def middle_term(hubs, pieces, slots, edge_map, mask, adj, edges, acc, arrays):
@@ -358,17 +345,12 @@
     lax.fori_loop(0, steps, hub_body, 0)
     table.wait()
 
-    def body(m, _):
-        lines = [
-            edge_line(edge_ref, edge_map, m * block + i, cols, sources, slots // size) for i in range(block)
-        ]
-        tiles = jnp.concatenate([jnp.concatenate(line, axis=1) for line in lines], axis=0)
-        total = total_ref[span(m), :] + dot(tiles, rhs_ref[...])
-        stage_ref[span(m), :] = jnp.maximum(dot(total.astype(BF), weight_ref[...]), 0.0).astype(BF)
+    lines = [edge_line(edge_ref, edge_map, row, cols, sources, slots // size) for row in range(rows // size)]
+    tiles = jnp.concatenate([jnp.concatenate(line, axis=1) for line in lines], axis=0)
+    total_ref[...] += dot(tiles, rhs_ref[...])
+    for m in range(steps):
+        stage_ref[span(m), :] = jnp.maximum(dot(total_ref[span(m), :].astype(BF), weight_ref[...]), 0.0).astype(BF)
         write(m).start()
-        return 0
-
-    lax.fori_loop(0, steps, body, 0)
     for m in range(steps):
         write(m).wait()
 

time: 24.2 us -> 23.8 us (0.983)
  Pallas kernels: 14.3 us -> 13.9 us
  transfers between devices with their start and end apart: 6 -> 6, of which waited for: 3 -> 3; matrix products, arithmetic and copies ran while one was open for 0% -> 0% of each run, Pallas kernels for 36% -> 37%
where the time goes in v8:
time: 23.8 us; the launch traced here: 23.6 us
  Pallas kernels  13.9 us (58%)
  starting transfers between devices  7.79 us (33%)
  waiting for transfers between devices  1.85 us (8%)
    pallas_call x1, Pallas kernels, local_term(): pl.pallas_call(functools.partial(local_kernel, 8), out_shape=[jax.ShapeDt...  5.22 us
    ppermute x5, starting transfers between devices, swap(): lax.ppermute(x, axis, [(i, i ^ offset) for i in range(lax.axis_size(axis))])  4.31 us
    ppermute x1, starting transfers between devices, swap_by_core(): return lax.ppermute(x, ('row', 'loop'), pairs)  3.48 us
    pallas_call x1, Pallas kernels, last_term(): pl.pallas_call(functools.partial(last_kernel, block, pieces, hubs), out_s...  3.19 us
    pallas_call x1, Pallas kernels, pack(): pl.pallas_call(functools.partial(pack_kernel, offsets), out_shape=[jax.Sh...  2.06 us
    pallas_call x1, Pallas kernels, middle_term(): pl.pallas_call(functools.partial(middle_kernel, 8, hubs, pieces), out_sha...  2.01 us
    ppermute x5, waiting for transfers between devices, swap(): lax.ppermute(x, axis, [(i, i ^ offset) for i in range(lax.axis_size(axis))])  1.85 us
    pallas_call x1, Pallas kernels, pack_more(): pl.pallas_call(functools.partial(more_kernel, offsets), out_shape=[jax.Sh...  1.39 us
  transfers between devices with their start and end apart: 6, of which 3 were waited for; matrix products, arithmetic and copies ran while one was open for 0% of the time, Pallas kernels for 37%

profile of v8, /device:TPU:1, one launch (start us, length us, event | category | flops | bytes accessed | tf_op | source)
XLA Modules:
  0.0 23.6 jit_solution(5380339080432132135)
XLA Ops:
  0.0 2.1 %pack.1 = (bf16[2048,256]{1,0:T(8,128)(2,1)S(1)}, s32[8,256]{1,0:T(8,128)S(1)}, s32[1,8]{1,0:T(1,128)S(1)}, bf16[256,256]{1,0:T(8,128)(2,1)S(1)}, s32[8,16]{1,0:T(8,128)S(1)}, /*index=5*/bf16[512,256]{1,0:T(8,128)(2,1)S(1)}) custom-call(bf16[2048,256]{1,0:T(8,128)(2,1)} %feat_hbm.1, s32[8,256]{1,0:T(8,128)} %bitcast.2, s32[1,8]{1,0:T(1,128)} %count_hbm.1, ...), custom_call_target="tpu_custom_call" | custom-call | tf_op jit(solution)/shard_map/pack/pallas_call | solution.py:86
  2.1 3.1 %collective-permute-start.2 = (bf16[512,256]{1,0:T(8,128)(2,1)S(1)}, bf16[512,256]{1,0:T(8,128)(2,1)S(1)}, u32[]{:S(2)}, u32[]{:S(2)}) collective-permute-start(bf16[512,256]{1,0:T(8,128)(2,1)S(1)} %get-tuple-element.25), channel_id=1, source_target_pairs={{0,24},{4,28},{8,16},{12,20},{16,8},{20,12},{24,0},{28,4},{1,25},{... | collective-permute-start | bytes 786440 | tf_op jit(solution)/shard_map/ppermute | solution.py:381
  5.1 0.0 copy-start
  5.1 0.0 copy-start.1
  5.1 0.0 copy-start.2
  5.1 1.4 %more.1 = (bf16[512,256]{1,0:T(8,128)(2,1)S(1)}, bf16[512,256]{1,0:T(8,128)(2,1)S(1)}) custom-call(bf16[2048,256]{1,0:T(8,128)(2,1)S(1)} %get-tuple-element.17.feat_ref, s32[8,256]{1,0:T(8,128)S(1)} %get-tuple-element.18.send_ref, s32[1,8]{1,0:T(1,128)S(1)} %get-tuple-element.19.count_ref), custom_call_target="tpu_custom_call" | custom-call | flops 34359738368 | tf_op jit(solution)/shard_map/more/pallas_call | solution.py:105
  6.5 0.3 %collective-permute-start.3 = (bf16[512,256]{1,0:T(8,128)(2,1)S(1)}, bf16[512,256]{1,0:T(8,128)(2,1)S(1)}, u32[]{:S(2)}, u32[]{:S(2)}) collective-permute-start(bf16[512,256]{1,0:T(8,128)(2,1)S(1)} %get-tuple-element.26), channel_id=1, source_target_pairs={{0,8},{4,12},{8,0},{12,4},{16,24},{20,28},{24,16},{28,20},{1,9},{5... | collective-permute-start | bytes 786440 | tf_op jit(solution)/shard_map/ppermute | solution.py:381
  6.9 0.1 collective-permute-start.4
  6.9 3.5 %collective-permute-start.1 = (bf16[256,256]{1,0:T(8,128)(2,1)S(1)}, bf16[256,256]{1,0:T(8,128)(2,1)S(1)}, u32[]{:S(2)}, u32[]{:S(2)}) collective-permute-start(bf16[256,256]{1,0:T(8,128)(2,1)S(1)} %get-tuple-element.21.hub_ref), channel_id=1, source_target_pairs={{0,2},{1,3},{2,0},{3,1},{4,7},{5,6},{6,5},{7,4},{8,10},{9,11},{10,... | collective-permute-start | bytes 393224 | tf_op jit(solution)/shard_map/ppermute | solution.py:387
  10.4 0.0 collective-permute-start
  10.4 0.0 copy-done
  10.4 0.0 copy-done.1
  10.4 0.0 copy-done.2
  10.4 5.2 %local.1 = (f32[2048,256]{1,0:T(8,128)S(1)}, s32[256]{0:T(256)S(1)}, bf16[256,256]{1,0:T(8,128)(2,1)S(1)}, f32[16,1024]{1,0:T(8,128)S(1)}) custom-call(bf16[2048,256]{1,0:T(8,128)(2,1)S(1)} %get-tuple-element.17.feat_ref, s32[8,256]{1,0:T(8,128)S(1)} %get-tuple-element.18.send_ref, s32[1,8]{1,0:T(1,128)S(1)} %get-tuple-element.19.count_ref, ...), custom_call_target="tpu_custom_call" | custom-call | tf_op jit(solution)/shard_map/local/pallas_call | solution.py:212
  15.7 0.0 collective-permute-done.1.refs_1_.refs_4_
  15.7 0.9 %collective-permute-done.refs_0_.refs_5_ = bf16[256,256]{1,0:T(8,128)(2,1)S(1)} collective-permute-done((bf16[256,256]{1,0:T(8,128)(2,1)S(1)}, bf16[256,256]{1,0:T(8,128)(2,1)S(1)}, u32[]{:S(2)}, u32[]{:S(2)}) %collective-permute-start) | collective-permute-done | bytes 131104 | tf_op jit(solution)/shard_map/ppermute | solution.py:381
  16.6 0.0 collective-permute-done.2.refs_2_.refs_1_
  16.6 0.2 collective-permute-done.3.refs_3_.refs_2_
  16.7 0.8 %collective-permute-done.4.refs_4_.refs_3_ = bf16[512,256]{1,0:T(8,128)(2,1)S(1)} collective-permute-done((bf16[512,256]{1,0:T(8,128)(2,1)S(1)}, bf16[512,256]{1,0:T(8,128)(2,1)S(1)}, u32[]{:S(2)}, u32[]{:S(2)}) %collective-permute-start.4) | collective-permute-done | bytes 262176 | tf_op jit(solution)/shard_map/ppermute | solution.py:381
  17.6 0.9 %collective-permute-start.5 = (bf16[1280,256]{1,0:T(8,128)(2,1)S(1)}, bf16[1280,256]{1,0:T(8,128)(2,1)S(1)}, u32[]{:S(2)}, u32[]{:S(2)}) collective-permute-start(bf16[1280,256]{1,0:T(8,128)(2,1)S(1)} %stack.1), channel_id=1, source_target_pairs={{0,4},{4,0},{8,12},{12,8},{16,20},{20,16},{24,28},{28,24},{1,5},{5... | collective-permute-start | bytes 1966088 | tf_op jit(solution)/shard_map/ppermute | solution.py:381
  18.4 2.0 %middle.1.acc_ref = f32[2048,256]{1,0:T(8,128)S(1)} custom-call(s32[256]{0:T(256)S(1)} %get-tuple-element.22.map_ref, f32[16,1024]{1,0:T(8,128)S(1)} %get-tuple-element.23.mask_ref, bf16[2048,1024]{1,0:T(8,128)(2,1)S(1)} %copy-done.1, bf16[144,128,128]{2,1,0:T(8,128)(2,1)S(1)} %copy-done, f32[2048,256]{1,0:T(8,128)S(1)} %get-tuple-element.24.acc_ref, ...), custom_call_target="tpu_custom_call" | custom-call | tf_op jit(solution)/shard_map/middle/pallas_call | solution.py:296
  20.4 0.0 collective-permute-done.5.refs_0_
  20.4 0.0 copy-done.3
  20.5 3.2 %last.1 = bf16[2048,256]{1,0:T(8,128)(2,1)} custom-call(s32[256]{0:T(256)S(1)} %get-tuple-element.22.map_ref, bf16[144,128,128]{2,1,0:T(8,128)(2,1)S(1)} %copy-done, bf16[2048,1024]{1,0:T(8,128)(2,1)S(1)} %copy-done.1, f32[16,1024]{1,0:T(8,128)S(1)} %get-tuple-element.23.mask_ref, f32[2048,256]{1,0:T(8,128)S(1)} %middle.1.acc_ref, ...), custom_call_target="tpu_custom_call" | custom-call | tf_op jit(solution)/shard_map/last/pallas_call | solution.py:361
  (2 shorter events, 0.0 us)
Async XLA Ops:
  2.1 14.5 %collective-permute-start.2 = (bf16[512,256]{1,0:T(8,128)(2,1)S(1)}, bf16[512,256]{1,0:T(8,128)(2,1)S(1)}, u32[]{:S(2)}, u32[]{:S(2)}) collective-permute-start(bf16[512,256]{1,0:T(8,128)(2,1)S(1)} %get-tuple-element.25), channel_id=1, source_target_pairs={{0,24},{4,28},{8,16},{12,20},{16,8},{20,12},{24,0},{28,4},{1,25},{... | collective-permute-start | bytes 786440 | tf_op jit(solution)/shard_map/ppermute | solution.py:381
  5.1 5.3 %copy-start = (bf16[144,128,128]{2,1,0:T(8,128)(2,1)S(1)}, bf16[144,128,128]{2,1,0:T(8,128)(2,1)}, u32[]{:S(2)}) copy-start(bf16[144,128,128]{2,1,0:T(8,128)(2,1)} %edge_ref.5) | copy-start | bytes 14155780
  5.1 5.3 %copy-start.1 = (bf16[2048,1024]{1,0:T(8,128)(2,1)S(1)}, bf16[2048,1024]{1,0:T(8,128)(2,1)}, u32[]{:S(2)}) copy-start(bf16[2048,1024]{1,0:T(8,128)(2,1)} %adj_ref.5) | copy-start | bytes 12582916
  5.1 5.3 %copy-start.2 = (bf16[128,128,128]{2,1,0:T(8,128)(2,1)S(1)}, bf16[128,128,128]{2,1,0:T(8,128)(2,1)}, u32[]{:S(2)}) copy-start(bf16[128,128,128]{2,1,0:T(8,128)(2,1)} %tiles_ref.1) | copy-start | bytes 12582916
  6.5 10.2 %collective-permute-start.3 = (bf16[512,256]{1,0:T(8,128)(2,1)S(1)}, bf16[512,256]{1,0:T(8,128)(2,1)S(1)}, u32[]{:S(2)}, u32[]{:S(2)}) collective-permute-start(bf16[512,256]{1,0:T(8,128)(2,1)S(1)} %get-tuple-element.26), channel_id=1, source_target_pairs={{0,8},{4,12},{8,0},{12,4},{16,24},{20,28},{24,16},{28,20},{1,9},{5... | collective-permute-start | bytes 786440 | tf_op jit(solution)/shard_map/ppermute | solution.py:381
  6.9 10.7 %collective-permute-start.4 = (bf16[512,256]{1,0:T(8,128)(2,1)S(1)}, bf16[512,256]{1,0:T(8,128)(2,1)S(1)}, u32[]{:S(2)}, u32[]{:S(2)}) collective-permute-start(bf16[512,256]{1,0:T(8,128)(2,1)S(1)} %get-tuple-element.27), channel_id=1, source_target_pairs={{0,16},{4,20},{8,24},{12,28},{16,0},{20,4},{24,8},{28,12},{1,17},{... | collective-permute-start | bytes 786440 | tf_op jit(solution)/shard_map/ppermute | solution.py:381
  6.9 8.7 %collective-permute-start.1 = (bf16[256,256]{1,0:T(8,128)(2,1)S(1)}, bf16[256,256]{1,0:T(8,128)(2,1)S(1)}, u32[]{:S(2)}, u32[]{:S(2)}) collective-permute-start(bf16[256,256]{1,0:T(8,128)(2,1)S(1)} %get-tuple-element.21.hub_ref), channel_id=1, source_target_pairs={{0,2},{1,3},{2,0},{3,1},{4,7},{5,6},{6,5},{7,4},{8,10},{9,11},{10,... | collective-permute-start | bytes 393224 | tf_op jit(solution)/shard_map/ppermute | solution.py:387
  10.4 6.2 %collective-permute-start = (bf16[256,256]{1,0:T(8,128)(2,1)S(1)}, bf16[256,256]{1,0:T(8,128)(2,1)S(1)}, u32[]{:S(2)}, u32[]{:S(2)}) collective-permute-start(bf16[256,256]{1,0:T(8,128)(2,1)S(1)} %get-tuple-element.21.hub_ref), channel_id=1, source_target_pairs={{0,1},{1,0},{2,3},{3,2},{4,5},{5,4},{6,7},{7,6},{8,9},{9,8},{10,11... | collective-permute-start | bytes 393224 | tf_op jit(solution)/shard_map/ppermute | solution.py:381
  17.6 2.9 %collective-permute-start.5 = (bf16[1280,256]{1,0:T(8,128)(2,1)S(1)}, bf16[1280,256]{1,0:T(8,128)(2,1)S(1)}, u32[]{:S(2)}, u32[]{:S(2)}) collective-permute-start(bf16[1280,256]{1,0:T(8,128)(2,1)S(1)} %stack.1), channel_id=1, source_target_pairs={{0,4},{4,0},{8,12},{12,8},{16,20},{20,16},{24,28},{28,24},{1,5},{5... | collective-permute-start | bytes 1966088 | tf_op jit(solution)/shard_map/ppermute | solution.py:381
  18.4 2.0 %copy-start.3 = (bf16[256,256]{1,0:T(8,128)(2,1)S(1)}, bf16[256,256]{1,0:T(8,128)(2,1)}, u32[]{:S(2)}) copy-start(bf16[256,256]{1,0:T(8,128)(2,1)} %weight_ref.1) | copy-start | bytes 393220

commit v9 on v8

--- a/solution.py
+++ b/solution.py
@@ -315,7 +315,7 @@
     size = edge_ref.shape[1]
     rows = acc_ref.shape[0]
     steps = rows // (block * size)
-    table = pltpu.make_async_copy(map_ref, edge_map, sems.at[steps])
+    table = pltpu.make_async_copy(map_ref, edge_map, sems.at[steps + 1])
     table.start()
     me, loop = lax.axis_index("row"), lax.axis_index("loop")
     core = lax.rem(me, 2)
@@ -334,9 +334,6 @@
     def span(m):
         return pl.ds(pl.multiple_of(m * block * size, block * size), block * size)
 
-    def write(m):
-        return pltpu.make_async_copy(stage_ref.at[span(m)], out_ref.at[span(m)], sems.at[m])
-
     def hub_body(m, _):
         blocks = [masked_line(adj_ref, mask_ref, m * block + i, size, columns) for i in range(block)]
         total_ref[span(m), :] = acc_ref[span(m), :] + dot(jnp.concatenate(blocks, axis=0), hub_ref[...])
@@ -348,11 +345,13 @@
     lines = [edge_line(edge_ref, edge_map, row, cols, sources, slots // size) for row in range(rows // size)]
     tiles = jnp.concatenate([jnp.concatenate(line, axis=1) for line in lines], axis=0)
     total_ref[...] += dot(tiles, rhs_ref[...])
-    for m in range(steps):
-        stage_ref[span(m), :] = jnp.maximum(dot(total_ref[span(m), :].astype(BF), weight_ref[...]), 0.0).astype(BF)
-        write(m).start()
-    for m in range(steps):
-        write(m).wait()
+    copies = []
+    for n, (start, stop) in enumerate([(0, rows // 2), (rows // 2, 3 * rows // 4), (3 * rows // 4, rows)]):
+        part = pl.ds(start, stop - start)
+        stage_ref[part, :] = jnp.maximum(dot(total_ref[part, :].astype(BF), weight_ref[...]), 0.0).astype(BF)
+        copies.append(pltpu.make_async_copy(stage_ref.at[part], out_ref.at[part], sems.at[n]))
+        copies[n].start()
+    wait_all(copies)
 
 
 def last_term(pieces, hubs, slots, shard, edge_map, edges, adj, mask, acc, weight, arrays):
@@ -369,7 +368,7 @@
             pltpu.VMEM((len(pieces) * slots, width), BF),
             pltpu.VMEM(acc.shape, F32),
             pltpu.VMEM(acc.shape, BF),
-            pltpu.SemaphoreType.DMA((rows // (block * edges.shape[1]) + 1,)),
+            pltpu.SemaphoreType.DMA((rows // (block * edges.shape[1]) + 2,)),
         ],
         compiler_params=params(16),
         cost_estimate=FREE,

time: 23.8 us -> 23.7 us (level)
  no operation moved by 1% of the time
where the time goes in v9:
time: 23.7 us; the launch traced here: 23.6 us
  Pallas kernels  13.8 us (58%)
  starting transfers between devices  7.79 us (33%)
  waiting for transfers between devices  1.85 us (8%)
    pallas_call x1, Pallas kernels, local_term(): pl.pallas_call(functools.partial(local_kernel, 8), out_shape=[jax.ShapeDt...  5.22 us
    ppermute x5, starting transfers between devices, swap(): lax.ppermute(x, axis, [(i, i ^ offset) for i in range(lax.axis_size(axis))])  4.31 us
    ppermute x1, starting transfers between devices, swap_by_core(): return lax.ppermute(x, ('row', 'loop'), pairs)  3.48 us
    pallas_call x1, Pallas kernels, last_term(): pl.pallas_call(functools.partial(last_kernel, block, pieces, hubs), out_s...  3.12 us
    pallas_call x1, Pallas kernels, pack(): pl.pallas_call(functools.partial(pack_kernel, offsets), out_shape=[jax.Sh...  2.06 us
    pallas_call x1, Pallas kernels, middle_term(): pl.pallas_call(functools.partial(middle_kernel, 8, hubs, pieces), out_sha...  2.01 us
    ppermute x5, waiting for transfers between devices, swap(): lax.ppermute(x, axis, [(i, i ^ offset) for i in range(lax.axis_size(axis))])  1.85 us
    pallas_call x1, Pallas kernels, pack_more(): pl.pallas_call(functools.partial(more_kernel, offsets), out_shape=[jax.Sh...  1.39 us
  transfers between devices with their start and end apart: 6, of which 3 were waited for; matrix products, arithmetic and copies ran while one was open for 0% of the time, Pallas kernels for 37%

profile of v9, /device:TPU:1, one launch (start us, length us, event | category | flops | bytes accessed | tf_op | source)
XLA Modules:
  0.0 23.6 jit_solution(1104556827194933782)
XLA Ops:
  0.0 2.1 %pack.1 = (bf16[2048,256]{1,0:T(8,128)(2,1)S(1)}, s32[8,256]{1,0:T(8,128)S(1)}, s32[1,8]{1,0:T(1,128)S(1)}, bf16[256,256]{1,0:T(8,128)(2,1)S(1)}, s32[8,16]{1,0:T(8,128)S(1)}, /*index=5*/bf16[512,256]{1,0:T(8,128)(2,1)S(1)}) custom-call(bf16[2048,256]{1,0:T(8,128)(2,1)} %feat_hbm.1, s32[8,256]{1,0:T(8,128)} %bitcast.2, s32[1,8]{1,0:T(1,128)} %count_hbm.1, ...), custom_call_target="tpu_custom_call" | custom-call | tf_op jit(solution)/shard_map/pack/pallas_call | solution.py:86
  2.1 3.1 %collective-permute-start.2 = (bf16[512,256]{1,0:T(8,128)(2,1)S(1)}, bf16[512,256]{1,0:T(8,128)(2,1)S(1)}, u32[]{:S(2)}, u32[]{:S(2)}) collective-permute-start(bf16[512,256]{1,0:T(8,128)(2,1)S(1)} %get-tuple-element.25), channel_id=1, source_target_pairs={{0,24},{4,28},{8,16},{12,20},{16,8},{20,12},{24,0},{28,4},{1,25},{... | collective-permute-start | bytes 786440 | tf_op jit(solution)/shard_map/ppermute | solution.py:380
  5.1 0.0 copy-start
  5.1 0.0 copy-start.1
  5.1 0.0 copy-start.2
  5.1 1.4 %more.1 = (bf16[512,256]{1,0:T(8,128)(2,1)S(1)}, bf16[512,256]{1,0:T(8,128)(2,1)S(1)}) custom-call(bf16[2048,256]{1,0:T(8,128)(2,1)S(1)} %get-tuple-element.17.feat_ref, s32[8,256]{1,0:T(8,128)S(1)} %get-tuple-element.18.send_ref, s32[1,8]{1,0:T(1,128)S(1)} %get-tuple-element.19.count_ref), custom_call_target="tpu_custom_call" | custom-call | flops 34359738368 | tf_op jit(solution)/shard_map/more/pallas_call | solution.py:105
  6.5 0.3 %collective-permute-start.3 = (bf16[512,256]{1,0:T(8,128)(2,1)S(1)}, bf16[512,256]{1,0:T(8,128)(2,1)S(1)}, u32[]{:S(2)}, u32[]{:S(2)}) collective-permute-start(bf16[512,256]{1,0:T(8,128)(2,1)S(1)} %get-tuple-element.26), channel_id=1, source_target_pairs={{0,8},{4,12},{8,0},{12,4},{16,24},{20,28},{24,16},{28,20},{1,9},{5... | collective-permute-start | bytes 786440 | tf_op jit(solution)/shard_map/ppermute | solution.py:380
  6.9 0.1 collective-permute-start.4
  6.9 3.5 %collective-permute-start.1 = (bf16[256,256]{1,0:T(8,128)(2,1)S(1)}, bf16[256,256]{1,0:T(8,128)(2,1)S(1)}, u32[]{:S(2)}, u32[]{:S(2)}) collective-permute-start(bf16[256,256]{1,0:T(8,128)(2,1)S(1)} %get-tuple-element.21.hub_ref), channel_id=1, source_target_pairs={{0,2},{1,3},{2,0},{3,1},{4,7},{5,6},{6,5},{7,4},{8,10},{9,11},{10,... | collective-permute-start | bytes 393224 | tf_op jit(solution)/shard_map/ppermute | solution.py:386
  10.4 0.0 collective-permute-start
  10.4 0.0 copy-done
  10.4 0.0 copy-done.1
  10.4 0.0 copy-done.2
  10.4 5.2 %local.1 = (f32[2048,256]{1,0:T(8,128)S(1)}, s32[256]{0:T(256)S(1)}, bf16[256,256]{1,0:T(8,128)(2,1)S(1)}, f32[16,1024]{1,0:T(8,128)S(1)}) custom-call(bf16[2048,256]{1,0:T(8,128)(2,1)S(1)} %get-tuple-element.17.feat_ref, s32[8,256]{1,0:T(8,128)S(1)} %get-tuple-element.18.send_ref, s32[1,8]{1,0:T(1,128)S(1)} %get-tuple-element.19.count_ref, ...), custom_call_target="tpu_custom_call" | custom-call | tf_op jit(solution)/shard_map/local/pallas_call | solution.py:212
  15.7 0.0 collective-permute-done.1.refs_1_.refs_4_
  15.7 0.9 %collective-permute-done.refs_0_.refs_5_ = bf16[256,256]{1,0:T(8,128)(2,1)S(1)} collective-permute-done((bf16[256,256]{1,0:T(8,128)(2,1)S(1)}, bf16[256,256]{1,0:T(8,128)(2,1)S(1)}, u32[]{:S(2)}, u32[]{:S(2)}) %collective-permute-start) | collective-permute-done | bytes 131104 | tf_op jit(solution)/shard_map/ppermute | solution.py:380
  16.6 0.0 collective-permute-done.2.refs_2_.refs_1_
  16.6 0.2 collective-permute-done.3.refs_3_.refs_2_
  16.7 0.8 %collective-permute-done.4.refs_4_.refs_3_ = bf16[512,256]{1,0:T(8,128)(2,1)S(1)} collective-permute-done((bf16[512,256]{1,0:T(8,128)(2,1)S(1)}, bf16[512,256]{1,0:T(8,128)(2,1)S(1)}, u32[]{:S(2)}, u32[]{:S(2)}) %collective-permute-start.4) | collective-permute-done | bytes 262176 | tf_op jit(solution)/shard_map/ppermute | solution.py:380
  17.6 0.9 %collective-permute-start.5 = (bf16[1280,256]{1,0:T(8,128)(2,1)S(1)}, bf16[1280,256]{1,0:T(8,128)(2,1)S(1)}, u32[]{:S(2)}, u32[]{:S(2)}) collective-permute-start(bf16[1280,256]{1,0:T(8,128)(2,1)S(1)} %stack.1), channel_id=1, source_target_pairs={{0,4},{4,0},{8,12},{12,8},{16,20},{20,16},{24,28},{28,24},{1,5},{5... | collective-permute-start | bytes 1966088 | tf_op jit(solution)/shard_map/ppermute | solution.py:380
  18.4 2.0 %middle.1.acc_ref = f32[2048,256]{1,0:T(8,128)S(1)} custom-call(s32[256]{0:T(256)S(1)} %get-tuple-element.22.map_ref, f32[16,1024]{1,0:T(8,128)S(1)} %get-tuple-element.23.mask_ref, bf16[2048,1024]{1,0:T(8,128)(2,1)S(1)} %copy-done.1, bf16[144,128,128]{2,1,0:T(8,128)(2,1)S(1)} %copy-done, f32[2048,256]{1,0:T(8,128)S(1)} %get-tuple-element.24.acc_ref, ...), custom_call_target="tpu_custom_call" | custom-call | tf_op jit(solution)/shard_map/middle/pallas_call | solution.py:296
  20.4 0.0 collective-permute-done.5.refs_0_
  20.4 0.0 copy-done.3
  20.5 3.1 %last.1 = bf16[2048,256]{1,0:T(8,128)(2,1)} custom-call(s32[256]{0:T(256)S(1)} %get-tuple-element.22.map_ref, bf16[144,128,128]{2,1,0:T(8,128)(2,1)S(1)} %copy-done, bf16[2048,1024]{1,0:T(8,128)(2,1)S(1)} %copy-done.1, f32[16,1024]{1,0:T(8,128)S(1)} %get-tuple-element.23.mask_ref, f32[2048,256]{1,0:T(8,128)S(1)} %middle.1.acc_ref, ...), custom_call_target="tpu_custom_call" | custom-call | tf_op jit(solution)/shard_map/last/pallas_call | solution.py:360
  (2 shorter events, 0.0 us)
Async XLA Ops:
  2.1 14.5 %collective-permute-start.2 = (bf16[512,256]{1,0:T(8,128)(2,1)S(1)}, bf16[512,256]{1,0:T(8,128)(2,1)S(1)}, u32[]{:S(2)}, u32[]{:S(2)}) collective-permute-start(bf16[512,256]{1,0:T(8,128)(2,1)S(1)} %get-tuple-element.25), channel_id=1, source_target_pairs={{0,24},{4,28},{8,16},{12,20},{16,8},{20,12},{24,0},{28,4},{1,25},{... | collective-permute-start | bytes 786440 | tf_op jit(solution)/shard_map/ppermute | solution.py:380
  5.1 5.3 %copy-start = (bf16[144,128,128]{2,1,0:T(8,128)(2,1)S(1)}, bf16[144,128,128]{2,1,0:T(8,128)(2,1)}, u32[]{:S(2)}) copy-start(bf16[144,128,128]{2,1,0:T(8,128)(2,1)} %edge_ref.5) | copy-start | bytes 14155780
  5.1 5.3 %copy-start.1 = (bf16[2048,1024]{1,0:T(8,128)(2,1)S(1)}, bf16[2048,1024]{1,0:T(8,128)(2,1)}, u32[]{:S(2)}) copy-start(bf16[2048,1024]{1,0:T(8,128)(2,1)} %adj_ref.5) | copy-start | bytes 12582916
  5.1 5.3 %copy-start.2 = (bf16[128,128,128]{2,1,0:T(8,128)(2,1)S(1)}, bf16[128,128,128]{2,1,0:T(8,128)(2,1)}, u32[]{:S(2)}) copy-start(bf16[128,128,128]{2,1,0:T(8,128)(2,1)} %tiles_ref.1) | copy-start | bytes 12582916
  6.5 10.2 %collective-permute-start.3 = (bf16[512,256]{1,0:T(8,128)(2,1)S(1)}, bf16[512,256]{1,0:T(8,128)(2,1)S(1)}, u32[]{:S(2)}, u32[]{:S(2)}) collective-permute-start(bf16[512,256]{1,0:T(8,128)(2,1)S(1)} %get-tuple-element.26), channel_id=1, source_target_pairs={{0,8},{4,12},{8,0},{12,4},{16,24},{20,28},{24,16},{28,20},{1,9},{5... | collective-permute-start | bytes 786440 | tf_op jit(solution)/shard_map/ppermute | solution.py:380
  6.9 10.7 %collective-permute-start.4 = (bf16[512,256]{1,0:T(8,128)(2,1)S(1)}, bf16[512,256]{1,0:T(8,128)(2,1)S(1)}, u32[]{:S(2)}, u32[]{:S(2)}) collective-permute-start(bf16[512,256]{1,0:T(8,128)(2,1)S(1)} %get-tuple-element.27), channel_id=1, source_target_pairs={{0,16},{4,20},{8,24},{12,28},{16,0},{20,4},{24,8},{28,12},{1,17},{... | collective-permute-start | bytes 786440 | tf_op jit(solution)/shard_map/ppermute | solution.py:380
  6.9 8.7 %collective-permute-start.1 = (bf16[256,256]{1,0:T(8,128)(2,1)S(1)}, bf16[256,256]{1,0:T(8,128)(2,1)S(1)}, u32[]{:S(2)}, u32[]{:S(2)}) collective-permute-start(bf16[256,256]{1,0:T(8,128)(2,1)S(1)} %get-tuple-element.21.hub_ref), channel_id=1, source_target_pairs={{0,2},{1,3},{2,0},{3,1},{4,7},{5,6},{6,5},{7,4},{8,10},{9,11},{10,... | collective-permute-start | bytes 393224 | tf_op jit(solution)/shard_map/ppermute | solution.py:386
  10.4 6.2 %collective-permute-start = (bf16[256,256]{1,0:T(8,128)(2,1)S(1)}, bf16[256,256]{1,0:T(8,128)(2,1)S(1)}, u32[]{:S(2)}, u32[]{:S(2)}) collective-permute-start(bf16[256,256]{1,0:T(8,128)(2,1)S(1)} %get-tuple-element.21.hub_ref), channel_id=1, source_target_pairs={{0,1},{1,0},{2,3},{3,2},{4,5},{5,4},{6,7},{7,6},{8,9},{9,8},{10,11... | collective-permute-start | bytes 393224 | tf_op jit(solution)/shard_map/ppermute | solution.py:380
  17.6 2.9 %collective-permute-start.5 = (bf16[1280,256]{1,0:T(8,128)(2,1)S(1)}, bf16[1280,256]{1,0:T(8,128)(2,1)S(1)}, u32[]{:S(2)}, u32[]{:S(2)}) collective-permute-start(bf16[1280,256]{1,0:T(8,128)(2,1)S(1)} %stack.1), channel_id=1, source_target_pairs={{0,4},{4,0},{8,12},{12,8},{16,20},{20,16},{24,28},{28,24},{1,5},{5... | collective-permute-start | bytes 1966088 | tf_op jit(solution)/shard_map/ppermute | solution.py:380
  18.4 2.0 %copy-start.3 = (bf16[256,256]{1,0:T(8,128)(2,1)S(1)}, bf16[256,256]{1,0:T(8,128)(2,1)}, u32[]{:S(2)}) copy-start(bf16[256,256]{1,0:T(8,128)(2,1)} %weight_ref.1) | copy-start | bytes 393220

commit v10 on v9

--- a/solution.py
+++ b/solution.py
@@ -73,11 +73,13 @@
 def pack_kernel(offsets, feat_hbm, send_hbm, count_hbm, hub_hbm, live_hbm, *refs):
     targets, (*packed, scalars, sems) = refs[:5], refs[5:]
     feat_ref, send_ref = targets[:2]
-    sources = [feat_hbm, send_hbm, count_hbm, hub_hbm, live_hbm, count_hbm]
-    copies = start_all(sources, [*targets, scalars], sems)
-    wait_all(copies[:2] + copies[5:])
+    quarter = feat_ref.shape[0] // 4
+    parts = [pl.ds(n * quarter, quarter) for n in range(4)]
+    sources = [send_hbm, count_hbm, *[feat_hbm.at[part] for part in parts], count_hbm, hub_hbm, live_hbm]
+    copies = start_all(sources, [send_ref, scalars, *[feat_ref.at[part] for part in parts], *targets[2:]], sems)
+    wait_all(copies[:6])
     gather_groups(offsets, send_ref, scalars, feat_ref, packed, scalar=True)
-    wait_all(copies[2:5])
+    wait_all(copies[6:])
 
 
 def pack(offsets, features, send_rows, send_count, hub_feats, hub_live):
@@ -89,7 +91,7 @@
         + [jax.ShapeDtypeStruct((len(group) * slots, width), BF) for group in offsets],
         in_specs=[HBM] * 5,
         out_specs=[VMEM] * (5 + len(offsets)),
-        scratch_shapes=[pltpu.SMEM(send_count.shape, I32), pltpu.SemaphoreType.DMA((6,))],
+        scratch_shapes=[pltpu.SMEM(send_count.shape, I32), pltpu.SemaphoreType.DMA((9,))],
         compiler_params=params(16),
         cost_estimate=FREE,
         name="pack",

time: 23.7 us -> 23.8 us (level)
  no operation moved by 1% of the time
where the time goes in v10:
time: 23.8 us; the launch traced here: 23.6 us
  Pallas kernels  13.8 us (58%)
  starting transfers between devices  7.79 us (33%)
  waiting for transfers between devices  1.85 us (8%)
    pallas_call x1, Pallas kernels, local_term(): pl.pallas_call(functools.partial(local_kernel, 8), out_shape=[jax.ShapeDt...  5.22 us
    ppermute x5, starting transfers between devices, swap(): lax.ppermute(x, axis, [(i, i ^ offset) for i in range(lax.axis_size(axis))])  4.31 us
    ppermute x1, starting transfers between devices, swap_by_core(): return lax.ppermute(x, ('row', 'loop'), pairs)  3.48 us
    pallas_call x1, Pallas kernels, last_term(): pl.pallas_call(functools.partial(last_kernel, block, pieces, hubs), out_s...  3.12 us
    pallas_call x1, Pallas kernels, pack(): pl.pallas_call(functools.partial(pack_kernel, offsets), out_shape=[jax.Sh...  2.05 us
    pallas_call x1, Pallas kernels, middle_term(): pl.pallas_call(functools.partial(middle_kernel, 8, hubs, pieces), out_sha...  2.01 us
    ppermute x5, waiting for transfers between devices, swap(): lax.ppermute(x, axis, [(i, i ^ offset) for i in range(lax.axis_size(axis))])  1.85 us
    pallas_call x1, Pallas kernels, pack_more(): pl.pallas_call(functools.partial(more_kernel, offsets), out_shape=[jax.Sh...  1.39 us
  transfers between devices with their start and end apart: 6, of which 3 were waited for; matrix products, arithmetic and copies ran while one was open for 0% of the time, Pallas kernels for 37%

profile of v10, /device:TPU:1, one launch (start us, length us, event | category | flops | bytes accessed | tf_op | source)
XLA Modules:
  0.0 23.6 jit_solution(12076348746696876372)
XLA Ops:
  0.0 2.1 %pack.1 = (bf16[2048,256]{1,0:T(8,128)(2,1)S(1)}, s32[8,256]{1,0:T(8,128)S(1)}, s32[1,8]{1,0:T(1,128)S(1)}, bf16[256,256]{1,0:T(8,128)(2,1)S(1)}, s32[8,16]{1,0:T(8,128)S(1)}, /*index=5*/bf16[512,256]{1,0:T(8,128)(2,1)S(1)}) custom-call(bf16[2048,256]{1,0:T(8,128)(2,1)} %feat_hbm.1, s32[8,256]{1,0:T(8,128)} %bitcast.2, s32[1,8]{1,0:T(1,128)} %count_hbm.1, ...), custom_call_target="tpu_custom_call" | custom-call | tf_op jit(solution)/shard_map/pack/pallas_call | solution.py:88
  2.1 3.1 %collective-permute-start.2 = (bf16[512,256]{1,0:T(8,128)(2,1)S(1)}, bf16[512,256]{1,0:T(8,128)(2,1)S(1)}, u32[]{:S(2)}, u32[]{:S(2)}) collective-permute-start(bf16[512,256]{1,0:T(8,128)(2,1)S(1)} %get-tuple-element.25), channel_id=1, source_target_pairs={{0,24},{4,28},{8,16},{12,20},{16,8},{20,12},{24,0},{28,4},{1,25},{... | collective-permute-start | bytes 786440 | tf_op jit(solution)/shard_map/ppermute | solution.py:382
  5.1 0.0 copy-start
  5.1 0.0 copy-start.1
  5.1 0.0 copy-start.2
  5.1 1.4 %more.1 = (bf16[512,256]{1,0:T(8,128)(2,1)S(1)}, bf16[512,256]{1,0:T(8,128)(2,1)S(1)}) custom-call(bf16[2048,256]{1,0:T(8,128)(2,1)S(1)} %get-tuple-element.17.feat_ref, s32[8,256]{1,0:T(8,128)S(1)} %get-tuple-element.18.send_ref, s32[1,8]{1,0:T(1,128)S(1)} %get-tuple-element.19.count_ref), custom_call_target="tpu_custom_call" | custom-call | flops 34359738368 | tf_op jit(solution)/shard_map/more/pallas_call | solution.py:107
  6.5 0.3 %collective-permute-start.3 = (bf16[512,256]{1,0:T(8,128)(2,1)S(1)}, bf16[512,256]{1,0:T(8,128)(2,1)S(1)}, u32[]{:S(2)}, u32[]{:S(2)}) collective-permute-start(bf16[512,256]{1,0:T(8,128)(2,1)S(1)} %get-tuple-element.26), channel_id=1, source_target_pairs={{0,8},{4,12},{8,0},{12,4},{16,24},{20,28},{24,16},{28,20},{1,9},{5... | collective-permute-start | bytes 786440 | tf_op jit(solution)/shard_map/ppermute | solution.py:382
  6.9 0.1 collective-permute-start.4
  6.9 3.5 %collective-permute-start.1 = (bf16[256,256]{1,0:T(8,128)(2,1)S(1)}, bf16[256,256]{1,0:T(8,128)(2,1)S(1)}, u32[]{:S(2)}, u32[]{:S(2)}) collective-permute-start(bf16[256,256]{1,0:T(8,128)(2,1)S(1)} %get-tuple-element.21.hub_ref), channel_id=1, source_target_pairs={{0,2},{1,3},{2,0},{3,1},{4,7},{5,6},{6,5},{7,4},{8,10},{9,11},{10,... | collective-permute-start | bytes 393224 | tf_op jit(solution)/shard_map/ppermute | solution.py:388
  10.4 0.0 collective-permute-start
  10.4 0.0 copy-done
  10.4 0.0 copy-done.1
  10.4 0.0 copy-done.2
  10.4 5.2 %local.1 = (f32[2048,256]{1,0:T(8,128)S(1)}, s32[256]{0:T(256)S(1)}, bf16[256,256]{1,0:T(8,128)(2,1)S(1)}, f32[16,1024]{1,0:T(8,128)S(1)}) custom-call(bf16[2048,256]{1,0:T(8,128)(2,1)S(1)} %get-tuple-element.17.feat_ref, s32[8,256]{1,0:T(8,128)S(1)} %get-tuple-element.18.send_ref, s32[1,8]{1,0:T(1,128)S(1)} %get-tuple-element.19.count_ref, ...), custom_call_target="tpu_custom_call" | custom-call | tf_op jit(solution)/shard_map/local/pallas_call | solution.py:214
  15.7 0.0 collective-permute-done.1.refs_1_.refs_4_
  15.7 0.9 %collective-permute-done.refs_0_.refs_5_ = bf16[256,256]{1,0:T(8,128)(2,1)S(1)} collective-permute-done((bf16[256,256]{1,0:T(8,128)(2,1)S(1)}, bf16[256,256]{1,0:T(8,128)(2,1)S(1)}, u32[]{:S(2)}, u32[]{:S(2)}) %collective-permute-start) | collective-permute-done | bytes 131104 | tf_op jit(solution)/shard_map/ppermute | solution.py:382
  16.6 0.0 collective-permute-done.2.refs_2_.refs_1_
  16.6 0.2 collective-permute-done.3.refs_3_.refs_2_
  16.7 0.8 %collective-permute-done.4.refs_4_.refs_3_ = bf16[512,256]{1,0:T(8,128)(2,1)S(1)} collective-permute-done((bf16[512,256]{1,0:T(8,128)(2,1)S(1)}, bf16[512,256]{1,0:T(8,128)(2,1)S(1)}, u32[]{:S(2)}, u32[]{:S(2)}) %collective-permute-start.4) | collective-permute-done | bytes 262176 | tf_op jit(solution)/shard_map/ppermute | solution.py:382
  17.6 0.9 %collective-permute-start.5 = (bf16[1280,256]{1,0:T(8,128)(2,1)S(1)}, bf16[1280,256]{1,0:T(8,128)(2,1)S(1)}, u32[]{:S(2)}, u32[]{:S(2)}) collective-permute-start(bf16[1280,256]{1,0:T(8,128)(2,1)S(1)} %stack.1), channel_id=1, source_target_pairs={{0,4},{4,0},{8,12},{12,8},{16,20},{20,16},{24,28},{28,24},{1,5},{5... | collective-permute-start | bytes 1966088 | tf_op jit(solution)/shard_map/ppermute | solution.py:382
  18.4 2.0 %middle.1.acc_ref = f32[2048,256]{1,0:T(8,128)S(1)} custom-call(s32[256]{0:T(256)S(1)} %get-tuple-element.22.map_ref, f32[16,1024]{1,0:T(8,128)S(1)} %get-tuple-element.23.mask_ref, bf16[2048,1024]{1,0:T(8,128)(2,1)S(1)} %copy-done.1, bf16[144,128,128]{2,1,0:T(8,128)(2,1)S(1)} %copy-done, f32[2048,256]{1,0:T(8,128)S(1)} %get-tuple-element.24.acc_ref, ...), custom_call_target="tpu_custom_call" | custom-call | tf_op jit(solution)/shard_map/middle/pallas_call | solution.py:298
  20.4 0.0 collective-permute-done.5.refs_0_
  20.4 0.0 copy-done.3
  20.4 3.1 %last.1 = bf16[2048,256]{1,0:T(8,128)(2,1)} custom-call(s32[256]{0:T(256)S(1)} %get-tuple-element.22.map_ref, bf16[144,128,128]{2,1,0:T(8,128)(2,1)S(1)} %copy-done, bf16[2048,1024]{1,0:T(8,128)(2,1)S(1)} %copy-done.1, f32[16,1024]{1,0:T(8,128)S(1)} %get-tuple-element.23.mask_ref, f32[2048,256]{1,0:T(8,128)S(1)} %middle.1.acc_ref, ...), custom_call_target="tpu_custom_call" | custom-call | tf_op jit(solution)/shard_map/last/pallas_call | solution.py:362
  (2 shorter events, 0.0 us)
Async XLA Ops:
  2.1 14.5 %collective-permute-start.2 = (bf16[512,256]{1,0:T(8,128)(2,1)S(1)}, bf16[512,256]{1,0:T(8,128)(2,1)S(1)}, u32[]{:S(2)}, u32[]{:S(2)}) collective-permute-start(bf16[512,256]{1,0:T(8,128)(2,1)S(1)} %get-tuple-element.25), channel_id=1, source_target_pairs={{0,24},{4,28},{8,16},{12,20},{16,8},{20,12},{24,0},{28,4},{1,25},{... | collective-permute-start | bytes 786440 | tf_op jit(solution)/shard_map/ppermute | solution.py:382
  5.1 5.3 %copy-start = (bf16[144,128,128]{2,1,0:T(8,128)(2,1)S(1)}, bf16[144,128,128]{2,1,0:T(8,128)(2,1)}, u32[]{:S(2)}) copy-start(bf16[144,128,128]{2,1,0:T(8,128)(2,1)} %edge_ref.5) | copy-start | bytes 14155780
  5.1 5.3 %copy-start.1 = (bf16[2048,1024]{1,0:T(8,128)(2,1)S(1)}, bf16[2048,1024]{1,0:T(8,128)(2,1)}, u32[]{:S(2)}) copy-start(bf16[2048,1024]{1,0:T(8,128)(2,1)} %adj_ref.5) | copy-start | bytes 12582916
  5.1 5.3 %copy-start.2 = (bf16[128,128,128]{2,1,0:T(8,128)(2,1)S(1)}, bf16[128,128,128]{2,1,0:T(8,128)(2,1)}, u32[]{:S(2)}) copy-start(bf16[128,128,128]{2,1,0:T(8,128)(2,1)} %tiles_ref.1) | copy-start | bytes 12582916
  6.5 10.2 %collective-permute-start.3 = (bf16[512,256]{1,0:T(8,128)(2,1)S(1)}, bf16[512,256]{1,0:T(8,128)(2,1)S(1)}, u32[]{:S(2)}, u32[]{:S(2)}) collective-permute-start(bf16[512,256]{1,0:T(8,128)(2,1)S(1)} %get-tuple-element.26), channel_id=1, source_target_pairs={{0,8},{4,12},{8,0},{12,4},{16,24},{20,28},{24,16},{28,20},{1,9},{5... | collective-permute-start | bytes 786440 | tf_op jit(solution)/shard_map/ppermute | solution.py:382
  6.9 10.7 %collective-permute-start.4 = (bf16[512,256]{1,0:T(8,128)(2,1)S(1)}, bf16[512,256]{1,0:T(8,128)(2,1)S(1)}, u32[]{:S(2)}, u32[]{:S(2)}) collective-permute-start(bf16[512,256]{1,0:T(8,128)(2,1)S(1)} %get-tuple-element.27), channel_id=1, source_target_pairs={{0,16},{4,20},{8,24},{12,28},{16,0},{20,4},{24,8},{28,12},{1,17},{... | collective-permute-start | bytes 786440 | tf_op jit(solution)/shard_map/ppermute | solution.py:382
  6.9 8.7 %collective-permute-start.1 = (bf16[256,256]{1,0:T(8,128)(2,1)S(1)}, bf16[256,256]{1,0:T(8,128)(2,1)S(1)}, u32[]{:S(2)}, u32[]{:S(2)}) collective-permute-start(bf16[256,256]{1,0:T(8,128)(2,1)S(1)} %get-tuple-element.21.hub_ref), channel_id=1, source_target_pairs={{0,2},{1,3},{2,0},{3,1},{4,7},{5,6},{6,5},{7,4},{8,10},{9,11},{10,... | collective-permute-start | bytes 393224 | tf_op jit(solution)/shard_map/ppermute | solution.py:388
  10.4 6.2 %collective-permute-start = (bf16[256,256]{1,0:T(8,128)(2,1)S(1)}, bf16[256,256]{1,0:T(8,128)(2,1)S(1)}, u32[]{:S(2)}, u32[]{:S(2)}) collective-permute-start(bf16[256,256]{1,0:T(8,128)(2,1)S(1)} %get-tuple-element.21.hub_ref), channel_id=1, source_target_pairs={{0,1},{1,0},{2,3},{3,2},{4,5},{5,4},{6,7},{7,6},{8,9},{9,8},{10,11... | collective-permute-start | bytes 393224 | tf_op jit(solution)/shard_map/ppermute | solution.py:382
  17.6 2.9 %collective-permute-start.5 = (bf16[1280,256]{1,0:T(8,128)(2,1)S(1)}, bf16[1280,256]{1,0:T(8,128)(2,1)S(1)}, u32[]{:S(2)}, u32[]{:S(2)}) collective-permute-start(bf16[1280,256]{1,0:T(8,128)(2,1)S(1)} %stack.1), channel_id=1, source_target_pairs={{0,4},{4,0},{8,12},{12,8},{16,20},{20,16},{24,28},{28,24},{1,5},{5... | collective-permute-start | bytes 1966088 | tf_op jit(solution)/shard_map/ppermute | solution.py:382
  18.4 2.0 %copy-start.3 = (bf16[256,256]{1,0:T(8,128)(2,1)S(1)}, bf16[256,256]{1,0:T(8,128)(2,1)}, u32[]{:S(2)}) copy-start(bf16[256,256]{1,0:T(8,128)(2,1)} %weight_ref.1) | copy-start | bytes 393220
